TPU v7x, 32 devices: a whole 2x2x4 slice. The times are simulated.
32 devices in a mesh: groups: 2 (over y), gx: 4 (over x, core), gy: 4 (over z).
Axes of the slice: x: 2, y: 2, z: 4, core: 2. Of those that a mesh axis runs over, the one named last changes fastest.
Arguments:
- hidden_states: bfloat16 [512, 16384], P(('groups', 'gx'), 'gy'), parts along dimension 0, may hold values from -36 to 36
- norm_gain: bfloat16 [16384], P('gy'), may hold values from 0.5 to 1.5
- projection_weight: bfloat16 [16384, 18432], P('gy', 'gx'), may hold values from -0.046875 to 0.046875
- key_cache: bfloat16 [512, 128, 1024], P(('groups', 'gx', 'gy')), parts along dimension 0, may hold values from -250 to 250
- value_cache: bfloat16 [512, 128, 1024], P(('groups', 'gx', 'gy')), parts along dimension 0, may hold values from -4 to 4
- lengths: int32 [512], P(('groups', 'gx', 'gy')), parts along dimension 0, may hold values from 1 to 128, as said below
Outputs:
- attended: bfloat16 [512, 16384], P(('groups', 'gx', 'gy')), parts along dimension 0
- new_cache_rows: bfloat16 [512, 2048], P(('groups', 'gx', 'gy')), parts along dimension 0
There are 2 independent parts, one for each index of `groups`. A program takes and returns all parts, laid end to end along the dimension named above; an argument that names none is the same for every part. Nothing has to cross between parts.
Inputs may be any that keep to these rules, and one draw needn't show every extreme that they name: Row r holds cached keys and values at positions 0 to lengths[r] - 1, and its new token stands at position lengths[r]; the first of every 128 rows has length 128.
All inputs are finite; a program needn't handle non-finite values.
Results may differ from a plain program's by a relative error of at most 0.012.
Values may be sent and summed in bfloat16 or wider, within the bound.
No kernel may reach another device: no remote copies, remote signals or barrier semaphores. Data moves between devices by JAX's collectives and lax.ppermute only.
A program may use at most 128 MiB of HBM per device.

v0:
```python
import math

import jax
import jax.numpy as jnp
from jax import lax
from jax.sharding import PartitionSpec as P

D = 16384
HEADS = 128
KV_HEADS = 8
HEAD_DIM = 128


norm_eps = 1e-05
rope_base = 500000.0


def rotate_heads(heads, position):
    half_dim = heads.shape[-1] // 2
    freq_steps = jnp.arange(half_dim, dtype=jnp.float32)
    inverse = jnp.exp(freq_steps * (-2.0 * math.log(rope_base) / heads.shape[-1]))
    angles = position[:, None, None] * inverse[None, None, :]
    cosine = jnp.cos(angles)
    sine = jnp.sin(angles)
    front = heads[..., :half_dim]
    second = heads[..., half_dim:]
    return jnp.concatenate(
        [front * cosine - second * sine, second * cosine + front * sine], axis=-1
    )


def head_scores(queries, key_block):
    shaped = key_block.reshape(key_block.shape[0], key_block.shape[1], KV_HEADS, HEAD_DIM)
    products = jnp.einsum("rkgd,rlkd->rkgl", queries, shaped, preferred_element_type=jnp.float32)
    return products * HEAD_DIM ** (-0.5)


def mix_values(weights, value_block):
    shaped = value_block.reshape(value_block.shape[0], value_block.shape[1], KV_HEADS, HEAD_DIM)
    return jnp.einsum("rkgl,rlkd->rkgd", weights, shaped, preferred_element_type=jnp.float32)


def softmax_weights(scores, usable, own_score):
    masked = jnp.where(usable[:, None, None, :], scores, -jnp.inf)
    top_score = jnp.maximum(jnp.max(masked, axis=3), own_score)
    raised = jnp.exp(masked - top_score[..., None])
    raised_own = jnp.exp(own_score - top_score)
    totals = jnp.sum(raised, axis=3) + raised_own
    return (
        (raised / totals[..., None]).astype(jnp.bfloat16),
        (raised_own / totals).astype(jnp.bfloat16),
    )


def attend(queries, new_key, own_values, key_cache, value_cache, lengths):
    row_count = key_cache.shape[0]
    cache_span = key_cache.shape[1]
    usable = jnp.arange(cache_span, dtype=jnp.int32)[None, :] < lengths[:, None]
    own_score = jnp.einsum(
        "rkgd,rkd->rkg", queries, new_key, preferred_element_type=jnp.float32
    ) * HEAD_DIM ** (-0.5)
    scores = head_scores(queries, key_cache)
    weights, own_weight = softmax_weights(scores, usable, own_score)
    mixed = mix_values(weights, value_cache)
    mixed = (
        mixed
        + own_weight.astype(jnp.float32)[..., None] * own_values.astype(jnp.float32)[:, :, None, :]
    )
    return mixed.reshape(row_count, HEADS * HEAD_DIM).astype(jnp.bfloat16)


def body(hidden_states, norm_gain, projection_weight, key_cache, value_cache, lengths):
    along_x = lax.axis_size("gx")
    along_y = lax.axis_size("gy")
    row_count = key_cache.shape[0]
    group_size = HEADS // KV_HEADS
    local_values = hidden_states.astype(jnp.float32)
    square_part = jnp.sum(local_values * local_values, axis=1).reshape(along_y, row_count)
    gain_float = norm_gain.astype(jnp.float32)
    normed = (
        lax.all_gather(hidden_states, "gx", axis=0, tiled=True).astype(jnp.float32)
        * gain_float[None, :]
    ).astype(jnp.bfloat16)
    partial_value = jnp.dot(normed, projection_weight, preferred_element_type=jnp.float32)
    blocks = partial_value.reshape(along_x, along_y, row_count, partial_value.shape[1])
    reduced, square = (
        lax.psum_scatter(blocks, "gy", scatter_dimension=1, tiled=True),
        lax.psum_scatter(square_part, "gy", scatter_dimension=0, tiled=True),
    )
    summed = lax.all_to_all(reduced, "gx", split_axis=0, concat_axis=3, tiled=True)
    scale_rows = lax.rsqrt(square.reshape(row_count) / D + norm_eps)
    projected = (summed.reshape(row_count, -1) * scale_rows[:, None]).astype(jnp.bfloat16)
    query_width = HEADS * HEAD_DIM
    key_width = KV_HEADS * HEAD_DIM
    position = lengths.astype(jnp.float32)
    query_heads = projected[:, :query_width].astype(jnp.float32).reshape(row_count, HEADS, HEAD_DIM)
    key_heads = (
        projected[:, query_width : query_width + key_width]
        .astype(jnp.float32)
        .reshape(row_count, KV_HEADS, HEAD_DIM)
    )
    value_heads = projected[:, query_width + key_width :]
    queries = rotate_heads(query_heads, position).astype(jnp.bfloat16)
    new_key = rotate_heads(key_heads, position).astype(jnp.bfloat16)
    new_cache_rows = jnp.concatenate([new_key.reshape(row_count, key_width), value_heads], axis=1)
    grouped = queries.reshape(row_count, KV_HEADS, group_size, HEAD_DIM)
    own_values = value_heads.reshape(row_count, KV_HEADS, HEAD_DIM)
    attended = attend(grouped, new_key, own_values, key_cache, value_cache, lengths)
    return (attended, new_cache_rows)


def solution(mesh):
    in_specs = (
        P(("groups", "gx"), "gy"),
        P("gy"),
        P("gy", "gx"),
        P(("groups", "gx", "gy"), None, None),
        P(("groups", "gx", "gy"), None, None),
        P(("groups", "gx", "gy")),
    )
    out_specs = (P(("groups", "gx", "gy"), None), P(("groups", "gx", "gy"), None))
    return jax.shard_map(body, mesh=mesh, in_specs=in_specs, out_specs=out_specs, check_vma=False)
```

profile of v0, /device:TPU:0, one launch (start us, length us, event | category | flops | bytes accessed | tf_op | source)
XLA Modules:
  0.0 265.0 jit_solution(15570539021653372426)
XLA Ops:
  7.2 0.0 all-gather.2.cloned.1.call-start
  7.2 0.7 all-gather.2.cloned.1.call-update
  7.9 0.0 all-reduce.4.cloned.1.call-start
  7.9 0.7 convert_element_type.55
  8.6 26.2 %all-gather.2.cloned.1.call-done = bf16[256,4096]{1,0:T(8,128)(2,1)} async-done(((bf16[64,4096]{1,0:T(8,128)(2,1)}), bf16[256,4096]{1,0:T(8,128)(2,1)}) %all-gather.2.cloned.1.call-update) | async-done | bytes 2097168 | tf_op jit(solution)/shard_map/all_gather | solution.py:81
  34.9 18.8 %fusion.6 = f32[256,4608]{1,0:T(8,128)} fusion(bf16[4096,4608]{1,0:T(8,128)(2,1)} %param.8, bf16[256,4096]{1,0:T(8,128)(2,1)} %all-gather.2.cloned.1.call-done, f32[4096]{0:T(1024)S(1)} %convert_element_type.55), kind=kOutput, calls=%fused_computation.7 | convolution fusion | flops 9666822144 | bytes 44580864 | tf_op jit(solution)/shard_map/dot_general | solution.py:84
  53.7 0.0 copy-start.4
  53.7 0.0 copy-start.1
  53.7 0.0 copy-start.2
  53.7 0.0 all-reduce.4.cloned.1.call-update
  53.7 0.6 copy-done.4
  54.3 0.6 dynamic-slice
  54.9 170.9 %all-reduce.4.cloned.1.call-done = f32[4,4,16,4608]{3,2,1,0:T(8,128)} async-done(((f32[4,4,16,4608]{3,2,1,0:T(8,128)}), f32[4,4,16,4608]{3,2,1,0:T(8,128)}) %all-reduce.4.cloned.1.call-update) | async-done | bytes 4718608
  225.8 3.1 %constant_dynamic-slice_fusion.1 = f32[4,1,16,4608]{3,2,1,0:T(8,128)} fusion(f32[4,4,16,4608]{3,2,1,0:T(8,128)} %all-reduce.4.cloned.1.call-done, u32[]{:T(128)} %bitcast.11), kind=kLoop, calls=%fused_computation.43 | loop fusion | bytes 2359300
  228.9 3.5 %all-to-all-start = ((f32[4,1,16,4608]{3,2,1,0:T(8,128)}), f32[4,1,16,4608]{3,2,1,0:T(8,128)S(1)}, u32[]{:S(2)}, u32[]{:S(2)}) async-start(f32[4,1,16,4608]{3,2,1,0:T(8,128)} %constant_dynamic-slice_fusion.1), calls=%async_computation | async-start | bytes 2359296 | tf_op jit(solution)/shard_map/all_to_all | solution.py:90
  232.4 0.0 copy-done.1
  232.4 0.2 multiply_reduce_fusion
  232.6 0.1 reshape.145
  232.7 0.0 copy-done.2
  232.7 9.4 %all-reduce.1 = f32[4,16]{1,0:T(4,128)S(1)} all-reduce(f32[4,16]{1,0:T(4,128)S(1)} %reshape.145), channel_id=3, replica_groups=mesh['groups'=2,'gx'=4,'gy'=4] {'gy'}, use_global_device_ids=true, to_apply=%region_2.0.clone | all-reduce | flops 64 | bytes 512
  242.2 0.7 rsqrt_bitcast_fusion
  242.8 0.1 iota_compare_fusion
  242.9 0.1 multiply_cosine_fusion
  243.0 5.2 %all-to-all-done = f32[4,1,16,4608]{3,2,1,0:T(8,128)S(1)} async-done(((f32[4,1,16,4608]{3,2,1,0:T(8,128)}), f32[4,1,16,4608]{3,2,1,0:T(8,128)S(1)}, u32[]{:S(2)}, u32[]{:S(2)}) %all-to-all-start) | async-done | bytes 1179680 | tf_op jit(solution)/shard_map/all_to_all | solution.py:90
  248.3 0.8 copy.13
  249.0 0.4 copy.22
  249.4 0.1 multiply_convert_fusion.2
  249.5 0.0 copy-start
  249.5 0.1 convert_bitcast_fusion
  249.6 0.1 multiply_subtract_fusion
  249.7 0.1 fusion.34
  249.8 0.1 maximum_convert_fusion
  249.9 0.2 copy.23
  250.1 0.5 subtract_convert_fusion
  250.7 0.5 fusion.23
  251.1 0.6 copy-done
  251.7 0.0 copy-start.3
  251.7 2.4 fusion.32
  254.1 0.7 fusion.20
  254.9 0.0 copy-done.3
  254.9 1.5 fusion.17
  256.3 1.1 copy.50
  257.5 0.6 pad_maximum_fusion.3
  (8 shorter events, 0.1 us)
Async XLA Ops:
  7.2 27.7 %all-gather.2.cloned.1.call-start = ((), (), s32[]{:S(2)}) async-start(), calls=%async_computation.1 | async-start | bytes 2621440 | tf_op jit(solution)/shard_map/all_gather | solution.py:81
  7.9 217.9 %all-reduce.4.cloned.1.call-start = ((), (), s32[]{:S(2)}) async-start(), calls=%async_computation.2 | async-start | bytes 9437184
  53.7 0.7 copy-start.4
  53.7 178.7 %copy-start.1 = (bf16[64,4096]{1,0:T(8,128)(2,1)S(1)}, bf16[64,4096]{1,0:T(8,128)(2,1)}, u32[]{:S(2)}) copy-start(bf16[64,4096]{1,0:T(8,128)(2,1)} %param.6) | copy-start | bytes 1572868
  53.7 179.0 %copy-start.2 = (s32[16]{0:T(128)S(1)}, s32[16]{0:T(128)}, u32[]{:S(2)}) copy-start(s32[16]{0:T(128)} %param.11) | copy-start | bytes 196
  228.9 19.4 %all-to-all-start = ((f32[4,1,16,4608]{3,2,1,0:T(8,128)}), f32[4,1,16,4608]{3,2,1,0:T(8,128)S(1)}, u32[]{:S(2)}, u32[]{:S(2)}) async-start(f32[4,1,16,4608]{3,2,1,0:T(8,128)} %constant_dynamic-slice_fusion.1), calls=%async_computation | async-start | bytes 2359296 | tf_op jit(solution)/shard_map/all_to_all | solution.py:90
  249.5 2.2 copy-start
  251.7 3.2 %copy-start.3 = (bf16[16,128,1024]{2,1,0:T(8,128)(2,1)S(1)}, bf16[16,128,1024]{2,1,0:T(8,128)(2,1)}, u32[]{:S(2)}) copy-start(bf16[16,128,1024]{2,1,0:T(8,128)(2,1)} %param.10) | copy-start | bytes 12582916
Sparse Core Ops, SparseCore 0:
  9.6 25.2 all-gather.1
  53.8 171.9 all-reduce.3
where the time goes:
time: 265 us
  waiting for transfers between devices  203 us (77%)
  matrix products  23.1 us (9%)
  between operations  14.2 us (5%)
  blocking collectives  9.41 us (4%)
  local copies, waits for them, and re-layouts  7.44 us (3%)
  other arithmetic  4.1 us (2%)
  starting transfers between devices  3.6 us (1%)
    unnamed x3, waiting for transfers between devices  172 us
    all_gather x1, waiting for transfers between devices, body(): lax.all_gather(hidden_states, 'gx', axis=0, tiled=True).astype(jnp.float32)  26.2 us
    dot_general x1, matrix products, body(): jnp.dot(normed, projection_weight, preferred_element_type=jnp.float32)  18.8 us
    unnamed x1, blocking collectives  9.41 us
    unnamed x18, local copies, waits for them, and re-layouts  6.59 us
  transfers between devices with their start and end apart: 3, of which 3 were waited for; matrix products, arithmetic and copies ran while one was open for 1% of the time, Pallas kernels for 0%

commit v1 on v0

v1 whole, which is shorter than its diff:
```python
import functools
import math

import jax
import jax.numpy as jnp
from jax import lax
from jax.experimental import pallas as pl
from jax.experimental.pallas import tpu as pltpu
from jax.sharding import PartitionSpec as P

D = 16384
HEADS = 128
KV_HEADS = 8
HEAD_DIM = 128
GROUP = HEADS // KV_HEADS
CORES = 2

norm_eps = 1e-05
rope_base = 500000.0
f32 = jnp.float32
bf16 = jnp.bfloat16


def prep_kernel(order, rows, z_ref, hidden_ref, gain_ref, normed_ref):
    gain = gain_ref[...].astype(f32)
    for place, m in enumerate(order):
        start = pl.multiple_of(jnp.bitwise_xor(z_ref[0], m) * rows, rows)
        block = hidden_ref[pl.ds(start, rows), :].astype(f32)
        normed_ref[pl.ds(place * rows, rows), :] = (block * gain).astype(bf16)


def prepare(hidden, gain, z, order, rows):
    return pl.pallas_call(
        functools.partial(prep_kernel, order, rows),
        out_shape=jax.ShapeDtypeStruct(hidden.shape, bf16),
        in_specs=[
            pl.BlockSpec(memory_space=pltpu.SMEM),
            pl.BlockSpec(memory_space=pltpu.VMEM),
            pl.BlockSpec(memory_space=pltpu.VMEM),
        ],
        out_specs=pl.BlockSpec(memory_space=pltpu.VMEM),
        name="prepare",
    )(z, hidden, gain.reshape(1, -1))


def project_kernel(half, a0_ref, a1_ref, w_ref, keep_ref, send_ref):
    rows = jnp.concatenate([a0_ref[...], a1_ref[...]], axis=0)
    total = jnp.dot(rows, w_ref[...], preferred_element_type=f32)
    for j in range(CORES):
        keep_ref[pl.ds(j * half, half), :] = total[2 * j * half : (2 * j + 1) * half]
        send_ref[pl.ds(j * half, half), :] = total[(2 * j + 1) * half : (2 * j + 2) * half].astype(bf16)


def project(a0, a1, weight, first, width):
    rows, depth = a0.shape
    tile = next(t for t in (256, 384, 128) if width % t == 0 and first % t == 0)
    begin = first // tile
    return pl.pallas_call(
        functools.partial(project_kernel, rows // 2),
        grid=(width // tile,),
        out_shape=(
            jax.ShapeDtypeStruct((rows, width), f32),
            jax.ShapeDtypeStruct((rows, width), bf16),
        ),
        in_specs=[
            pl.BlockSpec((rows, depth), lambda i: (0, 0)),
            pl.BlockSpec((rows, depth), lambda i: (0, 0)),
            pl.BlockSpec((depth, tile), lambda i: (0, begin + i)),
        ],
        out_specs=(
            pl.BlockSpec((rows, tile), lambda i: (0, i)),
            pl.BlockSpec((rows, tile), lambda i: (0, i)),
        ),
        compiler_params=pltpu.CompilerParams(vmem_limit_bytes=32 * 2**20),
        name="project",
    )(a0, a1, weight)


def attend_kernel(plan, rows, per_source, *refs):
    count = sum(len(parts) for _, _, _, parts in plan)
    places_ref, lengths_ref, square_ref, cosine_ref, sine_ref = refs[:5]
    pieces = refs[5 : 5 + count]
    keys_hbm, values_hbm, attended_ref, cache_rows_ref = refs[5 + count : 9 + count]
    keys, values, table, heads, mixed, sems = refs[9 + count :]
    copies = []
    for r in range(rows):
        pair = (
            pltpu.make_async_copy(keys_hbm.at[r], keys.at[r], sems.at[0, r]),
            pltpu.make_async_copy(values_hbm.at[r], values.at[r], sems.at[1, r]),
        )
        for copy in pair:
            copy.start()
        copies.append(pair)
    at = 0
    for source, first, width, parts in plan:
        total = pieces[at][...].astype(f32)
        for other in range(1, len(parts)):
            total = total + pieces[at + other][...].astype(f32)
        at += len(parts)
        table[places_ref[source], :, pl.ds(first, width)] = total
    scale_rows = lax.rsqrt(square_ref[...] * (1.0 / D) + norm_eps)
    cosine = cosine_ref[...]
    sine = sine_ref[...]
    for h in range(HEADS + 2 * KV_HEADS):
        column = (h % per_source) * HEAD_DIM
        head = table[h // per_source, :, pl.ds(column, HEAD_DIM)] * scale_rows
        head = head.astype(bf16)
        if h < HEADS + KV_HEADS:
            head = head.astype(f32)
            head = (head * cosine + pltpu.roll(head, HEAD_DIM // 2, 1) * sine).astype(bf16)
        if h >= HEADS:
            cache_rows_ref[:, pl.ds((h - HEADS) * HEAD_DIM, HEAD_DIM)] = head
        heads[pl.ds(h * rows, rows), :] = head.astype(f32)
    span = keys.shape[1]
    position = lax.broadcasted_iota(jnp.int32, (HEADS, span), 1)
    for r in range(rows):
        for copy in copies[r]:
            copy.wait()
        query = heads[pl.ds(r, HEADS, stride=rows), :]
        own_key = heads[pl.ds(HEADS * rows + r, KV_HEADS, stride=rows), :]
        own_value = heads[pl.ds((HEADS + KV_HEADS) * rows + r, KV_HEADS, stride=rows), :]
        spread = jnp.concatenate(
            [jnp.broadcast_to(own_key[k : k + 1], (GROUP, HEAD_DIM)) for k in range(KV_HEADS)], axis=0
        )
        own_score = jnp.sum(query * spread, axis=1, keepdims=True) * HEAD_DIM ** (-0.5)
        query = query.astype(bf16)
        scores = jnp.concatenate(
            [
                lax.dot_general(
                    query[k * GROUP : (k + 1) * GROUP],
                    keys[r, :, pl.ds(k * HEAD_DIM, HEAD_DIM)],
                    (((1,), (1,)), ((), ())),
                    preferred_element_type=f32,
                )
                for k in range(KV_HEADS)
            ],
            axis=0,
        ) * HEAD_DIM ** (-0.5)
        masked = jnp.where(position < lengths_ref[r], scores, -jnp.inf)
        top = jnp.maximum(jnp.max(masked, axis=1, keepdims=True), own_score)
        raised = jnp.exp(masked - top)
        raised_own = jnp.exp(own_score - top)
        inverse = 1.0 / (jnp.sum(raised, axis=1, keepdims=True) + raised_own)
        weights = (raised * inverse).astype(bf16)
        own_weight = (raised_own * inverse).astype(bf16).astype(f32)
        result = jnp.concatenate(
            [
                jnp.dot(
                    weights[k * GROUP : (k + 1) * GROUP],
                    values[r, :, pl.ds(k * HEAD_DIM, HEAD_DIM)],
                    preferred_element_type=f32,
                )
                + own_weight[k * GROUP : (k + 1) * GROUP] * own_value[k : k + 1]
                for k in range(KV_HEADS)
            ],
            axis=0,
        )
        mixed[pl.ds(r, HEADS, stride=rows), :] = result
    for h in range(HEADS):
        attended_ref[:, pl.ds(h * HEAD_DIM, HEAD_DIM)] = mixed[pl.ds(h * rows, rows), :].astype(bf16)


def attend(plan, pieces, places, lengths, square, cosine, sine, key_cache, value_cache, sources, width):
    rows, span, kv_width = key_cache.shape
    smem = pl.BlockSpec(memory_space=pltpu.SMEM)
    vmem = pl.BlockSpec(memory_space=pltpu.VMEM)
    hbm = pl.BlockSpec(memory_space=pl.ANY)
    return pl.pallas_call(
        functools.partial(attend_kernel, plan, rows, width // HEAD_DIM),
        out_shape=(
            jax.ShapeDtypeStruct((rows, HEADS * HEAD_DIM), bf16),
            jax.ShapeDtypeStruct((rows, 2 * KV_HEADS * HEAD_DIM), bf16),
        ),
        in_specs=[smem, smem, vmem, vmem, vmem] + [vmem] * len(pieces) + [hbm, hbm],
        out_specs=(vmem, vmem),
        scratch_shapes=[
            pltpu.VMEM((rows, span, kv_width), bf16),
            pltpu.VMEM((rows, span, kv_width), bf16),
            pltpu.VMEM((sources, rows, width), f32),
            pltpu.VMEM(((HEADS + 2 * KV_HEADS) * rows, HEAD_DIM), f32),
            pltpu.VMEM((HEADS * rows, HEAD_DIM), f32),
            pltpu.SemaphoreType.DMA((2, rows)),
        ],
        compiler_params=pltpu.CompilerParams(vmem_limit_bytes=40 * 2**20),
        name="attend",
    )(places, lengths, square, cosine, sine, *pieces, key_cache, value_cache)


def rotation(lengths):
    half = HEAD_DIM // 2
    steps = jnp.arange(half, dtype=f32)
    inverse = jnp.exp(steps * (-2.0 * math.log(rope_base) / HEAD_DIM))
    angles = lengths.astype(f32)[:, None] * inverse[None, :]
    cosine = jnp.cos(angles)
    sine = jnp.sin(angles)
    return jnp.concatenate([cosine, cosine], axis=1), jnp.concatenate([-sine, sine], axis=1)


def body(hidden_states, norm_gain, projection_weight, key_cache, value_cache, lengths):
    along_x = lax.axis_size("gx")
    along_z = lax.axis_size("gy")
    chips = along_x // CORES
    rows = key_cache.shape[0]
    width = projection_weight.shape[1]
    z = lax.axis_index("gy")
    gx = lax.axis_index("gx")
    order = list(range(0, along_z, 2)) + list(range(1, along_z, 2))
    kept = along_z // 2

    def on_gx(array, shift, flip):
        pairs = [
            ((x + shift) % chips * CORES + (c ^ flip), x * CORES + c)
            for x in range(chips)
            for c in range(CORES)
        ]
        return lax.ppermute(array, "gx", pairs)

    def on_z(array, flip):
        return lax.ppermute(array, "gy", [(s, s ^ flip) for s in range(along_z)])

    def deliver(array, shift, flip, m):
        pairs = [
            (
                (x * CORES + c) * along_z + s,
                ((x + shift) % chips * CORES + (c ^ flip)) * along_z + (s ^ m),
            )
            for x in range(chips)
            for c in range(CORES)
            for s in range(along_z)
        ]
        return lax.ppermute(array, ("gx", "gy"), pairs)

    normed = prepare(hidden_states, norm_gain, z.reshape(1).astype(jnp.int32), order, rows)
    here = [(normed, on_gx(normed, 0, 1))]
    for k in range(1, chips):
        there = on_gx(normed, k, 0)
        here.append((there, on_gx(there, 0, 1)))

    local = hidden_states.astype(f32)
    square = jnp.sum(local * local, axis=1).reshape(along_z, rows)
    square = jnp.concatenate(
        [lax.dynamic_slice_in_dim(square, jnp.bitwise_xor(z, m), 1, axis=0) for m in order], axis=0
    )
    square = square[:kept] + on_z(square[kept:], 1)
    square = sum(
        [on_z(square[i : i + 1], 2 * i) for i in range(1, kept)], square[:1]
    ).reshape(rows, 1)
    cosine, sine = rotation(lengths)

    cut = 2 if width % (2 * HEAD_DIM) == 0 else 1
    chunk = width // cut
    plan = []
    pieces = []
    for k in range(chips):
        for c in range(cut):
            keep, send = project(*here[k], projection_weight, c * chunk, chunk)
            both = (keep + on_z(send, 1).astype(f32)).astype(bf16).reshape(CORES, kept, rows, chunk)
            for j in range(CORES):
                parts = []
                for i in range(kept):
                    part = both[j, i]
                    if k or j or i:
                        part = deliver(part, k, j, 2 * i)
                    parts.append(part)
                plan.append((k * CORES + j, c * chunk, chunk, tuple(range(len(parts)))))
                pieces.extend(parts)
    x, core = gx // CORES, gx % CORES
    places = jnp.stack(
        [
            (x + chips - k) % chips * CORES + jnp.bitwise_xor(core, j)
            for k in range(chips)
            for j in range(CORES)
        ]
    ).astype(jnp.int32)
    return attend(
        plan, pieces, places, lengths, square, cosine, sine, key_cache, value_cache, along_x, width
    )


def solution(mesh):
    in_specs = (
        P(("groups", "gx"), "gy"),
        P("gy"),
        P("gy", "gx"),
        P(("groups", "gx", "gy"), None, None),
        P(("groups", "gx", "gy"), None, None),
        P(("groups", "gx", "gy")),
    )
    out_specs = (P(("groups", "gx", "gy"), None), P(("groups", "gx", "gy"), None))
    return jax.shard_map(body, mesh=mesh, in_specs=in_specs, out_specs=out_specs, check_vma=False)
```

time: 265 us -> 117 us (0.44)
  waiting for transfers between devices: 203 us -> 22.8 us
  Pallas kernels: 0 us -> 55.7 us
  starting transfers between devices: 3.6 us -> 27 us
  matrix products: 23.1 us -> 0 us
  between operations: 14.2 us -> 0.89 us
  blocking collectives: 9.41 us -> 0 us
    unnamed x3 -> x0, waiting for transfers between devices: 172 us -> none
    pallas_call x0 -> x6, Pallas kernels: none -> 55.7 us  [the longest x4 42.4 us: project(): pl.pallas_call(functools.partial(project_kernel, rows // 2), grid=(width...]
    ppermute x0 -> x23, starting transfers between devices: none -> 27 us  [the longest x14 15.4 us: deliver(): return lax.ppermute(array, ('gx', 'gy'), pairs)]
    all_gather x1 -> x0, waiting for transfers between devices: 26.2 us -> none  [body(): lax.all_gather(hidden_states, 'gx', axis=0, tiled=True).astype(jnp.float32)]
    dot_general x4 -> x0, matrix products: 23.1 us -> none  [the longest x1 18.8 us: body(): jnp.dot(normed, projection_weight, preferred_element_type=jnp.float32)]
    ppermute x0 -> x23, waiting for transfers between devices: none -> 22.8 us  [the longest x6 14 us: on_z(): return lax.ppermute(array, 'gy', [(s, s ^ flip) for s in range(along_z)])]
    unnamed x1 -> x0, blocking collectives: 9.41 us -> none
    all_to_all x1 -> x0, waiting for transfers between devices: 5.24 us -> none  [body(): lax.all_to_all(reduced, 'gx', split_axis=0, concat_axis=3, tiled=True)]
  transfers between devices with their start and end apart: 3 -> 23, of which waited for: 3 -> 6; matrix products, arithmetic and copies ran while one was open for 1% -> 2% of each run, Pallas kernels for 0% -> 37%
where the time goes in v1:
time: 117 us; the launch traced here: 116 us
  Pallas kernels  55.7 us (48%)
  starting transfers between devices  27 us (23%)
  waiting for transfers between devices  22.8 us (19%)
  local copies, waits for them, and re-layouts  7.01 us (6%)
  other arithmetic  2.42 us (2%)
    pallas_call x4, Pallas kernels, project(): pl.pallas_call(functools.partial(project_kernel, rows // 2), grid=(width...  42.4 us
    ppermute x14, starting transfers between devices, deliver(): return lax.ppermute(array, ('gx', 'gy'), pairs)  15.4 us
    ppermute x6, waiting for transfers between devices, on_z(): return lax.ppermute(array, 'gy', [(s, s ^ flip) for s in range(along_z)])  14 us
    pallas_call x1, Pallas kernels, attend(): pl.pallas_call(functools.partial(attend_kernel, plan, rows, width // HEAD...  11.4 us
    ppermute x14, waiting for transfers between devices, deliver(): return lax.ppermute(array, ('gx', 'gy'), pairs)  8.75 us
    ppermute x6, starting transfers between devices, on_z(): return lax.ppermute(array, 'gy', [(s, s ^ flip) for s in range(along_z)])  8.61 us
    unnamed x8, local copies, waits for them, and re-layouts  5.43 us
    ppermute x3, starting transfers between devices, on_gx(): return lax.ppermute(array, 'gx', pairs)  2.94 us
  transfers between devices with their start and end apart: 23, of which 6 were waited for; matrix products, arithmetic and copies ran while one was open for 2% of the time, Pallas kernels for 37%

profile of v1, /device:TPU:0, one launch (start us, length us, event | category | flops | bytes accessed | tf_op | source)
XLA Modules:
  0.0 115.8 jit_solution(3798569631118895454)
XLA Ops:
  0.6 1.3 %reshape.37.gain_ref = bf16[1,4096]{1,0:T(2,128)(2,1)} reshape(bf16[4096]{0:T(1024)(128)(2,1)} %param.7) | data formatting | bytes 16384 | tf_op jit(solution)/shard_map/reshape | solution.py:43
  1.9 1.9 %prepare.1.a0_ref = bf16[64,4096]{1,0:T(8,128)(2,1)} custom-call(s32[1]{0:T(128)} %bitcast.5.z_ref, bf16[64,4096]{1,0:T(8,128)(2,1)} %hidden_ref.1, bf16[1,4096]{1,0:T(2,128)(2,1)} %reshape.37.gain_ref), custom_call_target="tpu_custom_call" | custom-call | tf_op jit(solution)/shard_map/prepare/pallas_call | solution.py:33
  3.9 2.9 %collective-permute-start.11 = (bf16[64,4096]{1,0:T(8,128)(2,1)}, bf16[64,4096]{1,0:T(8,128)(2,1)S(1)}, u32[]{:S(2)}, u32[]{:S(2)}) collective-permute-start(bf16[64,4096]{1,0:T(8,128)(2,1)} %prepare.1.a0_ref), channel_id=1, source_target_pairs={{8,0},{12,4},{0,8},{4,12},{9,1},{13,5},{1,9},{5,13},{10,2},{14,6},... | collective-permute-start | bytes 1572872 | tf_op jit(solution)/shard_map/ppermute | solution.py:216
  6.8 1.2 %multiply_reduce_fusion = f32[64]{0:T(128)S(1)} fusion(bf16[64,4096]{1,0:T(8,128)(2,1)} %hidden_ref.1), kind=kLoop, calls=%fused_computation | loop fusion | flops 786368 | bytes 524544 | tf_op jit(solution)/shard_map/reduce_sum | solution.py:240
  8.1 0.1 reshape.34
  8.2 1.6 %collective-permute-start = (f32[2,16]{1,0:T(2,128)S(1)}, f32[2,16]{1,0:T(2,128)S(1)}, u32[]{:S(2)}, u32[]{:S(2)}) collective-permute-start(f32[2,16]{1,0:T(2,128)S(1)} %pad_maximum_fusion.2), channel_id=1, source_target_pairs={{0,1},{1,0},{2,3},{3,2},{4,5},{5,4},{6,7},{7,6},{8,9},{9,8},{10,11... | collective-permute-start | bytes 392 | tf_op jit(solution)/shard_map/ppermute | solution.py:219
  9.8 0.7 convert_element_type.31
  10.5 0.1 fusion
  10.7 0.1 pad_maximum_fusion
  10.8 0.0 collective-permute-done.2.a1_ref
  10.8 1.0 copy-done
  11.8 10.6 %project.5 = (f32[64,2304]{1,0:T(8,128)S(1)}, bf16[64,2304]{1,0:T(8,128)(2,1)S(1)}) custom-call(bf16[64,4096]{1,0:T(8,128)(2,1)S(1)} %copy-done, bf16[64,4096]{1,0:T(8,128)(2,1)S(1)} %collective-permute-done.2.a1_ref, bf16[4096,4608]{1,0:T(8,128)(2,1)} %w_ref.7), custom_call_target="tpu_custom_call" | custom-call | tf_op jit(solution)/shard_map/project/pallas_call | solution.py:58
  22.4 0.5 collective-permute-start.7
  22.9 0.1 pad_add_fusion.refs_0_
  23.0 0.0 collective-permute-done
  23.0 2.7 %collective-permute-start.1 = (f32[1,16]{1,0:T(1,128)S(1)}, f32[1,16]{1,0:T(1,128)S(1)}, u32[]{:S(2)}, u32[]{:S(2)}) collective-permute-start(f32[1,16]{1,0:T(1,128)S(1)} %slice.59), channel_id=1, source_target_pairs={{0,2},{1,3},{2,0},{3,1},{4,6},{5,7},{6,4},{7,5},{8,10},{9,11},{10,... | collective-permute-start | bytes 200 | tf_op jit(solution)/shard_map/ppermute | solution.py:219
  25.7 10.6 %project.4 = (f32[64,2304]{1,0:T(8,128)S(1)}, bf16[64,2304]{1,0:T(8,128)(2,1)S(1)}) custom-call(bf16[64,4096]{1,0:T(8,128)(2,1)S(1)} %copy-done, bf16[64,4096]{1,0:T(8,128)(2,1)S(1)} %collective-permute-done.2.a1_ref, bf16[4096,4608]{1,0:T(8,128)(2,1)} %w_ref.7), custom_call_target="tpu_custom_call" | custom-call | tf_op jit(solution)/shard_map/project/pallas_call | solution.py:58
  36.3 1.6 %collective-permute-start.3 = (bf16[64,2304]{1,0:T(8,128)(2,1)S(1)}, bf16[64,2304]{1,0:T(8,128)(2,1)S(1)}, u32[]{:S(2)}, u32[]{:S(2)}) collective-permute-start(bf16[64,2304]{1,0:T(8,128)(2,1)S(1)} %get-tuple-element.11), channel_id=1, source_target_pairs={{0,1},{1,0},{2,3},{3,2},{4,5},{5,4},{6,7},{7,6},{8,9},{9,8},{10,11... | collective-permute-start | bytes 884744 | tf_op jit(solution)/shard_map/ppermute | solution.py:219
  37.9 0.1 add_convert_fusion.2
  38.0 0.5 collective-permute-start.10
  38.5 2.6 %collective-permute-start.8 = (bf16[16,2304]{1,0:T(8,128)(2,1)S(1)}, bf16[16,2304]{1,0:T(8,128)(2,1)S(1)}, u32[]{:S(2)}, u32[]{:S(2)}) collective-permute-start(bf16[16,2304]{1,0:T(8,128)(2,1)S(1)} %get-tuple-element.28), channel_id=1, source_target_pairs={{0,2},{1,3},{2,0},{3,1},{4,6},{5,7},{6,4},{7,5},{8,10},{9,11},{10,... | collective-permute-start | bytes 221192 | tf_op jit(solution)/shard_map/ppermute | solution.py:231
  41.1 6.6 %collective-permute-done.3 = bf16[64,2304]{1,0:T(8,128)(2,1)S(1)} collective-permute-done((bf16[64,2304]{1,0:T(8,128)(2,1)S(1)}, bf16[64,2304]{1,0:T(8,128)(2,1)S(1)}, u32[]{:S(2)}, u32[]{:S(2)}) %collective-permute-start.3) | collective-permute-done | bytes 294944 | tf_op jit(solution)/shard_map/ppermute | solution.py:219
  47.7 0.1 add_convert_fusion.3
  47.8 10.6 %project.6 = (f32[64,2304]{1,0:T(8,128)S(1)}, bf16[64,2304]{1,0:T(8,128)(2,1)S(1)}) custom-call(bf16[64,4096]{1,0:T(8,128)(2,1)S(1)} %collective-permute-done.11.a0_ref, bf16[64,4096]{1,0:T(8,128)(2,1)S(1)} %collective-permute-done.12.a1_ref, bf16[4096,4608]{1,0:T(8,128)(2,1)} %w_ref.7), custom_call_target="tpu_custom_call" | custom-call | tf_op jit(solution)/shard_map/project/pallas_call | solution.py:58
  58.4 0.2 collective-permute-start.13
  58.6 0.0 copy-start.3
  58.6 10.6 %project.7 = (f32[64,2304]{1,0:T(8,128)S(1)}, bf16[64,2304]{1,0:T(8,128)(2,1)S(1)}) custom-call(bf16[64,4096]{1,0:T(8,128)(2,1)S(1)} %collective-permute-done.11.a0_ref, bf16[64,4096]{1,0:T(8,128)(2,1)S(1)} %collective-permute-done.12.a1_ref, bf16[4096,4608]{1,0:T(8,128)(2,1)} %w_ref.7), custom_call_target="tpu_custom_call" | custom-call | tf_op jit(solution)/shard_map/project/pallas_call | solution.py:58
  69.2 2.0 %collective-permute-start.18 = (bf16[64,2304]{1,0:T(8,128)(2,1)S(1)}, bf16[64,2304]{1,0:T(8,128)(2,1)S(1)}, u32[]{:S(2)}, u32[]{:S(2)}) collective-permute-start(bf16[64,2304]{1,0:T(8,128)(2,1)S(1)} %get-tuple-element.17), channel_id=1, source_target_pairs={{0,1},{1,0},{2,3},{3,2},{4,5},{5,4},{6,7},{7,6},{8,9},{9,8},{10,11... | collective-permute-start | bytes 884744 | tf_op jit(solution)/shard_map/ppermute | solution.py:219
  71.2 0.1 add_convert_fusion.1
  71.3 7.4 %collective-permute-done.18 = bf16[64,2304]{1,0:T(8,128)(2,1)S(1)} collective-permute-done((bf16[64,2304]{1,0:T(8,128)(2,1)S(1)}, bf16[64,2304]{1,0:T(8,128)(2,1)S(1)}, u32[]{:S(2)}, u32[]{:S(2)}) %collective-permute-start.18) | collective-permute-done | bytes 294944 | tf_op jit(solution)/shard_map/ppermute | solution.py:219
  78.7 2.0 %collective-permute-start.4 = (bf16[16,2304]{1,0:T(8,128)(2,1)S(1)}, bf16[16,2304]{1,0:T(8,128)(2,1)S(1)}, u32[]{:S(2)}, u32[]{:S(2)}) collective-permute-start(bf16[16,2304]{1,0:T(8,128)(2,1)S(1)} %get-tuple-element.32), channel_id=1, source_target_pairs={{0,2},{1,3},{2,0},{3,1},{4,6},{5,7},{6,4},{7,5},{8,10},{9,11},{10,... | collective-permute-start | bytes 221192 | tf_op jit(solution)/shard_map/ppermute | solution.py:231
  80.6 0.1 add_convert_fusion
  80.7 0.1 collective-permute-start.5
  80.8 1.1 collective-permute-start.6
  81.9 0.5 collective-permute-start.14
  82.3 3.0 %collective-permute-start.15 = (bf16[16,2304]{1,0:T(8,128)(2,1)S(1)}, bf16[16,2304]{1,0:T(8,128)(2,1)S(1)}, u32[]{:S(2)}, u32[]{:S(2)}) collective-permute-start(bf16[16,2304]{1,0:T(8,128)(2,1)S(1)} %get-tuple-element.24), channel_id=1, source_target_pairs={{0,10},{1,11},{2,8},{3,9},{4,14},{5,15},{6,12},{7,13},{8,2},{9,3},... | collective-permute-start | bytes 221192 | tf_op jit(solution)/shard_map/ppermute | solution.py:231
  85.3 2.2 %collective-permute-start.17 = (bf16[16,2304]{1,0:T(8,128)(2,1)S(1)}, bf16[16,2304]{1,0:T(8,128)(2,1)S(1)}, u32[]{:S(2)}, u32[]{:S(2)}) collective-permute-start(bf16[16,2304]{1,0:T(8,128)(2,1)S(1)} %get-tuple-element.22), channel_id=1, source_target_pairs={{0,14},{1,15},{2,12},{3,13},{4,10},{5,11},{6,8},{7,9},{8,6},{9,7},... | collective-permute-start | bytes 221192 | tf_op jit(solution)/shard_map/ppermute | solution.py:231
  87.6 3.0 %collective-permute-done.6.refs_8_ = bf16[16,2304]{1,0:T(8,128)(2,1)S(1)} collective-permute-done((bf16[16,2304]{1,0:T(8,128)(2,1)S(1)}, bf16[16,2304]{1,0:T(8,128)(2,1)S(1)}, u32[]{:S(2)}, u32[]{:S(2)}) %collective-permute-start.6) | collective-permute-done | bytes 73760 | tf_op jit(solution)/shard_map/ppermute | solution.py:231
  90.5 0.4 collective-permute-start.20
  91.0 2.0 %collective-permute-done.15.refs_14_ = bf16[16,2304]{1,0:T(8,128)(2,1)S(1)} collective-permute-done((bf16[16,2304]{1,0:T(8,128)(2,1)S(1)}, bf16[16,2304]{1,0:T(8,128)(2,1)S(1)}, u32[]{:S(2)}, u32[]{:S(2)}) %collective-permute-start.15) | collective-permute-done | bytes 73760 | tf_op jit(solution)/shard_map/ppermute | solution.py:231
  92.9 1.1 collective-permute-start.21
  94.1 2.0 %collective-permute-start.22 = (bf16[16,2304]{1,0:T(8,128)(2,1)S(1)}, bf16[16,2304]{1,0:T(8,128)(2,1)S(1)}, u32[]{:S(2)}, u32[]{:S(2)}) collective-permute-start(bf16[16,2304]{1,0:T(8,128)(2,1)S(1)} %get-tuple-element.18), channel_id=1, source_target_pairs={{0,14},{1,15},{2,12},{3,13},{4,10},{5,11},{6,8},{7,9},{8,6},{9,7},... | collective-permute-start | bytes 221192 | tf_op jit(solution)/shard_map/ppermute | solution.py:231
  96.1 0.1 copy.8.refs_2_
  96.2 3.1 %collective-permute-done.20.refs_18_ = bf16[16,2304]{1,0:T(8,128)(2,1)S(1)} collective-permute-done((bf16[16,2304]{1,0:T(8,128)(2,1)S(1)}, bf16[16,2304]{1,0:T(8,128)(2,1)S(1)}, u32[]{:S(2)}, u32[]{:S(2)}) %collective-permute-start.20) | collective-permute-done | bytes 73760 | tf_op jit(solution)/shard_map/ppermute | solution.py:231
  99.3 0.7 collective-permute-done.22.refs_20_
  100.0 2.2 %copy-done.1 = bf16[16,128,1024]{2,1,0:T(8,128)(2,1)S(1)} copy-done((bf16[16,128,1024]{2,1,0:T(8,128)(2,1)S(1)}, bf16[16,128,1024]{2,1,0:T(8,128)(2,1)}, u32[]{:S(2)}) %copy-start.1) | copy-done | bytes 4194328
  102.2 2.2 %copy-done.2 = bf16[16,128,1024]{2,1,0:T(8,128)(2,1)S(1)} copy-done((bf16[16,128,1024]{2,1,0:T(8,128)(2,1)S(1)}, bf16[16,128,1024]{2,1,0:T(8,128)(2,1)}, u32[]{:S(2)}) %copy-start.2) | copy-done | bytes 4194328
  104.4 11.4 %attend.1 = (bf16[16,16384]{1,0:T(8,128)(2,1)}, bf16[16,2048]{1,0:T(8,128)(2,1)}) custom-call(s32[4]{0:T(128)S(1)} %pad_add_fusion.refs_0_, s32[16]{0:T(128)S(1)} %copy-done.3, f32[16,1]{1,0:T(8,128)S(1)} %copy.8.refs_2_, f32[16,128]{1,0:T(8,128)S(1)} %get-tuple-element.41.refs_3_, f32[16,128]{1,0:T(8,128)S(1)} %get-tuple-element.42.refs_4_, ...), custom_call_target="tpu_custom_call" | custom-call | tf_op jit(solution)/shard_map/attend/pallas_call | solution.py:168
  (34 shorter events, 0.2 us)
Async XLA Ops:
  3.9 34.0 %collective-permute-start.11 = (bf16[64,4096]{1,0:T(8,128)(2,1)}, bf16[64,4096]{1,0:T(8,128)(2,1)S(1)}, u32[]{:S(2)}, u32[]{:S(2)}) collective-permute-start(bf16[64,4096]{1,0:T(8,128)(2,1)} %prepare.1.a0_ref), channel_id=1, source_target_pairs={{8,0},{12,4},{0,8},{4,12},{9,1},{13,5},{1,9},{5,13},{10,2},{14,6},... | collective-permute-start | bytes 1572872 | tf_op jit(solution)/shard_map/ppermute | solution.py:216
  6.8 3.9 %collective-permute-start.2 = (bf16[64,4096]{1,0:T(8,128)(2,1)}, bf16[64,4096]{1,0:T(8,128)(2,1)S(1)}, u32[]{:S(2)}, u32[]{:S(2)}) collective-permute-start(bf16[64,4096]{1,0:T(8,128)(2,1)} %prepare.1.a0_ref), channel_id=1, source_target_pairs={{4,0},{0,4},{12,8},{8,12},{5,1},{1,5},{13,9},{9,13},{6,2},{2,6},{1... | collective-permute-start | bytes 1572872 | tf_op jit(solution)/shard_map/ppermute | solution.py:216
  8.2 14.8 %collective-permute-start = (f32[2,16]{1,0:T(2,128)S(1)}, f32[2,16]{1,0:T(2,128)S(1)}, u32[]{:S(2)}, u32[]{:S(2)}) collective-permute-start(f32[2,16]{1,0:T(2,128)S(1)} %pad_maximum_fusion.2), channel_id=1, source_target_pairs={{0,1},{1,0},{2,3},{3,2},{4,5},{5,4},{6,7},{7,6},{8,9},{9,8},{10,11... | collective-permute-start | bytes 392 | tf_op jit(solution)/shard_map/ppermute | solution.py:219
  10.8 1.0 copy-start
  22.4 15.5 %collective-permute-start.7 = (bf16[64,2304]{1,0:T(8,128)(2,1)S(1)}, bf16[64,2304]{1,0:T(8,128)(2,1)S(1)}, u32[]{:S(2)}, u32[]{:S(2)}) collective-permute-start(bf16[64,2304]{1,0:T(8,128)(2,1)S(1)} %get-tuple-element.13), channel_id=1, source_target_pairs={{0,1},{1,0},{2,3},{3,2},{4,5},{5,4},{6,7},{7,6},{8,9},{9,8},{10,11... | collective-permute-start | bytes 884744 | tf_op jit(solution)/shard_map/ppermute | solution.py:219
  23.0 57.7 %collective-permute-start.1 = (f32[1,16]{1,0:T(1,128)S(1)}, f32[1,16]{1,0:T(1,128)S(1)}, u32[]{:S(2)}, u32[]{:S(2)}) collective-permute-start(f32[1,16]{1,0:T(1,128)S(1)} %slice.59), channel_id=1, source_target_pairs={{0,2},{1,3},{2,0},{3,1},{4,6},{5,7},{6,4},{7,5},{8,10},{9,11},{10,... | collective-permute-start | bytes 200 | tf_op jit(solution)/shard_map/ppermute | solution.py:219
  36.3 11.4 %collective-permute-start.3 = (bf16[64,2304]{1,0:T(8,128)(2,1)S(1)}, bf16[64,2304]{1,0:T(8,128)(2,1)S(1)}, u32[]{:S(2)}, u32[]{:S(2)}) collective-permute-start(bf16[64,2304]{1,0:T(8,128)(2,1)S(1)} %get-tuple-element.11), channel_id=1, source_target_pairs={{0,1},{1,0},{2,3},{3,2},{4,5},{5,4},{6,7},{7,6},{8,9},{9,8},{10,11... | collective-permute-start | bytes 884744 | tf_op jit(solution)/shard_map/ppermute | solution.py:219
  37.9 9.9 %collective-permute-start.12 = (bf16[64,4096]{1,0:T(8,128)(2,1)S(1)}, bf16[64,4096]{1,0:T(8,128)(2,1)S(1)}, u32[]{:S(2)}, u32[]{:S(2)}) collective-permute-start(bf16[64,4096]{1,0:T(8,128)(2,1)S(1)} %collective-permute-done.11.a0_ref), channel_id=1, source_target_pairs={{4,0},{0,4},{12,8},{8,12},{5,1},{1,5},{13,9},{9,13},{6,2},{2,6},{1... | collective-permute-start | bytes 1572872 | tf_op jit(solution)/shard_map/ppermute | solution.py:216
  38.0 42.8 %collective-permute-start.10 = (bf16[16,2304]{1,0:T(8,128)(2,1)S(1)}, bf16[16,2304]{1,0:T(8,128)(2,1)S(1)}, u32[]{:S(2)}, u32[]{:S(2)}) collective-permute-start(bf16[16,2304]{1,0:T(8,128)(2,1)S(1)} %get-tuple-element.26), channel_id=1, source_target_pairs={{0,6},{1,7},{2,4},{3,5},{4,2},{5,3},{6,0},{7,1},{8,14},{9,15},{10,... | collective-permute-start | bytes 221192 | tf_op jit(solution)/shard_map/ppermute | solution.py:231
  38.5 43.3 %collective-permute-start.8 = (bf16[16,2304]{1,0:T(8,128)(2,1)S(1)}, bf16[16,2304]{1,0:T(8,128)(2,1)S(1)}, u32[]{:S(2)}, u32[]{:S(2)}) collective-permute-start(bf16[16,2304]{1,0:T(8,128)(2,1)S(1)} %get-tuple-element.28), channel_id=1, source_target_pairs={{0,2},{1,3},{2,0},{3,1},{4,6},{5,7},{6,4},{7,5},{8,10},{9,11},{10,... | collective-permute-start | bytes 221192 | tf_op jit(solution)/shard_map/ppermute | solution.py:231
  47.7 34.6 %collective-permute-start.9 = (bf16[16,2304]{1,0:T(8,128)(2,1)S(1)}, bf16[16,2304]{1,0:T(8,128)(2,1)S(1)}, u32[]{:S(2)}, u32[]{:S(2)}) collective-permute-start(bf16[16,2304]{1,0:T(8,128)(2,1)S(1)} %get-tuple-element.27), channel_id=1, source_target_pairs={{0,4},{1,5},{2,6},{3,7},{4,0},{5,1},{6,2},{7,3},{8,12},{9,13},{10,... | collective-permute-start | bytes 221192 | tf_op jit(solution)/shard_map/ppermute | solution.py:231
  58.4 10.9 %collective-permute-start.13 = (bf16[64,2304]{1,0:T(8,128)(2,1)S(1)}, bf16[64,2304]{1,0:T(8,128)(2,1)S(1)}, u32[]{:S(2)}, u32[]{:S(2)}) collective-permute-start(bf16[64,2304]{1,0:T(8,128)(2,1)S(1)} %get-tuple-element.15), channel_id=1, source_target_pairs={{0,1},{1,0},{2,3},{3,2},{4,5},{5,4},{6,7},{7,6},{8,9},{9,8},{10,11... | collective-permute-start | bytes 884744 | tf_op jit(solution)/shard_map/ppermute | solution.py:219
  58.6 41.4 %copy-start.3 = (s32[16]{0:T(128)S(1)}, s32[16]{0:T(128)}, u32[]{:S(2)}) copy-start(s32[16]{0:T(128)} %refs_1_.1) | copy-start | bytes 196
  69.2 9.4 %collective-permute-start.18 = (bf16[64,2304]{1,0:T(8,128)(2,1)S(1)}, bf16[64,2304]{1,0:T(8,128)(2,1)S(1)}, u32[]{:S(2)}, u32[]{:S(2)}) collective-permute-start(bf16[64,2304]{1,0:T(8,128)(2,1)S(1)} %get-tuple-element.17), channel_id=1, source_target_pairs={{0,1},{1,0},{2,3},{3,2},{4,5},{5,4},{6,7},{7,6},{8,9},{9,8},{10,11... | collective-permute-start | bytes 884744 | tf_op jit(solution)/shard_map/ppermute | solution.py:219
  78.7 6.6 %collective-permute-start.4 = (bf16[16,2304]{1,0:T(8,128)(2,1)S(1)}, bf16[16,2304]{1,0:T(8,128)(2,1)S(1)}, u32[]{:S(2)}, u32[]{:S(2)}) collective-permute-start(bf16[16,2304]{1,0:T(8,128)(2,1)S(1)} %get-tuple-element.32), channel_id=1, source_target_pairs={{0,2},{1,3},{2,0},{3,1},{4,6},{5,7},{6,4},{7,5},{8,10},{9,11},{10,... | collective-permute-start | bytes 221192 | tf_op jit(solution)/shard_map/ppermute | solution.py:231
  80.7 4.6 %collective-permute-start.5 = (bf16[16,2304]{1,0:T(8,128)(2,1)S(1)}, bf16[16,2304]{1,0:T(8,128)(2,1)S(1)}, u32[]{:S(2)}, u32[]{:S(2)}) collective-permute-start(bf16[16,2304]{1,0:T(8,128)(2,1)S(1)} %get-tuple-element.31), channel_id=1, source_target_pairs={{0,4},{1,5},{2,6},{3,7},{4,0},{5,1},{6,2},{7,3},{8,12},{9,13},{10,... | collective-permute-start | bytes 221192 | tf_op jit(solution)/shard_map/ppermute | solution.py:231
  80.8 9.7 %collective-permute-start.6 = (bf16[16,2304]{1,0:T(8,128)(2,1)S(1)}, bf16[16,2304]{1,0:T(8,128)(2,1)S(1)}, u32[]{:S(2)}, u32[]{:S(2)}) collective-permute-start(bf16[16,2304]{1,0:T(8,128)(2,1)S(1)} %get-tuple-element.30), channel_id=1, source_target_pairs={{0,6},{1,7},{2,4},{3,5},{4,2},{5,3},{6,0},{7,1},{8,14},{9,15},{10,... | collective-permute-start | bytes 221192 | tf_op jit(solution)/shard_map/ppermute | solution.py:231
  81.9 8.7 %collective-permute-start.14 = (bf16[16,2304]{1,0:T(8,128)(2,1)S(1)}, bf16[16,2304]{1,0:T(8,128)(2,1)S(1)}, u32[]{:S(2)}, u32[]{:S(2)}) collective-permute-start(bf16[16,2304]{1,0:T(8,128)(2,1)S(1)} %get-tuple-element.25), channel_id=1, source_target_pairs={{0,8},{1,9},{2,10},{3,11},{4,12},{5,13},{6,14},{7,15},{8,0},{9,1},... | collective-permute-start | bytes 221192 | tf_op jit(solution)/shard_map/ppermute | solution.py:231
  82.3 10.6 %collective-permute-start.15 = (bf16[16,2304]{1,0:T(8,128)(2,1)S(1)}, bf16[16,2304]{1,0:T(8,128)(2,1)S(1)}, u32[]{:S(2)}, u32[]{:S(2)}) collective-permute-start(bf16[16,2304]{1,0:T(8,128)(2,1)S(1)} %get-tuple-element.24), channel_id=1, source_target_pairs={{0,10},{1,11},{2,8},{3,9},{4,14},{5,15},{6,12},{7,13},{8,2},{9,3},... | collective-permute-start | bytes 221192 | tf_op jit(solution)/shard_map/ppermute | solution.py:231
  85.3 8.8 %collective-permute-start.16 = (bf16[16,2304]{1,0:T(8,128)(2,1)S(1)}, bf16[16,2304]{1,0:T(8,128)(2,1)S(1)}, u32[]{:S(2)}, u32[]{:S(2)}) collective-permute-start(bf16[16,2304]{1,0:T(8,128)(2,1)S(1)} %get-tuple-element.23), channel_id=1, source_target_pairs={{0,12},{1,13},{2,14},{3,15},{4,8},{5,9},{6,10},{7,11},{8,4},{9,5},... | collective-permute-start | bytes 221192 | tf_op jit(solution)/shard_map/ppermute | solution.py:231
  85.3 10.9 %collective-permute-start.17 = (bf16[16,2304]{1,0:T(8,128)(2,1)S(1)}, bf16[16,2304]{1,0:T(8,128)(2,1)S(1)}, u32[]{:S(2)}, u32[]{:S(2)}) collective-permute-start(bf16[16,2304]{1,0:T(8,128)(2,1)S(1)} %get-tuple-element.22), channel_id=1, source_target_pairs={{0,14},{1,15},{2,12},{3,13},{4,10},{5,11},{6,8},{7,9},{8,6},{9,7},... | collective-permute-start | bytes 221192 | tf_op jit(solution)/shard_map/ppermute | solution.py:231
  90.5 5.7 %collective-permute-start.19 = (bf16[16,2304]{1,0:T(8,128)(2,1)S(1)}, bf16[16,2304]{1,0:T(8,128)(2,1)S(1)}, u32[]{:S(2)}, u32[]{:S(2)}) collective-permute-start(bf16[16,2304]{1,0:T(8,128)(2,1)S(1)} %get-tuple-element.21), channel_id=1, source_target_pairs={{0,8},{1,9},{2,10},{3,11},{4,12},{5,13},{6,14},{7,15},{8,0},{9,1},... | collective-permute-start | bytes 221192 | tf_op jit(solution)/shard_map/ppermute | solution.py:231
  90.5 8.7 %collective-permute-start.20 = (bf16[16,2304]{1,0:T(8,128)(2,1)S(1)}, bf16[16,2304]{1,0:T(8,128)(2,1)S(1)}, u32[]{:S(2)}, u32[]{:S(2)}) collective-permute-start(bf16[16,2304]{1,0:T(8,128)(2,1)S(1)} %get-tuple-element.20), channel_id=1, source_target_pairs={{0,10},{1,11},{2,8},{3,9},{4,14},{5,15},{6,12},{7,13},{8,2},{9,3},... | collective-permute-start | bytes 221192 | tf_op jit(solution)/shard_map/ppermute | solution.py:231
  92.9 6.3 %collective-permute-start.21 = (bf16[16,2304]{1,0:T(8,128)(2,1)S(1)}, bf16[16,2304]{1,0:T(8,128)(2,1)S(1)}, u32[]{:S(2)}, u32[]{:S(2)}) collective-permute-start(bf16[16,2304]{1,0:T(8,128)(2,1)S(1)} %get-tuple-element.19), channel_id=1, source_target_pairs={{0,12},{1,13},{2,14},{3,15},{4,8},{5,9},{6,10},{7,11},{8,4},{9,5},... | collective-permute-start | bytes 221192 | tf_op jit(solution)/shard_map/ppermute | solution.py:231
  94.1 5.9 %collective-permute-start.22 = (bf16[16,2304]{1,0:T(8,128)(2,1)S(1)}, bf16[16,2304]{1,0:T(8,128)(2,1)S(1)}, u32[]{:S(2)}, u32[]{:S(2)}) collective-permute-start(bf16[16,2304]{1,0:T(8,128)(2,1)S(1)} %get-tuple-element.18), channel_id=1, source_target_pairs={{0,14},{1,15},{2,12},{3,13},{4,10},{5,11},{6,8},{7,9},{8,6},{9,7},... | collective-permute-start | bytes 221192 | tf_op jit(solution)/shard_map/ppermute | solution.py:231
  100.0 2.2 %copy-start.1 = (bf16[16,128,1024]{2,1,0:T(8,128)(2,1)S(1)}, bf16[16,128,1024]{2,1,0:T(8,128)(2,1)}, u32[]{:S(2)}) copy-start(bf16[16,128,1024]{2,1,0:T(8,128)(2,1)} %refs_21_.1) | copy-start | bytes 12582916
  102.2 2.2 %copy-start.2 = (bf16[16,128,1024]{2,1,0:T(8,128)(2,1)S(1)}, bf16[16,128,1024]{2,1,0:T(8,128)(2,1)}, u32[]{:S(2)}) copy-start(bf16[16,128,1024]{2,1,0:T(8,128)(2,1)} %refs_22_.1) | copy-start | bytes 12582916

commit v2 on v1

v2 whole, which is shorter than its diff:
```python
import functools
import math

import jax
import jax.numpy as jnp
from jax import lax
from jax.experimental import pallas as pl
from jax.experimental.pallas import tpu as pltpu
from jax.sharding import PartitionSpec as P

D = 16384
HEADS = 128
KV_HEADS = 8
HEAD_DIM = 128
GROUP = HEADS // KV_HEADS
CORES = 2

norm_eps = 1e-05
rope_base = 500000.0
f32 = jnp.float32
bf16 = jnp.bfloat16


def project_kernel(rows, kept, first, tiles, squared, z_ref, a0_ref, a1_ref, gain_ref, w_hbm, keep_ref, send_ref, raw, acts, w, row_sems, w_sems):
    copies = []
    for at, (begin, width) in enumerate(tiles):
        copies.append(
            pltpu.make_async_copy(
                w_hbm.at[:, pl.ds(first + begin, width)], w.at[:, pl.ds(begin, width)], w_sems.at[at]
            )
        )
    half = kept * CORES * rows
    loads = []
    for m in range(2 * kept):
        source = pl.multiple_of(jnp.bitwise_xor(z_ref[0], m) * rows, rows)
        for j, ref in enumerate((a0_ref, a1_ref)):
            place = (m % 2) * half + ((m // 2) * CORES + j) * rows
            load = pltpu.make_async_copy(
                ref.at[pl.ds(source, rows), :], raw.at[pl.ds(place, rows), :], row_sems.at[m * CORES + j]
            )
            load.start()
            loads.append((place, load))
    for copy in copies:
        copy.start()
    gain = gain_ref[...].astype(f32)
    side = lax.broadcasted_iota(jnp.int32, (rows, HEAD_DIM), 1) < HEAD_DIM // 2
    offset = HEAD_DIM if squared else 0
    for place, load in loads:
        load.wait()
        block = raw[pl.ds(place, rows), :].astype(f32)
        acts[pl.ds(place, rows), :] = (block * gain).astype(bf16)
        if squared:
            square = jnp.broadcast_to(jnp.sum(block * block, axis=1, keepdims=True), (rows, HEAD_DIM))
            square = split(square, side)
            if place < half:
                keep_ref[pl.ds(place, rows), pl.ds(0, HEAD_DIM)] = square
            else:
                send_ref[pl.ds(place - half, rows), pl.ds(0, HEAD_DIM)] = square.astype(bf16)
    for copy, (begin, width) in zip(copies, tiles):
        copy.wait()
        total = jnp.dot(acts[...], w[:, pl.ds(begin, width)], preferred_element_type=f32)
        keep_ref[:, pl.ds(offset + begin, width)] = total[:half]
        send_ref[:, pl.ds(offset + begin, width)] = total[half:].astype(bf16)


def split(square, side):
    upper = square.astype(bf16).astype(f32)
    return jnp.where(side, upper, square - upper)


def joined(parts):
    return parts + pltpu.roll(parts, HEAD_DIM // 2, 1)


def project(z, a0, a1, gain, weight, rows, first, width, squared):
    depth = a0.shape[1]
    kept = a0.shape[0] // rows // 2
    half = kept * CORES * rows
    size = 512
    tiles = tuple((b, min(size, width - b)) for b in range(0, width, size))
    full = width + (HEAD_DIM if squared else 0)
    vmem = pl.BlockSpec(memory_space=pltpu.VMEM)
    hbm = pl.BlockSpec(memory_space=pl.ANY)
    return pl.pallas_call(
        functools.partial(project_kernel, rows, kept, first, tiles, squared),
        out_shape=(
            jax.ShapeDtypeStruct((half, full), f32),
            jax.ShapeDtypeStruct((half, full), bf16),
        ),
        in_specs=[pl.BlockSpec(memory_space=pltpu.SMEM), hbm, hbm, vmem, pl.BlockSpec(memory_space=pltpu.HBM)],
        out_specs=(vmem, vmem),
        scratch_shapes=[
            pltpu.VMEM((2 * half, depth), bf16),
            pltpu.VMEM((2 * half, depth), bf16),
            pltpu.VMEM((depth, width), bf16),
            pltpu.SemaphoreType.DMA((2 * kept * CORES,)),
            pltpu.SemaphoreType.DMA((len(tiles),)),
        ],
        compiler_params=pltpu.CompilerParams(vmem_limit_bytes=36 * 2**20),
        name="project",
    )(z, a0, a1, gain, weight)


def pair_kernel(widths, squared, first_rows, *refs):
    count = len(widths)
    keeps, receiveds = refs[:count], refs[count : 2 * count]
    own_ref, away_ref = refs[2 * count :]
    begin = 0
    for at, (keep, received, width) in enumerate(zip(keeps, receiveds, widths)):
        source = 0
        if squared and at == 0:
            side = lax.broadcasted_iota(jnp.int32, (keep.shape[0], HEAD_DIM), 1) < HEAD_DIM // 2
            columns = pl.ds(0, HEAD_DIM)
            total = split(joined(keep[:, columns] + received[:, columns].astype(f32)), side)
            own_ref[:, columns] = total[:first_rows]
            away_ref[:, columns] = total[first_rows:].astype(bf16)
            source = HEAD_DIM
            begin = HEAD_DIM
        columns = pl.ds(source, width)
        total = keep[:, columns] + received[:, columns].astype(f32)
        own_ref[:, pl.ds(begin, width)] = total[:first_rows]
        away_ref[:, pl.ds(begin, width)] = total[first_rows:].astype(bf16)
        begin += width


def pair_sums(keeps, receiveds, widths, squared, first_rows):
    full = sum(widths) + (HEAD_DIM if squared else 0)
    vmem = pl.BlockSpec(memory_space=pltpu.VMEM)
    return pl.pallas_call(
        functools.partial(pair_kernel, tuple(widths), squared, first_rows),
        out_shape=(
            jax.ShapeDtypeStruct((first_rows, full), f32),
            jax.ShapeDtypeStruct((keeps[0].shape[0] - first_rows, full), bf16),
        ),
        in_specs=[vmem] * (2 * len(widths)),
        out_specs=(vmem, vmem),
        name="pair_sums",
    )(*keeps, *receiveds)


def finish_kernel(squared, *refs):
    if squared:
        own, *others, projected_ref, scale_ref = refs
        columns = pl.ds(0, HEAD_DIM)
        square = joined(own[:, columns])
        for other in others:
            square = square + joined(other[:, columns].astype(f32))
        scale = lax.rsqrt(square * (1.0 / D) + norm_eps)
        scale_ref[...] = scale
        start = HEAD_DIM
    else:
        own, *others, scale_in, projected_ref = refs
        scale = scale_in[...]
        start = 0
    for begin in range(0, projected_ref.shape[1], HEAD_DIM):
        columns = pl.ds(start + begin, HEAD_DIM)
        total = own[:, columns]
        for other in others:
            total = total + other[:, columns].astype(f32)
        projected_ref[:, pl.ds(begin, HEAD_DIM)] = (total * scale).astype(bf16)


def finish(own, others, scale):
    squared = scale is None
    rows, full = own.shape
    width = full - (HEAD_DIM if squared else 0)
    vmem = pl.BlockSpec(memory_space=pltpu.VMEM)
    shapes = [jax.ShapeDtypeStruct((rows, width), bf16)]
    if squared:
        shapes.append(jax.ShapeDtypeStruct((rows, HEAD_DIM), f32))
    inputs = [own, *others] + ([] if squared else [scale])
    results = pl.pallas_call(
        functools.partial(finish_kernel, squared),
        out_shape=tuple(shapes),
        in_specs=[vmem] * len(inputs),
        out_specs=(vmem,) * len(shapes),
        name="finish",
    )(*inputs)
    return (results[0], results[1] if squared else scale)


def attend_kernel(plan, rows, per_source, *refs):
    count = len(plan)
    places_ref, lengths_ref, cosine_ref, sine_ref = refs[:4]
    pieces = refs[4 : 4 + count]
    keys_hbm, values_hbm, attended_ref, cache_rows_ref = refs[4 + count : 8 + count]
    keys, values, table, heads, mixed, sems = refs[8 + count :]
    copies = []
    for r in range(rows):
        pair = (
            pltpu.make_async_copy(keys_hbm.at[r], keys.at[r], sems.at[0, r]),
            pltpu.make_async_copy(values_hbm.at[r], values.at[r], sems.at[1, r]),
        )
        for copy in pair:
            copy.start()
        copies.append(pair)
    for (source, first, width, start), piece in zip(plan, pieces):
        table[places_ref[source], :, pl.ds(first, width)] = piece[pl.ds(start, rows), :].astype(f32)
    cosine = cosine_ref[...]
    sine = sine_ref[...]
    for h in range(HEADS + 2 * KV_HEADS):
        column = (h % per_source) * HEAD_DIM
        head = table[h // per_source, :, pl.ds(column, HEAD_DIM)]
        if h < HEADS + KV_HEADS:
            head = head * cosine + pltpu.roll(head, HEAD_DIM // 2, 1) * sine
        head = head.astype(bf16)
        if h >= HEADS:
            cache_rows_ref[:, pl.ds((h - HEADS) * HEAD_DIM, HEAD_DIM)] = head
        heads[pl.ds(h * rows, rows), :] = head.astype(f32)
    span = keys.shape[1]
    position = lax.broadcasted_iota(jnp.int32, (HEADS, span), 1)
    for r in range(rows):
        for copy in copies[r]:
            copy.wait()
        query = heads[pl.ds(r, HEADS, stride=rows), :]
        own_key = heads[pl.ds(HEADS * rows + r, KV_HEADS, stride=rows), :]
        own_value = heads[pl.ds((HEADS + KV_HEADS) * rows + r, KV_HEADS, stride=rows), :]
        spread = jnp.concatenate(
            [jnp.broadcast_to(own_key[k : k + 1], (GROUP, HEAD_DIM)) for k in range(KV_HEADS)], axis=0
        )
        own_score = jnp.sum(query * spread, axis=1, keepdims=True) * HEAD_DIM ** (-0.5)
        query = query.astype(bf16)
        scores = jnp.concatenate(
            [
                lax.dot_general(
                    query[k * GROUP : (k + 1) * GROUP],
                    keys[r, :, pl.ds(k * HEAD_DIM, HEAD_DIM)],
                    (((1,), (1,)), ((), ())),
                    preferred_element_type=f32,
                )
                for k in range(KV_HEADS)
            ],
            axis=0,
        ) * HEAD_DIM ** (-0.5)
        masked = jnp.where(position < lengths_ref[r], scores, -jnp.inf)
        top = jnp.maximum(jnp.max(masked, axis=1, keepdims=True), own_score)
        raised = jnp.exp(masked - top)
        raised_own = jnp.exp(own_score - top)
        inverse = 1.0 / (jnp.sum(raised, axis=1, keepdims=True) + raised_own)
        weights = (raised * inverse).astype(bf16)
        own_weight = (raised_own * inverse).astype(bf16).astype(f32)
        result = jnp.concatenate(
            [
                jnp.dot(
                    weights[k * GROUP : (k + 1) * GROUP],
                    values[r, :, pl.ds(k * HEAD_DIM, HEAD_DIM)],
                    preferred_element_type=f32,
                )
                + own_weight[k * GROUP : (k + 1) * GROUP] * own_value[k : k + 1]
                for k in range(KV_HEADS)
            ],
            axis=0,
        )
        mixed[pl.ds(r, HEADS, stride=rows), :] = result
    for h in range(HEADS):
        attended_ref[:, pl.ds(h * HEAD_DIM, HEAD_DIM)] = mixed[pl.ds(h * rows, rows), :].astype(bf16)


def attend(plan, pieces, places, lengths, cosine, sine, key_cache, value_cache, sources, width):
    rows, span, kv_width = key_cache.shape
    smem = pl.BlockSpec(memory_space=pltpu.SMEM)
    vmem = pl.BlockSpec(memory_space=pltpu.VMEM)
    hbm = pl.BlockSpec(memory_space=pltpu.HBM)
    return pl.pallas_call(
        functools.partial(attend_kernel, plan, rows, width // HEAD_DIM),
        out_shape=(
            jax.ShapeDtypeStruct((rows, HEADS * HEAD_DIM), bf16),
            jax.ShapeDtypeStruct((rows, 2 * KV_HEADS * HEAD_DIM), bf16),
        ),
        in_specs=[smem, smem, vmem, vmem] + [vmem] * len(pieces) + [hbm, hbm],
        out_specs=(vmem, vmem),
        scratch_shapes=[
            pltpu.VMEM((rows, span, kv_width), bf16),
            pltpu.VMEM((rows, span, kv_width), bf16),
            pltpu.VMEM((sources, rows, width), f32),
            pltpu.VMEM(((HEADS + 2 * KV_HEADS) * rows, HEAD_DIM), f32),
            pltpu.VMEM((HEADS * rows, HEAD_DIM), f32),
            pltpu.SemaphoreType.DMA((2, rows)),
        ],
        compiler_params=pltpu.CompilerParams(vmem_limit_bytes=40 * 2**20),
        name="attend",
    )(places, lengths, cosine, sine, *pieces, key_cache, value_cache)


def rotation(lengths):
    half = HEAD_DIM // 2
    steps = jnp.arange(half, dtype=f32)
    inverse = jnp.exp(steps * (-2.0 * math.log(rope_base) / HEAD_DIM))
    angles = lengths.astype(f32)[:, None] * inverse[None, :]
    cosine = jnp.cos(angles)
    sine = jnp.sin(angles)
    return jnp.concatenate([cosine, cosine], axis=1), jnp.concatenate([-sine, sine], axis=1)


def body(hidden_states, norm_gain, projection_weight, key_cache, value_cache, lengths):
    along_x = lax.axis_size("gx")
    along_z = lax.axis_size("gy")
    chips = along_x // CORES
    rows = key_cache.shape[0]
    width = projection_weight.shape[1]
    z = lax.axis_index("gy").reshape(1).astype(jnp.int32)
    gx = lax.axis_index("gx")
    kept = along_z // 2
    first_rows = CORES * rows

    def on_gx(array, shift, flip):
        pairs = [
            ((x + shift) % chips * CORES + (c ^ flip), x * CORES + c)
            for x in range(chips)
            for c in range(CORES)
        ]
        return lax.ppermute(array, "gx", pairs)

    def on_z(array, flip):
        return lax.ppermute(array, "gy", [(s, s ^ flip) for s in range(along_z)])

    gain = norm_gain.reshape(1, -1)
    there = [on_gx(hidden_states, k, 0) for k in range(1, chips)]
    here = [(hidden_states, on_gx(hidden_states, 0, 1))]
    for array in there:
        here.append((array, on_gx(array, 0, 1)))
    cosine, sine = rotation(lengths)

    unit = HEAD_DIM * 2
    if width % unit == 0 and width >= 4 * unit:
        cuts = {0: split_at(width, unit, 0.5), 1: split_at(width, unit, 0.6)}
    else:
        cuts = {0: (width,), 1: (width,)}
    plan = []
    pieces = []
    before = None
    for k in range(chips):
        chunks = cuts[min(k, 1)]
        a0, a1 = here[k]
        keeps = []
        receiveds = []
        first = 0
        groups = []
        for c, chunk in enumerate(chunks):
            if before is not None and c == 1:
                a0, before = lax.optimization_barrier((a0, before))
            keep, send = project(z, a0, a1, gain, projection_weight, rows, first, chunk, c == 0)
            first += chunk
            keeps.append(keep)
            receiveds.append(on_z(send, 1))
        if k == 0:
            groups = [list(range(len(chunks)))]
        else:
            groups = [[c] for c in range(len(chunks))]
        scale = None
        first = 0
        for group in groups:
            own, away = pair_sums(
                [keeps[c] for c in group],
                [receiveds[c] for c in group],
                [chunks[c] for c in group],
                scale is None,
                first_rows,
            )
            if k == 0:
                before = away
            others = [
                on_z(away if kept == 2 else away[(i - 1) * first_rows : i * first_rows], 2 * i)
                for i in range(1, kept)
            ]
            projected, scale = finish(own, others, scale)
            if k:
                projected = on_gx(projected, chips - k, 0)
            size = projected.shape[1]
            plan.append((k * CORES, first, size, 0))
            pieces.append(projected)
            plan.append((k * CORES + 1, first, size, rows))
            pieces.append(on_gx(projected, 0, 1))
            first += size
    x, core = gx // CORES, gx % CORES
    places = jnp.stack(
        [
            (x + chips - k) % chips * CORES + jnp.bitwise_xor(core, j)
            for k in range(chips)
            for j in range(CORES)
        ]
    ).astype(jnp.int32)
    return attend(plan, pieces, places, lengths, cosine, sine, key_cache, value_cache, along_x, width)


def split_at(width, unit, share):
    first = round(width * share / unit) * unit
    return (first, width - first)


def solution(mesh):
    in_specs = (
        P(("groups", "gx"), "gy"),
        P("gy"),
        P("gy", "gx"),
        P(("groups", "gx", "gy"), None, None),
        P(("groups", "gx", "gy"), None, None),
        P(("groups", "gx", "gy")),
    )
    out_specs = (P(("groups", "gx", "gy"), None), P(("groups", "gx", "gy"), None))
    return jax.shard_map(body, mesh=mesh, in_specs=in_specs, out_specs=out_specs, check_vma=False)
```

time: 117 us -> 123 us (1.051)
  starting transfers between devices: 27 us -> 12.1 us
  waiting for transfers between devices: 22.8 us -> 36.6 us
  local copies, waits for them, and re-layouts: 7.01 us -> 13.9 us
  Pallas kernels: 55.7 us -> 58.5 us
  other arithmetic: 2.42 us -> 0.28 us
    ppermute x3 -> x8, waiting for transfers between devices: 0.01 us -> 19.8 us  [on_gx(): return lax.ppermute(array, 'gx', pairs)]
    ppermute x14 -> x0, starting transfers between devices: 15.4 us -> none  [deliver(): return lax.ppermute(array, ('gx', 'gy'), pairs)]
    ppermute x14 -> x0, waiting for transfers between devices: 8.75 us -> none  [deliver(): return lax.ppermute(array, ('gx', 'gy'), pairs)]
    unnamed x8 -> x34, local copies, waits for them, and re-layouts: 5.43 us -> 13.1 us
    pallas_call x5 -> x10, Pallas kernels: 44.3 us -> 47.1 us  [the longest x4 35.2 us: project(): pl.pallas_call(functools.partial(project_kernel, rows, kept, first, tiles...]
    ppermute x6 -> x7, waiting for transfers between devices: 14 us -> 16.8 us  [on_z(): return lax.ppermute(array, 'gy', [(s, s ^ flip) for s in range(along_z)])]
    ppermute x3 -> x8, starting transfers between devices: 2.94 us -> 5.04 us  [on_gx(): return lax.ppermute(array, 'gx', pairs)]
    ppermute x6 -> x7, starting transfers between devices: 8.61 us -> 7.05 us  [on_z(): return lax.ppermute(array, 'gy', [(s, s ^ flip) for s in range(along_z)])]
  transfers between devices with their start and end apart: 23 -> 15, of which waited for: 6 -> 7; matrix products, arithmetic and copies ran while one was open for 2% -> 1% of each run, Pallas kernels for 37% -> 39%
where the time goes in v2:
time: 123 us; the launch traced here: 122 us
  Pallas kernels  58.5 us (48%)
  waiting for transfers between devices  36.6 us (30%)
  local copies, waits for them, and re-layouts  13.9 us (11%)
  starting transfers between devices  12.1 us (10%)
    pallas_call x4, Pallas kernels, project(): pl.pallas_call(functools.partial(project_kernel, rows, kept, first, tiles...  35.2 us
    ppermute x8, waiting for transfers between devices, on_gx(): return lax.ppermute(array, 'gx', pairs)  19.8 us
    ppermute x7, waiting for transfers between devices, on_z(): return lax.ppermute(array, 'gy', [(s, s ^ flip) for s in range(along_z)])  16.8 us
    unnamed x34, local copies, waits for them, and re-layouts  13.1 us
    pallas_call x1, Pallas kernels, attend(): pl.pallas_call(functools.partial(attend_kernel, plan, rows, width // HEAD...  11.4 us
    ppermute x7, starting transfers between devices, on_z(): return lax.ppermute(array, 'gy', [(s, s ^ flip) for s in range(along_z)])  7.05 us
    pallas_call x3, Pallas kernels, pair_sums(): pl.pallas_call(functools.partial(pair_kernel, tuple(widths), squared, fir...  6.43 us
    pallas_call x3, Pallas kernels, finish(): pl.pallas_call(functools.partial(finish_kernel, squared), out_shape=tuple...  5.47 us
  transfers between devices with their start and end apart: 15, of which 7 were waited for; matrix products, arithmetic and copies ran while one was open for 1% of the time, Pallas kernels for 39%

profile of v2, /device:TPU:0, one launch (start us, length us, event | category | flops | bytes accessed | tf_op | source)
XLA Modules:
  0.0 122.3 jit_solution(8085829129560741167)
XLA Ops:
  0.6 3.0 %collective-permute-start.5 = (bf16[64,4096]{1,0:T(8,128)(2,1)}, bf16[64,4096]{1,0:T(8,128)(2,1)S(1)}, u32[]{:S(2)}, u32[]{:S(2)}) collective-permute-start(bf16[64,4096]{1,0:T(8,128)(2,1)} %a0_ref.3), channel_id=1, source_target_pairs={{8,0},{12,4},{0,8},{4,12},{9,1},{13,5},{1,9},{5,13},{10,2},{14,6},... | collective-permute-start | bytes 1572872 | tf_op jit(solution)/shard_map/ppermute | solution.py:312
  3.6 12.1 %collective-permute-done.5.a0_ref = bf16[64,4096]{1,0:T(8,128)(2,1)S(1)} collective-permute-done((bf16[64,4096]{1,0:T(8,128)(2,1)}, bf16[64,4096]{1,0:T(8,128)(2,1)S(1)}, u32[]{:S(2)}, u32[]{:S(2)}) %collective-permute-start.5) | collective-permute-done | bytes 524320 | tf_op jit(solution)/shard_map/ppermute | solution.py:312
  15.8 0.7 reshape.17.gain_ref
  16.5 0.0 copy-start.2
  16.5 1.0 copy-done.2
  17.5 8.7 %project.4 = (f32[64,2432]{1,0:T(8,128)S(1)}, bf16[64,2432]{1,0:T(8,128)(2,1)S(1)}) custom-call(s32[1]{0:T(128)} %bitcast.4.z_ref, bf16[64,4096]{1,0:T(8,128)(2,1)S(1)} %copy-done.2, bf16[64,4096]{1,0:T(8,128)(2,1)S(1)} %collective-permute-done.a1_ref, bf16[1,4096]{1,0:T(2,128)(2,1)S(1)} %reshape.17.gain_ref, bf16[4096,4608]{1,0:T(8,128)(2,1)} %w_hbm.7), custom_call_target="tpu_custom_call" | custom-call | tf_op jit(solution)/shard_map/project/pallas_call | solution.py:84
  26.3 0.9 copy-done.4
  27.2 1.8 %collective-permute-start.1 = (bf16[64,2432]{1,0:T(8,128)(2,1)S(1)}, bf16[64,2432]{1,0:T(8,128)(2,1)S(1)}, u32[]{:S(2)}, u32[]{:S(2)}) collective-permute-start(bf16[64,2432]{1,0:T(8,128)(2,1)S(1)} %get-tuple-element.22), channel_id=1, source_target_pairs={{0,1},{1,0},{2,3},{3,2},{4,5},{5,4},{6,7},{7,6},{8,9},{9,8},{10,11... | collective-permute-start | bytes 933896 | tf_op jit(solution)/shard_map/ppermute | solution.py:315
  29.0 8.8 %project.5 = (f32[64,2304]{1,0:T(8,128)S(1)}, bf16[64,2304]{1,0:T(8,128)(2,1)S(1)}) custom-call(s32[1]{0:T(128)} %bitcast.4.z_ref, bf16[64,4096]{1,0:T(8,128)(2,1)S(1)} %copy-done.2, bf16[64,4096]{1,0:T(8,128)(2,1)S(1)} %collective-permute-done.a1_ref, bf16[1,4096]{1,0:T(2,128)(2,1)S(1)} %reshape.17.gain_ref, bf16[4096,4608]{1,0:T(8,128)(2,1)} %w_hbm.7), custom_call_target="tpu_custom_call" | custom-call | tf_op jit(solution)/shard_map/project/pallas_call | solution.py:84
  37.8 0.3 collective-permute-start.2
  38.0 10.0 %project.6 = (f32[64,2944]{1,0:T(8,128)S(1)}, bf16[64,2944]{1,0:T(8,128)(2,1)S(1)}) custom-call(s32[1]{0:T(128)} %bitcast.4.z_ref, bf16[64,4096]{1,0:T(8,128)(2,1)S(1)} %collective-permute-done.5.a0_ref, bf16[64,4096]{1,0:T(8,128)(2,1)S(1)} %collective-permute-done.6.a1_ref, bf16[1,4096]{1,0:T(2,128)(2,1)S(1)} %reshape.17.gain_ref, bf16[4096,4608]{1,0:T(8,128)(2,1)} %w_hbm.7), custom_call_target="tpu_custom_call" | custom-call | tf_op jit(solution)/shard_map/project/pallas_call | solution.py:84
  48.0 0.9 copy-done.3
  48.9 1.8 %collective-permute-start.7 = (bf16[64,2944]{1,0:T(8,128)(2,1)S(1)}, bf16[64,2944]{1,0:T(8,128)(2,1)S(1)}, u32[]{:S(2)}, u32[]{:S(2)}) collective-permute-start(bf16[64,2944]{1,0:T(8,128)(2,1)S(1)} %get-tuple-element.28), channel_id=1, source_target_pairs={{0,1},{1,0},{2,3},{3,2},{4,5},{5,4},{6,7},{7,6},{8,9},{9,8},{10,11... | collective-permute-start | bytes 1130504 | tf_op jit(solution)/shard_map/ppermute | solution.py:315
  50.7 0.0 copy-start.10
  50.7 0.7 copy-done.12
  51.5 0.1 copy-done.10
  51.5 2.5 %pair_sums.3 = (f32[32,4736]{1,0:T(8,128)}, bf16[32,4736]{1,0:T(8,128)(2,1)}) custom-call(f32[64,2432]{1,0:T(8,128)} %copy-done.4, f32[64,2304]{1,0:T(8,128)} %copy-done.5, bf16[64,2432]{1,0:T(8,128)(2,1)} %copy-done.10, bf16[64,2304]{1,0:T(8,128)(2,1)} %copy-done.12), custom_call_target="tpu_custom_call" | custom-call | tf_op jit(solution)/shard_map/pair_sums/pallas_call | solution.py:129
  54.0 7.7 %project.7 = (f32[64,1792]{1,0:T(8,128)S(1)}, bf16[64,1792]{1,0:T(8,128)(2,1)S(1)}) custom-call(s32[1]{0:T(128)} %bitcast.4.z_ref, bf16[64,4096]{1,0:T(8,128)(2,1)S(1)} %collective-permute-done.5.a0_ref, bf16[64,4096]{1,0:T(8,128)(2,1)S(1)} %collective-permute-done.6.a1_ref, bf16[1,4096]{1,0:T(2,128)(2,1)S(1)} %reshape.17.gain_ref, bf16[4096,4608]{1,0:T(8,128)(2,1)} %w_hbm.7), custom_call_target="tpu_custom_call" | custom-call | tf_op jit(solution)/shard_map/project/pallas_call | solution.py:84
  61.8 0.0 copy-start.6
  61.8 0.8 copy-done.6
  62.5 0.2 collective-permute-start.11
  62.7 2.8 %collective-permute-start.3 = (bf16[32,4736]{1,0:T(8,128)(2,1)S(1)}, bf16[32,4736]{1,0:T(8,128)(2,1)S(1)}, u32[]{:S(2)}, u32[]{:S(2)}) collective-permute-start(bf16[32,4736]{1,0:T(8,128)(2,1)S(1)} %copy-done.16), channel_id=1, source_target_pairs={{0,2},{1,3},{2,0},{3,1},{4,6},{5,7},{6,4},{7,5},{8,10},{9,11},{10,... | collective-permute-start | bytes 909320 | tf_op jit(solution)/shard_map/ppermute | solution.py:315
  65.6 0.7 copy-done.9
  66.3 2.1 %pair_sums.4 = (f32[32,2944]{1,0:T(8,128)}, bf16[32,2944]{1,0:T(8,128)(2,1)}) custom-call(f32[64,2944]{1,0:T(8,128)} %copy-done.3, bf16[64,2944]{1,0:T(8,128)(2,1)} %copy-done.9), custom_call_target="tpu_custom_call" | custom-call | tf_op jit(solution)/shard_map/pair_sums/pallas_call | solution.py:129
  68.4 0.1 collective-permute-start.8
  68.5 7.2 %collective-permute-done.11.refs_1_ = bf16[64,1792]{1,0:T(8,128)(2,1)S(1)} collective-permute-done((bf16[64,1792]{1,0:T(8,128)(2,1)S(1)}, bf16[64,1792]{1,0:T(8,128)(2,1)S(1)}, u32[]{:S(2)}, u32[]{:S(2)}) %collective-permute-start.11) | collective-permute-done | bytes 229408 | tf_op jit(solution)/shard_map/ppermute | solution.py:315
  75.7 0.7 copy-done.13
  76.4 1.8 %pair_sums.5 = (f32[32,1792]{1,0:T(8,128)}, bf16[32,1792]{1,0:T(8,128)(2,1)}) custom-call(f32[64,1792]{1,0:T(8,128)} %copy-done.6, bf16[64,1792]{1,0:T(8,128)(2,1)} %copy-done.13), custom_call_target="tpu_custom_call" | custom-call | tf_op jit(solution)/shard_map/pair_sums/pallas_call | solution.py:129
  78.3 8.5 %collective-permute-done.3.refs_1_ = bf16[32,4736]{1,0:T(8,128)(2,1)S(1)} collective-permute-done((bf16[32,4736]{1,0:T(8,128)(2,1)S(1)}, bf16[32,4736]{1,0:T(8,128)(2,1)S(1)}, u32[]{:S(2)}, u32[]{:S(2)}) %collective-permute-start.3) | collective-permute-done | bytes 303136 | tf_op jit(solution)/shard_map/ppermute | solution.py:315
  86.7 0.7 copy-done.11
  87.5 2.0 %finish.3 = (bf16[32,4608]{1,0:T(8,128)(2,1)}, f32[32,128]{1,0:T(8,128)}) custom-call(f32[32,4736]{1,0:T(8,128)} %get-tuple-element.24.refs_0_, bf16[32,4736]{1,0:T(8,128)(2,1)} %copy-done.11), custom_call_target="tpu_custom_call" | custom-call | tf_op jit(solution)/shard_map/finish/pallas_call | solution.py:172
  89.4 1.2 collective-permute-done.8.refs_1_
  90.6 0.7 copy-done.14
  91.3 1.8 %finish.4 = (bf16[32,2816]{1,0:T(8,128)(2,1)}, f32[32,128]{1,0:T(8,128)}) custom-call(f32[32,2944]{1,0:T(8,128)} %get-tuple-element.29.refs_0_, bf16[32,2944]{1,0:T(8,128)(2,1)} %copy-done.14), custom_call_target="tpu_custom_call" | custom-call | tf_op jit(solution)/shard_map/finish/pallas_call | solution.py:172
  93.1 0.6 copy-done.15
  93.7 1.7 %finish.5 = bf16[32,1792]{1,0:T(8,128)(2,1)} custom-call(f32[32,1792]{1,0:T(8,128)} %get-tuple-element.35.refs_0_, bf16[32,1792]{1,0:T(8,128)(2,1)} %copy-done.15, f32[32,128]{1,0:T(8,128)} %get-tuple-element.37.refs_2_), custom_call_target="tpu_custom_call" | custom-call | tf_op jit(solution)/shard_map/finish/pallas_call | solution.py:172
  95.4 1.5 %collective-permute-start.13 = (bf16[32,1792]{1,0:T(8,128)(2,1)}, bf16[32,1792]{1,0:T(8,128)(2,1)S(1)}, u32[]{:S(2)}, u32[]{:S(2)}) collective-permute-start(bf16[32,1792]{1,0:T(8,128)(2,1)} %finish.5), channel_id=1, source_target_pairs={{8,0},{12,4},{0,8},{4,12},{9,1},{13,5},{1,9},{5,13},{10,2},{14,6},... | collective-permute-start | bytes 344072 | tf_op jit(solution)/shard_map/ppermute | solution.py:312
  97.0 0.5 collective-permute-start.9
  97.4 0.1 fusion
  97.6 4.0 %collective-permute-done.13.refs_8_ = bf16[32,1792]{1,0:T(8,128)(2,1)S(1)} collective-permute-done((bf16[32,1792]{1,0:T(8,128)(2,1)}, bf16[32,1792]{1,0:T(8,128)(2,1)S(1)}, u32[]{:S(2)}, u32[]{:S(2)}) %collective-permute-start.13) | collective-permute-done | bytes 114720 | tf_op jit(solution)/shard_map/ppermute | solution.py:312
  101.6 2.4 %collective-permute-done.9.refs_6_ = bf16[32,2816]{1,0:T(8,128)(2,1)S(1)} collective-permute-done((bf16[32,2816]{1,0:T(8,128)(2,1)}, bf16[32,2816]{1,0:T(8,128)(2,1)S(1)}, u32[]{:S(2)}, u32[]{:S(2)}) %collective-permute-start.9) | collective-permute-done | bytes 180256 | tf_op jit(solution)/shard_map/ppermute | solution.py:312
  104.0 0.1 pad_add_fusion.refs_0_
  104.1 0.1 pad_maximum_fusion
  104.2 1.3 %collective-permute-done.10.refs_7_ = bf16[32,2816]{1,0:T(8,128)(2,1)S(1)} collective-permute-done((bf16[32,2816]{1,0:T(8,128)(2,1)S(1)}, bf16[32,2816]{1,0:T(8,128)(2,1)S(1)}, u32[]{:S(2)}, u32[]{:S(2)}) %collective-permute-start.10) | collective-permute-done | bytes 180256 | tf_op jit(solution)/shard_map/ppermute | solution.py:312
  105.4 2.2 %copy-done = bf16[16,128,1024]{2,1,0:T(8,128)(2,1)S(1)} copy-done((bf16[16,128,1024]{2,1,0:T(8,128)(2,1)S(1)}, bf16[16,128,1024]{2,1,0:T(8,128)(2,1)}, u32[]{:S(2)}) %copy-start) | copy-done | bytes 4194328
  107.6 2.2 %copy-done.1 = bf16[16,128,1024]{2,1,0:T(8,128)(2,1)S(1)} copy-done((bf16[16,128,1024]{2,1,0:T(8,128)(2,1)S(1)}, bf16[16,128,1024]{2,1,0:T(8,128)(2,1)}, u32[]{:S(2)}) %copy-start.1) | copy-done | bytes 4194328
  109.8 1.0 copy-done.7
  110.8 11.4 %attend.1 = (bf16[16,16384]{1,0:T(8,128)(2,1)}, bf16[16,2048]{1,0:T(8,128)(2,1)}) custom-call(s32[4]{0:T(128)S(1)} %pad_add_fusion.refs_0_, s32[16]{0:T(128)S(1)} %copy-done.8, f32[16,128]{1,0:T(8,128)S(1)} %get-tuple-element.41.refs_2_, f32[16,128]{1,0:T(8,128)S(1)} %get-tuple-element.42.refs_3_, bf16[32,4608]{1,0:T(8,128)(2,1)S(1)} %copy-done.7, ...), custom_call_target="tpu_custom_call" | custom-call | tf_op jit(solution)/shard_map/attend/pallas_call | solution.py:264
  (33 shorter events, 0.1 us)
Async XLA Ops:
  0.6 15.1 %collective-permute-start.5 = (bf16[64,4096]{1,0:T(8,128)(2,1)}, bf16[64,4096]{1,0:T(8,128)(2,1)S(1)}, u32[]{:S(2)}, u32[]{:S(2)}) collective-permute-start(bf16[64,4096]{1,0:T(8,128)(2,1)} %a0_ref.3), channel_id=1, source_target_pairs={{8,0},{12,4},{0,8},{4,12},{9,1},{13,5},{1,9},{5,13},{10,2},{14,6},... | collective-permute-start | bytes 1572872 | tf_op jit(solution)/shard_map/ppermute | solution.py:312
  3.6 12.9 %collective-permute-start = (bf16[64,4096]{1,0:T(8,128)(2,1)}, bf16[64,4096]{1,0:T(8,128)(2,1)S(1)}, u32[]{:S(2)}, u32[]{:S(2)}) collective-permute-start(bf16[64,4096]{1,0:T(8,128)(2,1)} %a0_ref.3), channel_id=1, source_target_pairs={{4,0},{0,4},{12,8},{8,12},{5,1},{1,5},{13,9},{9,13},{6,2},{2,6},{1... | collective-permute-start | bytes 1572872 | tf_op jit(solution)/shard_map/ppermute | solution.py:312
  15.8 22.3 %collective-permute-start.6 = (bf16[64,4096]{1,0:T(8,128)(2,1)S(1)}, bf16[64,4096]{1,0:T(8,128)(2,1)S(1)}, u32[]{:S(2)}, u32[]{:S(2)}) collective-permute-start(bf16[64,4096]{1,0:T(8,128)(2,1)S(1)} %collective-permute-done.5.a0_ref), channel_id=1, source_target_pairs={{4,0},{0,4},{12,8},{8,12},{5,1},{1,5},{13,9},{9,13},{6,2},{2,6},{1... | collective-permute-start | bytes 1572872 | tf_op jit(solution)/shard_map/ppermute | solution.py:312
  16.5 1.0 copy-start.2
  26.3 0.9 copy-start.4
  27.2 23.6 %collective-permute-start.1 = (bf16[64,2432]{1,0:T(8,128)(2,1)S(1)}, bf16[64,2432]{1,0:T(8,128)(2,1)S(1)}, u32[]{:S(2)}, u32[]{:S(2)}) collective-permute-start(bf16[64,2432]{1,0:T(8,128)(2,1)S(1)} %get-tuple-element.22), channel_id=1, source_target_pairs={{0,1},{1,0},{2,3},{3,2},{4,5},{5,4},{6,7},{7,6},{8,9},{9,8},{10,11... | collective-permute-start | bytes 933896 | tf_op jit(solution)/shard_map/ppermute | solution.py:315
  37.7 10.3 %copy-start.5 = (f32[64,2304]{1,0:T(8,128)}, f32[64,2304]{1,0:T(8,128)S(1)}, u32[]{:S(2)}) copy-start(f32[64,2304]{1,0:T(8,128)S(1)} %get-tuple-element.21.refs_1_) | copy-start | bytes 1769476
  37.8 13.0 %collective-permute-start.2 = (bf16[64,2304]{1,0:T(8,128)(2,1)S(1)}, bf16[64,2304]{1,0:T(8,128)(2,1)S(1)}, u32[]{:S(2)}, u32[]{:S(2)}) collective-permute-start(bf16[64,2304]{1,0:T(8,128)(2,1)S(1)} %get-tuple-element.23), channel_id=1, source_target_pairs={{0,1},{1,0},{2,3},{3,2},{4,5},{5,4},{6,7},{7,6},{8,9},{9,8},{10,11... | collective-permute-start | bytes 884744 | tf_op jit(solution)/shard_map/ppermute | solution.py:315
  48.0 0.9 copy-start.3
  48.9 16.7 %collective-permute-start.7 = (bf16[64,2944]{1,0:T(8,128)(2,1)S(1)}, bf16[64,2944]{1,0:T(8,128)(2,1)S(1)}, u32[]{:S(2)}, u32[]{:S(2)}) collective-permute-start(bf16[64,2944]{1,0:T(8,128)(2,1)S(1)} %get-tuple-element.28), channel_id=1, source_target_pairs={{0,1},{1,0},{2,3},{3,2},{4,5},{5,4},{6,7},{7,6},{8,9},{9,8},{10,11... | collective-permute-start | bytes 1130504 | tf_op jit(solution)/shard_map/ppermute | solution.py:315
  50.7 0.7 copy-start.12
  50.7 0.8 copy-start.10
  54.0 8.7 %copy-start.16 = (bf16[32,4736]{1,0:T(8,128)(2,1)S(1)}, bf16[32,4736]{1,0:T(8,128)(2,1)}, u32[]{:S(2)}) copy-start(bf16[32,4736]{1,0:T(8,128)(2,1)} %get-tuple-element.25) | copy-start | bytes 909316
  54.0 24.2 %copy-start.8 = (s32[16]{0:T(128)S(1)}, s32[16]{0:T(128)}, u32[]{:S(2)}) copy-start(s32[16]{0:T(128)} %refs_1_.1) | copy-start | bytes 196
  61.8 0.8 copy-start.6
  62.5 13.2 %collective-permute-start.11 = (bf16[64,1792]{1,0:T(8,128)(2,1)S(1)}, bf16[64,1792]{1,0:T(8,128)(2,1)S(1)}, u32[]{:S(2)}, u32[]{:S(2)}) collective-permute-start(bf16[64,1792]{1,0:T(8,128)(2,1)S(1)} %get-tuple-element.34), channel_id=1, source_target_pairs={{0,1},{1,0},{2,3},{3,2},{4,5},{5,4},{6,7},{7,6},{8,9},{9,8},{10,11... | collective-permute-start | bytes 688136 | tf_op jit(solution)/shard_map/ppermute | solution.py:315
  62.7 24.0 %collective-permute-start.3 = (bf16[32,4736]{1,0:T(8,128)(2,1)S(1)}, bf16[32,4736]{1,0:T(8,128)(2,1)S(1)}, u32[]{:S(2)}, u32[]{:S(2)}) collective-permute-start(bf16[32,4736]{1,0:T(8,128)(2,1)S(1)} %copy-done.16), channel_id=1, source_target_pairs={{0,2},{1,3},{2,0},{3,1},{4,6},{5,7},{6,4},{7,5},{8,10},{9,11},{10,... | collective-permute-start | bytes 909320 | tf_op jit(solution)/shard_map/ppermute | solution.py:315
  65.6 0.7 copy-start.9
  68.4 22.2 %collective-permute-start.8 = (bf16[32,2944]{1,0:T(8,128)(2,1)}, bf16[32,2944]{1,0:T(8,128)(2,1)S(1)}, u32[]{:S(2)}, u32[]{:S(2)}) collective-permute-start(bf16[32,2944]{1,0:T(8,128)(2,1)} %get-tuple-element.30), channel_id=1, source_target_pairs={{0,2},{1,3},{2,0},{3,1},{4,6},{5,7},{6,4},{7,5},{8,10},{9,11},{10,... | collective-permute-start | bytes 565256 | tf_op jit(solution)/shard_map/ppermute | solution.py:315
  75.7 0.7 copy-start.13
  78.2 14.9 %collective-permute-start.12 = (bf16[32,1792]{1,0:T(8,128)(2,1)}, bf16[32,1792]{1,0:T(8,128)(2,1)S(1)}, u32[]{:S(2)}, u32[]{:S(2)}) collective-permute-start(bf16[32,1792]{1,0:T(8,128)(2,1)} %get-tuple-element.36), channel_id=1, source_target_pairs={{0,2},{1,3},{2,0},{3,1},{4,6},{5,7},{6,4},{7,5},{8,10},{9,11},{10,... | collective-permute-start | bytes 344072 | tf_op jit(solution)/shard_map/ppermute | solution.py:315
  86.7 0.7 copy-start.11
  89.4 14.7 %collective-permute-start.4 = (bf16[32,4608]{1,0:T(8,128)(2,1)}, bf16[32,4608]{1,0:T(8,128)(2,1)S(1)}, u32[]{:S(2)}, u32[]{:S(2)}) collective-permute-start(bf16[32,4608]{1,0:T(8,128)(2,1)} %get-tuple-element.26.refs_4_), channel_id=1, source_target_pairs={{4,0},{0,4},{12,8},{8,12},{5,1},{1,5},{13,9},{9,13},{6,2},{2,6},{1... | collective-permute-start | bytes 884744 | tf_op jit(solution)/shard_map/ppermute | solution.py:312
  90.6 0.7 copy-start.14
  93.1 0.6 copy-start.15
  95.4 6.2 %collective-permute-start.13 = (bf16[32,1792]{1,0:T(8,128)(2,1)}, bf16[32,1792]{1,0:T(8,128)(2,1)S(1)}, u32[]{:S(2)}, u32[]{:S(2)}) collective-permute-start(bf16[32,1792]{1,0:T(8,128)(2,1)} %finish.5), channel_id=1, source_target_pairs={{8,0},{12,4},{0,8},{4,12},{9,1},{13,5},{1,9},{5,13},{10,2},{14,6},... | collective-permute-start | bytes 344072 | tf_op jit(solution)/shard_map/ppermute | solution.py:312
  97.0 7.1 %collective-permute-start.9 = (bf16[32,2816]{1,0:T(8,128)(2,1)}, bf16[32,2816]{1,0:T(8,128)(2,1)S(1)}, u32[]{:S(2)}, u32[]{:S(2)}) collective-permute-start(bf16[32,2816]{1,0:T(8,128)(2,1)} %get-tuple-element.31), channel_id=1, source_target_pairs={{8,0},{12,4},{0,8},{4,12},{9,1},{13,5},{1,9},{5,13},{10,2},{14,6},... | collective-permute-start | bytes 540680 | tf_op jit(solution)/shard_map/ppermute | solution.py:312
  101.6 2.5 %collective-permute-start.14 = (bf16[32,1792]{1,0:T(8,128)(2,1)S(1)}, bf16[32,1792]{1,0:T(8,128)(2,1)S(1)}, u32[]{:S(2)}, u32[]{:S(2)}) collective-permute-start(bf16[32,1792]{1,0:T(8,128)(2,1)S(1)} %collective-permute-done.13.refs_8_), channel_id=1, source_target_pairs={{4,0},{0,4},{12,8},{8,12},{5,1},{1,5},{13,9},{9,13},{6,2},{2,6},{1... | collective-permute-start | bytes 344072 | tf_op jit(solution)/shard_map/ppermute | solution.py:312
  104.0 1.4 %collective-permute-start.10 = (bf16[32,2816]{1,0:T(8,128)(2,1)S(1)}, bf16[32,2816]{1,0:T(8,128)(2,1)S(1)}, u32[]{:S(2)}, u32[]{:S(2)}) collective-permute-start(bf16[32,2816]{1,0:T(8,128)(2,1)S(1)} %collective-permute-done.9.refs_6_), channel_id=1, source_target_pairs={{4,0},{0,4},{12,8},{8,12},{5,1},{1,5},{13,9},{9,13},{6,2},{2,6},{1... | collective-permute-start | bytes 540680 | tf_op jit(solution)/shard_map/ppermute | solution.py:312
  105.4 2.2 %copy-start = (bf16[16,128,1024]{2,1,0:T(8,128)(2,1)S(1)}, bf16[16,128,1024]{2,1,0:T(8,128)(2,1)}, u32[]{:S(2)}) copy-start(bf16[16,128,1024]{2,1,0:T(8,128)(2,1)} %refs_10_.1) | copy-start | bytes 12582916
  107.6 2.2 %copy-start.1 = (bf16[16,128,1024]{2,1,0:T(8,128)(2,1)S(1)}, bf16[16,128,1024]{2,1,0:T(8,128)(2,1)}, u32[]{:S(2)}) copy-start(bf16[16,128,1024]{2,1,0:T(8,128)(2,1)} %refs_11_.1) | copy-start | bytes 12582916
  109.8 1.0 copy-start.7

commit v3 on v2

v3 whole, which is shorter than its diff:
```python
import functools
import math

import jax
import jax.numpy as jnp
from jax import lax
from jax.experimental import pallas as pl
from jax.experimental.pallas import tpu as pltpu
from jax.sharding import PartitionSpec as P

D = 16384
HEADS = 128
KV_HEADS = 8
HEAD_DIM = 128
GROUP = HEADS // KV_HEADS
CORES = 2
IN_FLIGHT = 2

norm_eps = 1e-05
rope_base = 500000.0
f32 = jnp.float32
bf16 = jnp.bfloat16


def project_kernel(rows, kept, first, tiles, squared, z_ref, a0_ref, a1_ref, gain_ref, w_hbm, keep_hbm, send_ref, raw, acts, w, keep, row_sems, w_sems, keep_sems):
    half = kept * CORES * rows
    loads = []
    for m in range(2 * kept):
        source = pl.multiple_of(jnp.bitwise_xor(z_ref[0], m) * rows, rows)
        for j, ref in enumerate((a0_ref, a1_ref)):
            place = (m % 2) * half + ((m // 2) * CORES + j) * rows
            load = pltpu.make_async_copy(
                ref.at[pl.ds(source, rows), :], raw.at[pl.ds(place, rows), :], row_sems.at[m * CORES + j]
            )
            load.start()
            loads.append((place, load))
    copies = [
        pltpu.make_async_copy(
            w_hbm.at[:, pl.ds(first + begin, width)], w.at[:, pl.ds(begin, width)], w_sems.at[at]
        )
        for at, (begin, width) in enumerate(tiles)
    ]
    for copy in copies[:IN_FLIGHT]:
        copy.start()
    gain = gain_ref[...].astype(f32)
    offset = HEAD_DIM if squared else 0
    for place, load in loads:
        load.wait()
        block = raw[pl.ds(place, rows), :].astype(f32)
        acts[pl.ds(place, rows), :] = (block * gain).astype(bf16)
        if squared:
            square = jnp.broadcast_to(jnp.sum(block * block, axis=1, keepdims=True), (rows, HEAD_DIM))
            if place < half:
                keep[pl.ds(place, rows), pl.ds(0, HEAD_DIM)] = square
            else:
                upper = square.astype(bf16)
                send_ref[pl.ds(place - half, rows), pl.ds(0, HEAD_DIM)] = upper
                lower = (square - upper.astype(f32)).astype(bf16)
                send_ref[pl.ds(place - half, rows), pl.ds(HEAD_DIM, HEAD_DIM)] = lower
    stores = []
    for at, (copy, (begin, width)) in enumerate(zip(copies, tiles)):
        copy.wait()
        if at + IN_FLIGHT < len(copies):
            copies[at + IN_FLIGHT].start()
        total = jnp.dot(acts[...], w[:, pl.ds(begin, width)], preferred_element_type=f32)
        keep[:, pl.ds(offset + begin, width)] = total[:half]
        send_ref[:, pl.ds(2 * offset + begin, width)] = total[half:].astype(bf16)
        left = 0 if at == 0 else offset + begin
        columns = pl.ds(left, offset + begin + width - left)
        store = pltpu.make_async_copy(keep.at[:, columns], keep_hbm.at[:, columns], keep_sems.at[at])
        store.start()
        stores.append(store)
    for store in stores:
        store.wait()


def tiles_of(width):
    sizes = []
    while width:
        size = min(512, width) if width >= 1024 or width % 256 else 256
        sizes.append(size)
        width -= size
    return tuple((sum(sizes[:i]), size) for i, size in enumerate(sizes))


def project(z, a0, a1, gain, weight, rows, first, width, squared):
    depth = a0.shape[1]
    kept = a0.shape[0] // rows // 2
    half = kept * CORES * rows
    tiles = tiles_of(width)
    full = width + (HEAD_DIM if squared else 0)
    vmem = pl.BlockSpec(memory_space=pltpu.VMEM)
    hbm = pl.BlockSpec(memory_space=pltpu.HBM)
    return pl.pallas_call(
        functools.partial(project_kernel, rows, kept, first, tiles, squared),
        out_shape=(
            jax.ShapeDtypeStruct((half, full), f32),
            jax.ShapeDtypeStruct((half, 2 * full - width), bf16),
        ),
        in_specs=[pl.BlockSpec(memory_space=pltpu.SMEM), hbm, hbm, vmem, hbm],
        out_specs=(hbm, vmem),
        scratch_shapes=[
            pltpu.VMEM((2 * half, depth), bf16),
            pltpu.VMEM((2 * half, depth), bf16),
            pltpu.VMEM((depth, width), bf16),
            pltpu.VMEM((half, full), f32),
            pltpu.SemaphoreType.DMA((2 * kept * CORES,)),
            pltpu.SemaphoreType.DMA((len(tiles),)),
            pltpu.SemaphoreType.DMA((len(tiles),)),
        ],
        compiler_params=pltpu.CompilerParams(vmem_limit_bytes=32 * 2**20),
        name="project",
    )(z, a0, a1, gain, weight)


def attend_kernel(plan, rows, per_source, *refs):
    count = len(plan)
    places_ref, lengths_ref, cosine_ref, sine_ref = refs[:4]
    pieces = refs[4 : 4 + count]
    keys_hbm, values_hbm, attended_ref, cache_rows_ref = refs[4 + count : 8 + count]
    keys, values, table, heads, mixed, piece_sems, sems = refs[8 + count :]
    fills = []
    for at, ((source, first, width, start), piece) in enumerate(zip(plan, pieces)):
        fill = pltpu.make_async_copy(
            piece.at[pl.ds(start, rows), :], table.at[places_ref[source], :, pl.ds(first, width)], piece_sems.at[at]
        )
        fill.start()
        fills.append(fill)
    batch = 4
    copies = []
    for at in range(0, rows, batch):
        span = pl.ds(at, batch)
        copies.append(pltpu.make_async_copy(keys_hbm.at[span], keys.at[span], sems.at[0, at // batch]))
        copies.append(pltpu.make_async_copy(values_hbm.at[span], values.at[span], sems.at[1, at // batch]))
    for copy in copies:
        copy.start()
    for fill in fills:
        fill.wait()
    cosine = cosine_ref[...]
    sine = sine_ref[...]
    for h in range(HEADS + 2 * KV_HEADS):
        column = (h % per_source) * HEAD_DIM
        head = table[h // per_source, :, pl.ds(column, HEAD_DIM)].astype(f32)
        if h < HEADS + KV_HEADS:
            head = head * cosine + pltpu.roll(head, HEAD_DIM // 2, 1) * sine
        head = head.astype(bf16)
        if h >= HEADS:
            cache_rows_ref[:, pl.ds((h - HEADS) * HEAD_DIM, HEAD_DIM)] = head
        heads[pl.ds(h * rows, rows), :] = head.astype(f32)
    span = keys.shape[1]
    position = lax.broadcasted_iota(jnp.int32, (HEADS, span), 1)
    for r in range(rows):
        if r % batch == 0:
            copies[r // batch * 2].wait()
            copies[r // batch * 2 + 1].wait()
        query = heads[pl.ds(r, HEADS, stride=rows), :]
        own_key = heads[pl.ds(HEADS * rows + r, KV_HEADS, stride=rows), :]
        own_value = heads[pl.ds((HEADS + KV_HEADS) * rows + r, KV_HEADS, stride=rows), :]
        spread = jnp.concatenate(
            [jnp.broadcast_to(own_key[k : k + 1], (GROUP, HEAD_DIM)) for k in range(KV_HEADS)], axis=0
        )
        own_score = jnp.sum(query * spread, axis=1, keepdims=True) * HEAD_DIM ** (-0.5)
        query = query.astype(bf16)
        scores = jnp.concatenate(
            [
                lax.dot_general(
                    query[k * GROUP : (k + 1) * GROUP],
                    keys[r, :, pl.ds(k * HEAD_DIM, HEAD_DIM)],
                    (((1,), (1,)), ((), ())),
                    preferred_element_type=f32,
                )
                for k in range(KV_HEADS)
            ],
            axis=0,
        ) * HEAD_DIM ** (-0.5)
        masked = jnp.where(position < lengths_ref[r], scores, -jnp.inf)
        top = jnp.maximum(jnp.max(masked, axis=1, keepdims=True), own_score)
        raised = jnp.exp(masked - top)
        raised_own = jnp.exp(own_score - top)
        inverse = 1.0 / (jnp.sum(raised, axis=1, keepdims=True) + raised_own)
        weights = (raised * inverse).astype(bf16)
        own_weight = (raised_own * inverse).astype(bf16).astype(f32)
        result = jnp.concatenate(
            [
                jnp.dot(
                    weights[k * GROUP : (k + 1) * GROUP],
                    values[r, :, pl.ds(k * HEAD_DIM, HEAD_DIM)],
                    preferred_element_type=f32,
                )
                + own_weight[k * GROUP : (k + 1) * GROUP] * own_value[k : k + 1]
                for k in range(KV_HEADS)
            ],
            axis=0,
        )
        mixed[pl.ds(r, HEADS, stride=rows), :] = result
    for h in range(HEADS):
        attended_ref[:, pl.ds(h * HEAD_DIM, HEAD_DIM)] = mixed[pl.ds(h * rows, rows), :].astype(bf16)


def attend(plan, pieces, places, lengths, cosine, sine, key_cache, value_cache, sources, width):
    rows, span, kv_width = key_cache.shape
    smem = pl.BlockSpec(memory_space=pltpu.SMEM)
    vmem = pl.BlockSpec(memory_space=pltpu.VMEM)
    hbm = pl.BlockSpec(memory_space=pltpu.HBM)
    return pl.pallas_call(
        functools.partial(attend_kernel, plan, rows, width // HEAD_DIM),
        out_shape=(
            jax.ShapeDtypeStruct((rows, HEADS * HEAD_DIM), bf16),
            jax.ShapeDtypeStruct((rows, 2 * KV_HEADS * HEAD_DIM), bf16),
        ),
        in_specs=[smem, smem, vmem, vmem] + [hbm] * len(pieces) + [hbm, hbm],
        out_specs=(vmem, vmem),
        scratch_shapes=[
            pltpu.VMEM((rows, span, kv_width), bf16),
            pltpu.VMEM((rows, span, kv_width), bf16),
            pltpu.VMEM((sources, rows, width), bf16),
            pltpu.VMEM(((HEADS + 2 * KV_HEADS) * rows, HEAD_DIM), f32),
            pltpu.VMEM((HEADS * rows, HEAD_DIM), f32),
            pltpu.SemaphoreType.DMA((len(pieces),)),
            pltpu.SemaphoreType.DMA((2, rows // 4)),
        ],
        compiler_params=pltpu.CompilerParams(vmem_limit_bytes=24 * 2**20),
        name="attend",
    )(places, lengths, cosine, sine, *pieces, key_cache, value_cache)


def rotation(lengths):
    half = HEAD_DIM // 2
    steps = jnp.arange(half, dtype=f32)
    inverse = jnp.exp(steps * (-2.0 * math.log(rope_base) / HEAD_DIM))
    angles = lengths.astype(f32)[:, None] * inverse[None, :]
    cosine = jnp.cos(angles)
    sine = jnp.sin(angles)
    return jnp.concatenate([cosine, cosine], axis=1), jnp.concatenate([-sine, sine], axis=1)


def body(hidden_states, norm_gain, projection_weight, key_cache, value_cache, lengths):
    along_x = lax.axis_size("gx")
    along_z = lax.axis_size("gy")
    chips = along_x // CORES
    rows = key_cache.shape[0]
    width = projection_weight.shape[1]
    z = lax.axis_index("gy").reshape(1).astype(jnp.int32)
    gx = lax.axis_index("gx")
    kept = along_z // 2
    first_rows = CORES * rows

    def on_gx(array, shift, flip):
        pairs = [
            ((x + shift) % chips * CORES + (c ^ flip), x * CORES + c)
            for x in range(chips)
            for c in range(CORES)
        ]
        return lax.ppermute(array, "gx", pairs)

    def on_z(array, flip):
        return lax.ppermute(array, "gy", [(s, s ^ flip) for s in range(along_z)])

    def in_hbm(array):
        return pltpu.with_memory_space_constraint(array, pltpu.HBM)

    gain = norm_gain.reshape(1, -1)
    weight = in_hbm(projection_weight)
    there = [on_gx(hidden_states, k, 0) for k in range(1, chips)]
    here = [(in_hbm(hidden_states), on_gx(hidden_states, 0, 1))]
    cosine, sine = rotation(lengths)

    unit = HEAD_DIM * 2
    if width % unit == 0 and width >= 4 * unit:
        cuts = {0: split_at(width, unit, 0.5), 1: split_at(width, unit, 0.6)}
    else:
        cuts = {0: (width,), 1: (width,)}
    plan = []
    pieces = []

    def after(array, other):
        return lax.optimization_barrier((array, other))[0]

    kinds = range(chips)
    chunks = {k: cuts[min(k, 1)] for k in kinds}
    keeps = {k: [] for k in kinds}
    receiveds = {k: [] for k in kinds}
    aways = {}

    def add_pairs(k):
        owns, away = [], []
        for c, chunk in enumerate(chunks[k]):
            keep, received = keeps[k][c], receiveds[k][c]
            if k and c:
                received = after(received, away[2])
            for part, start in ((owns, 0), (away, first_rows)):
                span = slice(start, start + first_rows) if start == 0 else slice(start, None)
                if c == 0:
                    square = (
                        keep[span, :HEAD_DIM]
                        + received[span, :HEAD_DIM].astype(f32)
                        + received[span, HEAD_DIM : 2 * HEAD_DIM].astype(f32)
                    )
                    if start:
                        upper = lax.reduce_precision(square, 8, 7)
                        part.append(upper.astype(bf16))
                        part.append((square - upper).astype(bf16))
                    else:
                        part.append(square)
                skip = HEAD_DIM if c == 0 else 0
                total = keep[span, skip:] + received[span, 2 * skip :].astype(f32)
                part.append(total.astype(bf16) if start else total)
        if k == 0:
            return owns, [jnp.concatenate(away, axis=1)]
        return owns, [jnp.concatenate(away[:3], axis=1), *away[3:]]

    owns = {}
    for k in kinds:
        if k:
            a0 = after(there[k - 1], keeps[k - 1])
            a1 = on_gx(a0, 0, 1)
        else:
            a0, a1 = here[0]
        first = 0
        for c, chunk in enumerate(chunks[k]):
            if k and c == 1:
                a0 = after(a0, aways[k - 1])
            keep, send = project(z, a0, a1, gain, weight, rows, first, chunk, c == 0)
            first += chunk
            keeps[k].append(keep)
            receiveds[k].append(on_z(send, 1))
        owns[k], aways[k] = add_pairs(k)
    for k in kinds:
        arrived = [
            [on_z(away[(i - 1) * first_rows : i * first_rows], 2 * i) for i in range(1, kept)]
            for away in aways[k]
        ]
        if k + 1 < chips:
            arrived = after(arrived, keeps[k + 1])
        square = owns[k][0]
        for other in arrived[0]:
            square = square + other[:, :HEAD_DIM].astype(f32) + other[:, HEAD_DIM : 2 * HEAD_DIM].astype(f32)
        scale = lax.rsqrt(square[:, :1] * (1.0 / D) + norm_eps)
        done = []
        first = 0
        for c, chunk in enumerate(chunks[k]):
            total = owns[k][c + 1]
            for other in arrived[0] if k == 0 else arrived[c]:
                skip = 2 * HEAD_DIM + first if k == 0 else (2 * HEAD_DIM if c == 0 else 0)
                total = total + other[:, skip : skip + chunk].astype(f32)
            done.append((total * scale).astype(bf16))
            first += chunk
        first = 0
        for projected in [jnp.concatenate(done, axis=1)] if k == 0 else done:
            if k:
                projected = on_gx(projected, chips - k, 0)
            size = projected.shape[1]
            plan.append((k * CORES, first, size, 0))
            pieces.append(projected)
            plan.append((k * CORES + 1, first, size, rows))
            pieces.append(on_gx(projected, 0, 1))
            first += size
    x, core = gx // CORES, gx % CORES
    places = jnp.stack(
        [
            (x + chips - k) % chips * CORES + jnp.bitwise_xor(core, j)
            for k in range(chips)
            for j in range(CORES)
        ]
    ).astype(jnp.int32)
    return attend(
        plan, pieces, places, lengths, cosine, sine, in_hbm(key_cache), in_hbm(value_cache), along_x, width
    )


def split_at(width, unit, share):
    first = round(width * share / unit) * unit
    return (first, width - first)


def solution(mesh):
    in_specs = (
        P(("groups", "gx"), "gy"),
        P("gy"),
        P("gy", "gx"),
        P(("groups", "gx", "gy"), None, None),
        P(("groups", "gx", "gy"), None, None),
        P(("groups", "gx", "gy")),
    )
    out_specs = (P(("groups", "gx", "gy"), None), P(("groups", "gx", "gy"), None))
    return jax.shard_map(body, mesh=mesh, in_specs=in_specs, out_specs=out_specs, check_vma=False)
```

time: 123 us -> 101 us (0.82)
  local copies, waits for them, and re-layouts: 13.9 us -> 0.73 us
  Pallas kernels: 58.5 us -> 47.9 us
  starting transfers between devices: 12.1 us -> 15.3 us
  waiting for transfers between devices: 36.6 us -> 34.7 us
    unnamed x34 -> x2, local copies, waits for them, and re-layouts: 13.1 us -> 0.01 us
    ppermute x8, waiting for transfers between devices: 19.8 us -> 6.78 us  [on_gx(): return lax.ppermute(array, 'gx', pairs)]
    pallas_call x6 -> x0, Pallas kernels: 11.9 us -> none  [the longest x3 6.43 us: pair_sums(): pl.pallas_call(functools.partial(pair_kernel, tuple(widths), squared, fir...]
    ppermute x7, waiting for transfers between devices: 16.8 us -> 27.9 us  [on_z(): return lax.ppermute(array, 'gy', [(s, s ^ flip) for s in range(along_z)])]
    ppermute x7, starting transfers between devices: 7.05 us -> 10 us  [on_z(): return lax.ppermute(array, 'gy', [(s, s ^ flip) for s in range(along_z)])]
    pallas_call x4, Pallas kernels: 35.2 us -> 36.9 us  [project(): pl.pallas_call(functools.partial(project_kernel, rows, kept, first, tiles...]
  transfers between devices with their start and end apart: 15 -> 15, of which waited for: 7 -> 6; matrix products, arithmetic and copies ran while one was open for 1% -> 2% of each run, Pallas kernels for 39% -> 37%
where the time goes in v3:
time: 101 us
  Pallas kernels  47.9 us (47%)
  waiting for transfers between devices  34.7 us (34%)
  starting transfers between devices  15.3 us (15%)
  other arithmetic  1.02 us (1%)
  between operations  1.02 us (1%)
    pallas_call x4, Pallas kernels, project(): pl.pallas_call(functools.partial(project_kernel, rows, kept, first, tiles...  36.9 us
    ppermute x7, waiting for transfers between devices, on_z(): return lax.ppermute(array, 'gy', [(s, s ^ flip) for s in range(along_z)])  27.9 us
    pallas_call x1, Pallas kernels, attend(): pl.pallas_call(functools.partial(attend_kernel, plan, rows, width // HEAD...  10.9 us
    ppermute x7, starting transfers between devices, on_z(): return lax.ppermute(array, 'gy', [(s, s ^ flip) for s in range(along_z)])  10 us
    ppermute x8, waiting for transfers between devices, on_gx(): return lax.ppermute(array, 'gx', pairs)  6.78 us
    ppermute x8, starting transfers between devices, on_gx(): return lax.ppermute(array, 'gx', pairs)  5.32 us
  transfers between devices with their start and end apart: 15, of which 6 were waited for; matrix products, arithmetic and copies ran while one was open for 2% of the time, Pallas kernels for 37%

profile of v3, /device:TPU:0, one launch (start us, length us, event | category | flops | bytes accessed | tf_op | source)
XLA Modules:
  0.0 100.7 jit_solution(6070375520494607344)
XLA Ops:
  0.6 0.5 collective-permute-start
  1.1 2.6 %collective-permute-start.4 = (bf16[64,4096]{1,0:T(8,128)(2,1)}, bf16[64,4096]{1,0:T(8,128)(2,1)S(1)}, u32[]{:S(2)}, u32[]{:S(2)}) collective-permute-start(bf16[64,4096]{1,0:T(8,128)(2,1)} %a0_ref.3), channel_id=1, source_target_pairs={{8,0},{12,4},{0,8},{4,12},{9,1},{13,5},{1,9},{5,13},{10,2},{14,6},... | collective-permute-start | bytes 1572872 | tf_op jit(solution)/shard_map/ppermute | solution.py:254
  3.7 0.7 reshape.17.gain_ref
  4.4 0.0 collective-permute-done.a1_ref
  4.4 0.0 copy-start
  4.4 8.9 %project.5 = (f32[64,2304]{1,0:T(8,128)S(1)}, bf16[64,2304]{1,0:T(8,128)(2,1)S(1)}) custom-call(s32[1]{0:T(128)} %bitcast.4.z_ref, bf16[64,4096]{1,0:T(8,128)(2,1)} %a0_ref.3, bf16[64,4096]{1,0:T(8,128)(2,1)S(1)} %collective-permute-done.a1_ref, bf16[1,4096]{1,0:T(2,128)(2,1)S(1)} %reshape.17.gain_ref, bf16[4096,4608]{1,0:T(8,128)(2,1)} %w_hbm.7), custom_call_target="tpu_custom_call" | custom-call | tf_op jit(solution)/shard_map/project/pallas_call | solution.py:94
  13.4 1.6 %collective-permute-start.2 = (bf16[64,2304]{1,0:T(8,128)(2,1)S(1)}, bf16[64,2304]{1,0:T(8,128)(2,1)S(1)}, u32[]{:S(2)}, u32[]{:S(2)}) collective-permute-start(bf16[64,2304]{1,0:T(8,128)(2,1)S(1)} %get-tuple-element.17), channel_id=1, source_target_pairs={{0,1},{1,0},{2,3},{3,2},{4,5},{5,4},{6,7},{7,6},{8,9},{9,8},{10,11... | collective-permute-start | bytes 884744 | tf_op jit(solution)/shard_map/ppermute | solution.py:257
  15.0 0.0 copy-done
  15.1 8.9 %project.4 = (f32[64,2432]{1,0:T(8,128)S(1)}, bf16[64,2560]{1,0:T(8,128)(2,1)S(1)}) custom-call(s32[1]{0:T(128)} %bitcast.4.z_ref, bf16[64,4096]{1,0:T(8,128)(2,1)} %a0_ref.3, bf16[64,4096]{1,0:T(8,128)(2,1)S(1)} %collective-permute-done.a1_ref, bf16[1,4096]{1,0:T(2,128)(2,1)S(1)} %reshape.17.gain_ref, bf16[4096,4608]{1,0:T(8,128)(2,1)} %w_hbm.7), custom_call_target="tpu_custom_call" | custom-call | tf_op jit(solution)/shard_map/project/pallas_call | solution.py:94
  24.0 0.5 collective-permute-start.1
  24.5 0.0 collective-permute-done.4.a0_ref
  24.5 0.0 collective-permute-start.5
  24.5 0.0 collective-permute-done.2
  24.6 9.0 %collective-permute-done.1 = bf16[64,2560]{1,0:T(8,128)(2,1)S(1)} collective-permute-done((bf16[64,2560]{1,0:T(8,128)(2,1)S(1)}, bf16[64,2560]{1,0:T(8,128)(2,1)S(1)}, u32[]{:S(2)}, u32[]{:S(2)}) %collective-permute-start.1) | collective-permute-done | bytes 327712 | tf_op jit(solution)/shard_map/ppermute | solution.py:257
  33.6 2.7 %collective-permute-start.3 = (bf16[32,4864]{1,0:T(8,128)(2,1)S(1)}, bf16[32,4864]{1,0:T(8,128)(2,1)S(1)}, u32[]{:S(2)}, u32[]{:S(2)}) collective-permute-start(bf16[32,4864]{1,0:T(8,128)(2,1)S(1)} %pad_maximum_fusion), channel_id=1, source_target_pairs={{0,2},{1,3},{2,0},{3,1},{4,6},{5,7},{6,4},{7,5},{8,10},{9,11},{10,... | collective-permute-start | bytes 933896 | tf_op jit(solution)/shard_map/ppermute | solution.py:257
  36.3 0.0 collective-permute-done.5.a1_ref
  36.3 8.3 %project.7 = (f32[64,1792]{1,0:T(8,128)S(1)}, bf16[64,1792]{1,0:T(8,128)(2,1)S(1)}) custom-call(s32[1]{0:T(128)} %bitcast.4.z_ref, bf16[64,4096]{1,0:T(8,128)(2,1)S(1)} %collective-permute-done.4.a0_ref, bf16[64,4096]{1,0:T(8,128)(2,1)S(1)} %collective-permute-done.5.a1_ref, bf16[1,4096]{1,0:T(2,128)(2,1)S(1)} %reshape.17.gain_ref, bf16[4096,4608]{1,0:T(8,128)(2,1)} %w_hbm.7), custom_call_target="tpu_custom_call" | custom-call | tf_op jit(solution)/shard_map/project/pallas_call | solution.py:94
  44.6 0.5 collective-permute-start.11
  45.1 10.8 %project.6 = (f32[64,2944]{1,0:T(8,128)S(1)}, bf16[64,3072]{1,0:T(8,128)(2,1)S(1)}) custom-call(s32[1]{0:T(128)} %bitcast.4.z_ref, bf16[64,4096]{1,0:T(8,128)(2,1)S(1)} %collective-permute-done.4.a0_ref, bf16[64,4096]{1,0:T(8,128)(2,1)S(1)} %collective-permute-done.5.a1_ref, bf16[1,4096]{1,0:T(2,128)(2,1)S(1)} %reshape.17.gain_ref, bf16[4096,4608]{1,0:T(8,128)(2,1)} %w_hbm.7), custom_call_target="tpu_custom_call" | custom-call | tf_op jit(solution)/shard_map/project/pallas_call | solution.py:94
  55.9 1.6 %collective-permute-start.7 = (bf16[64,3072]{1,0:T(8,128)(2,1)S(1)}, bf16[64,3072]{1,0:T(8,128)(2,1)S(1)}, u32[]{:S(2)}, u32[]{:S(2)}) collective-permute-start(bf16[64,3072]{1,0:T(8,128)(2,1)S(1)} %get-tuple-element.23), channel_id=1, source_target_pairs={{0,1},{1,0},{2,3},{3,2},{4,5},{5,4},{6,7},{7,6},{8,9},{9,8},{10,11... | collective-permute-start | bytes 1179656 | tf_op jit(solution)/shard_map/ppermute | solution.py:257
  57.6 0.0 collective-permute-done.3
  57.6 0.1 fusion.15
  57.7 0.1 multiply_convert_fusion.2
  57.8 0.1 collective-permute-start.6
  57.9 7.5 %collective-permute-done.7 = bf16[64,3072]{1,0:T(8,128)(2,1)S(1)} collective-permute-done((bf16[64,3072]{1,0:T(8,128)(2,1)S(1)}, bf16[64,3072]{1,0:T(8,128)(2,1)S(1)}, u32[]{:S(2)}, u32[]{:S(2)}) %collective-permute-start.7) | collective-permute-done | bytes 393248 | tf_op jit(solution)/shard_map/ppermute | solution.py:257
  65.5 0.0 collective-permute-done.11
  65.5 0.4 collective-permute-start.12
  66.0 2.7 %collective-permute-start.8 = (bf16[32,3072]{1,0:T(8,128)(2,1)S(1)}, bf16[32,3072]{1,0:T(8,128)(2,1)S(1)}, u32[]{:S(2)}, u32[]{:S(2)}) collective-permute-start(bf16[32,3072]{1,0:T(8,128)(2,1)S(1)} %pad_maximum_fusion.2), channel_id=1, source_target_pairs={{0,2},{1,3},{2,0},{3,1},{4,6},{5,7},{6,4},{7,5},{8,10},{9,11},{10,... | collective-permute-start | bytes 589832 | tf_op jit(solution)/shard_map/ppermute | solution.py:257
  68.6 11.3 %collective-permute-done.8 = bf16[32,3072]{1,0:T(8,128)(2,1)S(1)} collective-permute-done((bf16[32,3072]{1,0:T(8,128)(2,1)S(1)}, bf16[32,3072]{1,0:T(8,128)(2,1)S(1)}, u32[]{:S(2)}, u32[]{:S(2)}) %collective-permute-start.8) | collective-permute-done | bytes 196640 | tf_op jit(solution)/shard_map/ppermute | solution.py:257
  80.0 0.1 fusion.8
  80.1 0.0 collective-permute-done.12
  80.1 0.1 multiply_convert_fusion.3
  80.2 1.2 %collective-permute-start.13 = (bf16[32,1792]{1,0:T(8,128)(2,1)S(1)}, bf16[32,1792]{1,0:T(8,128)(2,1)S(1)}, u32[]{:S(2)}, u32[]{:S(2)}) collective-permute-start(bf16[32,1792]{1,0:T(8,128)(2,1)S(1)} %multiply_convert_fusion.3), channel_id=1, source_target_pairs={{8,0},{12,4},{0,8},{4,12},{9,1},{13,5},{1,9},{5,13},{10,2},{14,6},... | collective-permute-start | bytes 344072 | tf_op jit(solution)/shard_map/ppermute | solution.py:254
  81.4 0.1 multiply_convert_fusion
  81.5 0.9 collective-permute-start.9
  82.5 0.1 fusion.16
  82.6 3.6 %collective-permute-done.13.refs_8_ = bf16[32,1792]{1,0:T(8,128)(2,1)S(1)} collective-permute-done((bf16[32,1792]{1,0:T(8,128)(2,1)S(1)}, bf16[32,1792]{1,0:T(8,128)(2,1)S(1)}, u32[]{:S(2)}, u32[]{:S(2)}) %collective-permute-start.13) | collective-permute-done | bytes 114720 | tf_op jit(solution)/shard_map/ppermute | solution.py:254
  86.2 0.0 collective-permute-start.14
  86.2 1.9 %collective-permute-done.9.refs_6_ = bf16[32,2816]{1,0:T(8,128)(2,1)S(1)} collective-permute-done((bf16[32,2816]{1,0:T(8,128)(2,1)S(1)}, bf16[32,2816]{1,0:T(8,128)(2,1)S(1)}, u32[]{:S(2)}, u32[]{:S(2)}) %collective-permute-start.9) | collective-permute-done | bytes 180256 | tf_op jit(solution)/shard_map/ppermute | solution.py:254
  88.1 0.0 collective-permute-start.10
  88.2 0.1 pad_add_fusion.refs_0_
  88.2 0.1 pad_maximum_fusion.3
  88.3 0.0 collective-permute-done.6.refs_5_
  88.3 0.0 collective-permute-done.14.refs_9_
  88.3 1.3 %collective-permute-done.10.refs_7_ = bf16[32,2816]{1,0:T(8,128)(2,1)S(1)} collective-permute-done((bf16[32,2816]{1,0:T(8,128)(2,1)S(1)}, bf16[32,2816]{1,0:T(8,128)(2,1)S(1)}, u32[]{:S(2)}, u32[]{:S(2)}) %collective-permute-start.10) | collective-permute-done | bytes 180256 | tf_op jit(solution)/shard_map/ppermute | solution.py:254
  89.6 10.9 %attend.1 = (bf16[16,16384]{1,0:T(8,128)(2,1)}, bf16[16,2048]{1,0:T(8,128)(2,1)}) custom-call(s32[4]{0:T(128)S(1)} %pad_add_fusion.refs_0_, s32[16]{0:T(128)S(1)} %copy-done, f32[16,128]{1,0:T(8,128)S(1)} %get-tuple-element.45.refs_2_, f32[16,128]{1,0:T(8,128)S(1)} %get-tuple-element.46.refs_3_, bf16[32,4608]{1,0:T(8,128)(2,1)S(1)} %pad_maximum_fusion.1.refs_4_, ...), custom_call_target="tpu_custom_call" | custom-call | tf_op jit(solution)/shard_map/attend/pallas_call | solution.py:205
  (15 shorter events, 0.2 us)
Async XLA Ops:
  0.6 3.8 %collective-permute-start = (bf16[64,4096]{1,0:T(8,128)(2,1)}, bf16[64,4096]{1,0:T(8,128)(2,1)S(1)}, u32[]{:S(2)}, u32[]{:S(2)}) collective-permute-start(bf16[64,4096]{1,0:T(8,128)(2,1)} %a0_ref.3), channel_id=1, source_target_pairs={{4,0},{0,4},{12,8},{8,12},{5,1},{1,5},{13,9},{9,13},{6,2},{2,6},{1... | collective-permute-start | bytes 1572872 | tf_op jit(solution)/shard_map/ppermute | solution.py:254
  1.1 23.4 %collective-permute-start.4 = (bf16[64,4096]{1,0:T(8,128)(2,1)}, bf16[64,4096]{1,0:T(8,128)(2,1)S(1)}, u32[]{:S(2)}, u32[]{:S(2)}) collective-permute-start(bf16[64,4096]{1,0:T(8,128)(2,1)} %a0_ref.3), channel_id=1, source_target_pairs={{8,0},{12,4},{0,8},{4,12},{9,1},{13,5},{1,9},{5,13},{10,2},{14,6},... | collective-permute-start | bytes 1572872 | tf_op jit(solution)/shard_map/ppermute | solution.py:254
  4.4 10.6 %copy-start = (s32[16]{0:T(128)S(1)}, s32[16]{0:T(128)}, u32[]{:S(2)}) copy-start(s32[16]{0:T(128)} %refs_1_.1) | copy-start | bytes 196
  13.4 11.1 %collective-permute-start.2 = (bf16[64,2304]{1,0:T(8,128)(2,1)S(1)}, bf16[64,2304]{1,0:T(8,128)(2,1)S(1)}, u32[]{:S(2)}, u32[]{:S(2)}) collective-permute-start(bf16[64,2304]{1,0:T(8,128)(2,1)S(1)} %get-tuple-element.17), channel_id=1, source_target_pairs={{0,1},{1,0},{2,3},{3,2},{4,5},{5,4},{6,7},{7,6},{8,9},{9,8},{10,11... | collective-permute-start | bytes 884744 | tf_op jit(solution)/shard_map/ppermute | solution.py:257
  24.0 9.6 %collective-permute-start.1 = (bf16[64,2560]{1,0:T(8,128)(2,1)S(1)}, bf16[64,2560]{1,0:T(8,128)(2,1)S(1)}, u32[]{:S(2)}, u32[]{:S(2)}) collective-permute-start(bf16[64,2560]{1,0:T(8,128)(2,1)S(1)} %get-tuple-element.15), channel_id=1, source_target_pairs={{0,1},{1,0},{2,3},{3,2},{4,5},{5,4},{6,7},{7,6},{8,9},{9,8},{10,11... | collective-permute-start | bytes 983048 | tf_op jit(solution)/shard_map/ppermute | solution.py:257
  24.5 11.8 %collective-permute-start.5 = (bf16[64,4096]{1,0:T(8,128)(2,1)S(1)}, bf16[64,4096]{1,0:T(8,128)(2,1)S(1)}, u32[]{:S(2)}, u32[]{:S(2)}) collective-permute-start(bf16[64,4096]{1,0:T(8,128)(2,1)S(1)} %collective-permute-done.4.a0_ref), channel_id=1, source_target_pairs={{4,0},{0,4},{12,8},{8,12},{5,1},{1,5},{13,9},{9,13},{6,2},{2,6},{1... | collective-permute-start | bytes 1572872 | tf_op jit(solution)/shard_map/ppermute | solution.py:254
  33.6 23.9 %collective-permute-start.3 = (bf16[32,4864]{1,0:T(8,128)(2,1)S(1)}, bf16[32,4864]{1,0:T(8,128)(2,1)S(1)}, u32[]{:S(2)}, u32[]{:S(2)}) collective-permute-start(bf16[32,4864]{1,0:T(8,128)(2,1)S(1)} %pad_maximum_fusion), channel_id=1, source_target_pairs={{0,2},{1,3},{2,0},{3,1},{4,6},{5,7},{6,4},{7,5},{8,10},{9,11},{10,... | collective-permute-start | bytes 933896 | tf_op jit(solution)/shard_map/ppermute | solution.py:257
  44.6 20.9 %collective-permute-start.11 = (bf16[64,1792]{1,0:T(8,128)(2,1)S(1)}, bf16[64,1792]{1,0:T(8,128)(2,1)S(1)}, u32[]{:S(2)}, u32[]{:S(2)}) collective-permute-start(bf16[64,1792]{1,0:T(8,128)(2,1)S(1)} %get-tuple-element.24), channel_id=1, source_target_pairs={{0,1},{1,0},{2,3},{3,2},{4,5},{5,4},{6,7},{7,6},{8,9},{9,8},{10,11... | collective-permute-start | bytes 688136 | tf_op jit(solution)/shard_map/ppermute | solution.py:257
  55.9 9.5 %collective-permute-start.7 = (bf16[64,3072]{1,0:T(8,128)(2,1)S(1)}, bf16[64,3072]{1,0:T(8,128)(2,1)S(1)}, u32[]{:S(2)}, u32[]{:S(2)}) collective-permute-start(bf16[64,3072]{1,0:T(8,128)(2,1)S(1)} %get-tuple-element.23), channel_id=1, source_target_pairs={{0,1},{1,0},{2,3},{3,2},{4,5},{5,4},{6,7},{7,6},{8,9},{9,8},{10,11... | collective-permute-start | bytes 1179656 | tf_op jit(solution)/shard_map/ppermute | solution.py:257
  57.8 30.5 %collective-permute-start.6 = (bf16[32,4608]{1,0:T(8,128)(2,1)S(1)}, bf16[32,4608]{1,0:T(8,128)(2,1)S(1)}, u32[]{:S(2)}, u32[]{:S(2)}) collective-permute-start(bf16[32,4608]{1,0:T(8,128)(2,1)S(1)} %pad_maximum_fusion.1.refs_4_), channel_id=1, source_target_pairs={{4,0},{0,4},{12,8},{8,12},{5,1},{1,5},{13,9},{9,13},{6,2},{2,6},{1... | collective-permute-start | bytes 884744 | tf_op jit(solution)/shard_map/ppermute | solution.py:254
  65.5 14.6 %collective-permute-start.12 = (bf16[32,1792]{1,0:T(8,128)(2,1)S(1)}, bf16[32,1792]{1,0:T(8,128)(2,1)S(1)}, u32[]{:S(2)}, u32[]{:S(2)}) collective-permute-start(bf16[32,1792]{1,0:T(8,128)(2,1)S(1)} %add_convert_fusion.3), channel_id=1, source_target_pairs={{0,2},{1,3},{2,0},{3,1},{4,6},{5,7},{6,4},{7,5},{8,10},{9,11},{10,... | collective-permute-start | bytes 344072 | tf_op jit(solution)/shard_map/ppermute | solution.py:257
  66.0 14.0 %collective-permute-start.8 = (bf16[32,3072]{1,0:T(8,128)(2,1)S(1)}, bf16[32,3072]{1,0:T(8,128)(2,1)S(1)}, u32[]{:S(2)}, u32[]{:S(2)}) collective-permute-start(bf16[32,3072]{1,0:T(8,128)(2,1)S(1)} %pad_maximum_fusion.2), channel_id=1, source_target_pairs={{0,2},{1,3},{2,0},{3,1},{4,6},{5,7},{6,4},{7,5},{8,10},{9,11},{10,... | collective-permute-start | bytes 589832 | tf_op jit(solution)/shard_map/ppermute | solution.py:257
  80.2 6.0 %collective-permute-start.13 = (bf16[32,1792]{1,0:T(8,128)(2,1)S(1)}, bf16[32,1792]{1,0:T(8,128)(2,1)S(1)}, u32[]{:S(2)}, u32[]{:S(2)}) collective-permute-start(bf16[32,1792]{1,0:T(8,128)(2,1)S(1)} %multiply_convert_fusion.3), channel_id=1, source_target_pairs={{8,0},{12,4},{0,8},{4,12},{9,1},{13,5},{1,9},{5,13},{10,2},{14,6},... | collective-permute-start | bytes 344072 | tf_op jit(solution)/shard_map/ppermute | solution.py:254
  81.5 6.6 %collective-permute-start.9 = (bf16[32,2816]{1,0:T(8,128)(2,1)S(1)}, bf16[32,2816]{1,0:T(8,128)(2,1)S(1)}, u32[]{:S(2)}, u32[]{:S(2)}) collective-permute-start(bf16[32,2816]{1,0:T(8,128)(2,1)S(1)} %multiply_convert_fusion), channel_id=1, source_target_pairs={{8,0},{12,4},{0,8},{4,12},{9,1},{13,5},{1,9},{5,13},{10,2},{14,6},... | collective-permute-start | bytes 540680 | tf_op jit(solution)/shard_map/ppermute | solution.py:254
  86.2 2.1 %collective-permute-start.14 = (bf16[32,1792]{1,0:T(8,128)(2,1)S(1)}, bf16[32,1792]{1,0:T(8,128)(2,1)S(1)}, u32[]{:S(2)}, u32[]{:S(2)}) collective-permute-start(bf16[32,1792]{1,0:T(8,128)(2,1)S(1)} %collective-permute-done.13.refs_8_), channel_id=1, source_target_pairs={{4,0},{0,4},{12,8},{8,12},{5,1},{1,5},{13,9},{9,13},{6,2},{2,6},{1... | collective-permute-start | bytes 344072 | tf_op jit(solution)/shard_map/ppermute | solution.py:254
  88.1 1.4 %collective-permute-start.10 = (bf16[32,2816]{1,0:T(8,128)(2,1)S(1)}, bf16[32,2816]{1,0:T(8,128)(2,1)S(1)}, u32[]{:S(2)}, u32[]{:S(2)}) collective-permute-start(bf16[32,2816]{1,0:T(8,128)(2,1)S(1)} %collective-permute-done.9.refs_6_), channel_id=1, source_target_pairs={{4,0},{0,4},{12,8},{8,12},{5,1},{1,5},{13,9},{9,13},{6,2},{2,6},{1... | collective-permute-start | bytes 540680 | tf_op jit(solution)/shard_map/ppermute | solution.py:254

commit v4 on v3

--- a/solution.py
+++ b/solution.py
@@ -14,7 +14,7 @@
 HEAD_DIM = 128
 GROUP = HEADS // KV_HEADS
 CORES = 2
-IN_FLIGHT = 2
+IN_FLIGHT = 3
 
 norm_eps = 1e-05
 rope_base = 500000.0
@@ -75,11 +75,9 @@
 
 
 def tiles_of(width):
-    sizes = []
-    while width:
-        size = min(512, width) if width >= 1024 or width % 256 else 256
-        sizes.append(size)
-        width -= size
+    sizes = [256] if width % 256 == 0 else []
+    while width > sum(sizes):
+        sizes.append(min(512, width - sum(sizes)))
     return tuple((sum(sizes[:i]), size) for i, size in enumerate(sizes))
 
 
@@ -310,37 +308,45 @@
         return owns, [jnp.concatenate(away[:3], axis=1), *away[3:]]
 
     owns = {}
+    arrived = {}
     for k in kinds:
         if k:
             a0 = after(there[k - 1], keeps[k - 1])
             a1 = on_gx(a0, 0, 1)
+            if len(chunks[0]) > 1:
+                a0 = after(a0, receiveds[k - 1][0])
         else:
             a0, a1 = here[0]
         first = 0
         for c, chunk in enumerate(chunks[k]):
-            if k and c == 1:
-                a0 = after(a0, aways[k - 1])
+            if k == 0 and c:
+                a0 = after(a0, keeps[0][0])
             keep, send = project(z, a0, a1, gain, weight, rows, first, chunk, c == 0)
             first += chunk
             keeps[k].append(keep)
             receiveds[k].append(on_z(send, 1))
-        owns[k], aways[k] = add_pairs(k)
+            if k and c == 0:
+                receiveds[k - 1][-1] = after(receiveds[k - 1][-1], keep)
+                owns[k - 1], aways[k - 1] = add_pairs(k - 1)
+                a0 = after(a0, aways[k - 1])
+    owns[chips - 1], aways[chips - 1] = add_pairs(chips - 1)
     for k in kinds:
-        arrived = [
+        arrived[k] = [
             [on_z(away[(i - 1) * first_rows : i * first_rows], 2 * i) for i in range(1, kept)]
             for away in aways[k]
         ]
         if k + 1 < chips:
-            arrived = after(arrived, keeps[k + 1])
+            arrived[k] = after(arrived[k], keeps[k + 1][-1])
+    for k in kinds:
         square = owns[k][0]
-        for other in arrived[0]:
+        for other in arrived[k][0]:
             square = square + other[:, :HEAD_DIM].astype(f32) + other[:, HEAD_DIM : 2 * HEAD_DIM].astype(f32)
         scale = lax.rsqrt(square[:, :1] * (1.0 / D) + norm_eps)
         done = []
         first = 0
         for c, chunk in enumerate(chunks[k]):
             total = owns[k][c + 1]
-            for other in arrived[0] if k == 0 else arrived[c]:
+            for other in arrived[k][0 if k == 0 else c]:
                 skip = 2 * HEAD_DIM + first if k == 0 else (2 * HEAD_DIM if c == 0 else 0)
                 total = total + other[:, skip : skip + chunk].astype(f32)
             done.append((total * scale).astype(bf16))

time: 101 us -> 90.2 us (0.89)
  waiting for transfers between devices: 34.7 us -> 27.8 us
  Pallas kernels: 47.9 us -> 45.4 us
  starting transfers between devices: 15.3 us -> 14 us
    ppermute x7, waiting for transfers between devices: 27.9 us -> 20.9 us  [on_z(): return lax.ppermute(array, 'gy', [(s, s ^ flip) for s in range(along_z)])]
    pallas_call x4, Pallas kernels: 36.9 us -> 34.4 us  [project(): pl.pallas_call(functools.partial(project_kernel, rows, kept, first, tiles...]
    ppermute x7, starting transfers between devices: 10 us -> 7.73 us  [on_z(): return lax.ppermute(array, 'gy', [(s, s ^ flip) for s in range(along_z)])]
  transfers between devices with their start and end apart: 15 -> 15, of which waited for: 6 -> 8; matrix products, arithmetic and copies ran while one was open for 2% -> 2% of each run, Pallas kernels for 37% -> 38%
where the time goes in v4:
time: 90.2 us; the launch traced here: 90 us
  Pallas kernels  45.4 us (50%)
  waiting for transfers between devices  27.8 us (31%)
  starting transfers between devices  14 us (16%)
  other arithmetic  1.02 us (1%)
  between operations  1.02 us (1%)
    pallas_call x4, Pallas kernels, project(): pl.pallas_call(functools.partial(project_kernel, rows, kept, first, tiles...  34.4 us
    ppermute x7, waiting for transfers between devices, on_z(): return lax.ppermute(array, 'gy', [(s, s ^ flip) for s in range(along_z)])  20.9 us
    pallas_call x1, Pallas kernels, attend(): pl.pallas_call(functools.partial(attend_kernel, plan, rows, width // HEAD...  10.9 us
    ppermute x7, starting transfers between devices, on_z(): return lax.ppermute(array, 'gy', [(s, s ^ flip) for s in range(along_z)])  7.73 us
    ppermute x8, waiting for transfers between devices, on_gx(): return lax.ppermute(array, 'gx', pairs)  6.92 us
    ppermute x8, starting transfers between devices, on_gx(): return lax.ppermute(array, 'gx', pairs)  6.31 us
  transfers between devices with their start and end apart: 15, of which 8 were waited for; matrix products, arithmetic and copies ran while one was open for 2% of the time, Pallas kernels for 38%

profile of v4, /device:TPU:0, one launch (start us, length us, event | category | flops | bytes accessed | tf_op | source)
XLA Modules:
  0.0 90.0 jit_solution(13723627261431338148)
XLA Ops:
  0.6 0.5 collective-permute-start
  1.1 2.6 %collective-permute-start.3 = (bf16[64,4096]{1,0:T(8,128)(2,1)}, bf16[64,4096]{1,0:T(8,128)(2,1)S(1)}, u32[]{:S(2)}, u32[]{:S(2)}) collective-permute-start(bf16[64,4096]{1,0:T(8,128)(2,1)} %a0_ref.2), channel_id=1, source_target_pairs={{8,0},{12,4},{0,8},{4,12},{9,1},{13,5},{1,9},{5,13},{10,2},{14,6},... | collective-permute-start | bytes 1572872 | tf_op jit(solution)/shard_map/ppermute | solution.py:252
  3.7 0.7 reshape.17.gain_ref
  4.4 0.0 collective-permute-done.a1_ref
  4.4 8.3 %project.4 = (f32[64,2432]{1,0:T(8,128)S(1)}, bf16[64,2560]{1,0:T(8,128)(2,1)S(1)}) custom-call(s32[1]{0:T(128)} %bitcast.4.z_ref, bf16[64,4096]{1,0:T(8,128)(2,1)} %a0_ref.2, bf16[64,4096]{1,0:T(8,128)(2,1)S(1)} %collective-permute-done.a1_ref, bf16[1,4096]{1,0:T(2,128)(2,1)S(1)} %reshape.17.gain_ref, bf16[4096,4608]{1,0:T(8,128)(2,1)} %w_hbm.7), custom_call_target="tpu_custom_call" | custom-call | tf_op jit(solution)/shard_map/project/pallas_call | solution.py:92
  12.7 1.6 %collective-permute-start.1 = (bf16[64,2560]{1,0:T(8,128)(2,1)S(1)}, bf16[64,2560]{1,0:T(8,128)(2,1)S(1)}, u32[]{:S(2)}, u32[]{:S(2)}) collective-permute-start(bf16[64,2560]{1,0:T(8,128)(2,1)S(1)} %get-tuple-element.18), channel_id=1, source_target_pairs={{0,1},{1,0},{2,3},{3,2},{4,5},{5,4},{6,7},{7,6},{8,9},{9,8},{10,11... | collective-permute-start | bytes 983048 | tf_op jit(solution)/shard_map/ppermute | solution.py:255
  14.4 0.0 copy-start
  14.4 8.3 %project.5 = (f32[64,2304]{1,0:T(8,128)S(1)}, bf16[64,2304]{1,0:T(8,128)(2,1)S(1)}) custom-call(s32[1]{0:T(128)} %bitcast.4.z_ref, bf16[64,4096]{1,0:T(8,128)(2,1)} %a0_ref.2, bf16[64,4096]{1,0:T(8,128)(2,1)S(1)} %collective-permute-done.a1_ref, bf16[1,4096]{1,0:T(2,128)(2,1)S(1)} %reshape.17.gain_ref, bf16[4096,4608]{1,0:T(8,128)(2,1)} %w_hbm.7), custom_call_target="tpu_custom_call" | custom-call | tf_op jit(solution)/shard_map/project/pallas_call | solution.py:92
  22.7 0.0 collective-permute-done.3.a0_ref
  22.7 0.1 collective-permute-start.4
  22.8 0.5 collective-permute-start.2
  23.3 0.0 copy-done
  23.3 0.0 collective-permute-done.1
  23.3 1.3 %collective-permute-done.4.a1_ref = bf16[64,4096]{1,0:T(8,128)(2,1)S(1)} collective-permute-done((bf16[64,4096]{1,0:T(8,128)(2,1)S(1)}, bf16[64,4096]{1,0:T(8,128)(2,1)S(1)}, u32[]{:S(2)}, u32[]{:S(2)}) %collective-permute-start.4) | collective-permute-done | bytes 524320 | tf_op jit(solution)/shard_map/ppermute | solution.py:252
  24.7 10.1 %project.6 = (f32[64,2944]{1,0:T(8,128)S(1)}, bf16[64,3072]{1,0:T(8,128)(2,1)S(1)}) custom-call(s32[1]{0:T(128)} %bitcast.4.z_ref, bf16[64,4096]{1,0:T(8,128)(2,1)S(1)} %collective-permute-done.3.a0_ref, bf16[64,4096]{1,0:T(8,128)(2,1)S(1)} %collective-permute-done.4.a1_ref, bf16[1,4096]{1,0:T(2,128)(2,1)S(1)} %reshape.17.gain_ref, bf16[4096,4608]{1,0:T(8,128)(2,1)} %w_hbm.7), custom_call_target="tpu_custom_call" | custom-call | tf_op jit(solution)/shard_map/project/pallas_call | solution.py:92
  34.8 0.0 collective-permute-done.2
  34.8 0.1 add_convert_fusion.1
  34.9 2.6 %collective-permute-start.5 = (bf16[32,4864]{1,0:T(8,128)(2,1)S(1)}, bf16[32,4864]{1,0:T(8,128)(2,1)S(1)}, u32[]{:S(2)}, u32[]{:S(2)}) collective-permute-start(bf16[32,4864]{1,0:T(8,128)(2,1)S(1)} %pad_maximum_fusion), channel_id=1, source_target_pairs={{0,2},{1,3},{2,0},{3,1},{4,6},{5,7},{6,4},{7,5},{8,10},{9,11},{10,... | collective-permute-start | bytes 933896 | tf_op jit(solution)/shard_map/ppermute | solution.py:255
  37.6 0.5 collective-permute-start.7
  38.1 7.7 %project.7 = (f32[64,1792]{1,0:T(8,128)S(1)}, bf16[64,1792]{1,0:T(8,128)(2,1)S(1)}) custom-call(s32[1]{0:T(128)} %bitcast.4.z_ref, bf16[64,4096]{1,0:T(8,128)(2,1)S(1)} %collective-permute-done.3.a0_ref, bf16[64,4096]{1,0:T(8,128)(2,1)S(1)} %collective-permute-done.4.a1_ref, bf16[1,4096]{1,0:T(2,128)(2,1)S(1)} %reshape.17.gain_ref, bf16[4096,4608]{1,0:T(8,128)(2,1)} %w_hbm.7), custom_call_target="tpu_custom_call" | custom-call | tf_op jit(solution)/shard_map/project/pallas_call | solution.py:92
  45.8 1.6 %collective-permute-start.11 = (bf16[64,1792]{1,0:T(8,128)(2,1)S(1)}, bf16[64,1792]{1,0:T(8,128)(2,1)S(1)}, u32[]{:S(2)}, u32[]{:S(2)}) collective-permute-start(bf16[64,1792]{1,0:T(8,128)(2,1)S(1)} %get-tuple-element.30), channel_id=1, source_target_pairs={{0,1},{1,0},{2,3},{3,2},{4,5},{5,4},{6,7},{7,6},{8,9},{9,8},{10,11... | collective-permute-start | bytes 688136 | tf_op jit(solution)/shard_map/ppermute | solution.py:255
  47.4 4.5 %collective-permute-done.5 = bf16[32,4864]{1,0:T(8,128)(2,1)S(1)} collective-permute-done((bf16[32,4864]{1,0:T(8,128)(2,1)S(1)}, bf16[32,4864]{1,0:T(8,128)(2,1)S(1)}, u32[]{:S(2)}, u32[]{:S(2)}) %collective-permute-start.5) | collective-permute-done | bytes 311328 | tf_op jit(solution)/shard_map/ppermute | solution.py:255
  51.9 0.1 fusion.15
  52.0 0.1 multiply_convert_fusion.2
  52.2 0.1 collective-permute-start.6
  52.3 3.9 %collective-permute-done.7 = bf16[64,3072]{1,0:T(8,128)(2,1)S(1)} collective-permute-done((bf16[64,3072]{1,0:T(8,128)(2,1)S(1)}, bf16[64,3072]{1,0:T(8,128)(2,1)S(1)}, u32[]{:S(2)}, u32[]{:S(2)}) %collective-permute-start.7) | collective-permute-done | bytes 393248 | tf_op jit(solution)/shard_map/ppermute | solution.py:255
  56.3 0.1 collective-permute-start.8
  56.4 4.6 %collective-permute-done.11 = bf16[64,1792]{1,0:T(8,128)(2,1)S(1)} collective-permute-done((bf16[64,1792]{1,0:T(8,128)(2,1)S(1)}, bf16[64,1792]{1,0:T(8,128)(2,1)S(1)}, u32[]{:S(2)}, u32[]{:S(2)}) %collective-permute-start.11) | collective-permute-done | bytes 229408 | tf_op jit(solution)/shard_map/ppermute | solution.py:255
  61.0 0.7 collective-permute-start.12
  61.7 7.9 %collective-permute-done.8 = bf16[32,3072]{1,0:T(8,128)(2,1)S(1)} collective-permute-done((bf16[32,3072]{1,0:T(8,128)(2,1)S(1)}, bf16[32,3072]{1,0:T(8,128)(2,1)S(1)}, u32[]{:S(2)}, u32[]{:S(2)}) %collective-permute-start.8) | collective-permute-done | bytes 196640 | tf_op jit(solution)/shard_map/ppermute | solution.py:255
  69.6 0.1 fusion.8
  69.7 0.1 multiply_convert_fusion
  69.8 1.3 %collective-permute-start.9 = (bf16[32,2816]{1,0:T(8,128)(2,1)S(1)}, bf16[32,2816]{1,0:T(8,128)(2,1)S(1)}, u32[]{:S(2)}, u32[]{:S(2)}) collective-permute-start(bf16[32,2816]{1,0:T(8,128)(2,1)S(1)} %multiply_convert_fusion), channel_id=1, source_target_pairs={{8,0},{12,4},{0,8},{4,12},{9,1},{13,5},{1,9},{5,13},{10,2},{14,6},... | collective-permute-start | bytes 540680 | tf_op jit(solution)/shard_map/ppermute | solution.py:252
  71.2 0.0 collective-permute-done.12
  71.2 0.1 multiply_convert_fusion.3
  71.2 1.2 %collective-permute-start.13 = (bf16[32,1792]{1,0:T(8,128)(2,1)S(1)}, bf16[32,1792]{1,0:T(8,128)(2,1)S(1)}, u32[]{:S(2)}, u32[]{:S(2)}) collective-permute-start(bf16[32,1792]{1,0:T(8,128)(2,1)S(1)} %multiply_convert_fusion.3), channel_id=1, source_target_pairs={{8,0},{12,4},{0,8},{4,12},{9,1},{13,5},{1,9},{5,13},{10,2},{14,6},... | collective-permute-start | bytes 344072 | tf_op jit(solution)/shard_map/ppermute | solution.py:252
  72.5 0.1 fusion.16
  72.6 4.6 %collective-permute-done.13.refs_8_ = bf16[32,1792]{1,0:T(8,128)(2,1)S(1)} collective-permute-done((bf16[32,1792]{1,0:T(8,128)(2,1)S(1)}, bf16[32,1792]{1,0:T(8,128)(2,1)S(1)}, u32[]{:S(2)}, u32[]{:S(2)}) %collective-permute-start.13) | collective-permute-done | bytes 114720 | tf_op jit(solution)/shard_map/ppermute | solution.py:252
  77.3 0.0 collective-permute-start.14
  77.3 0.0 collective-permute-done.9.refs_6_
  77.3 0.5 collective-permute-start.10
  77.8 0.1 pad_add_fusion.refs_0_
  77.9 0.1 pad_maximum_fusion.3
  78.0 0.0 collective-permute-done.6.refs_5_
  78.0 0.7 collective-permute-done.14.refs_9_
  78.6 0.3 collective-permute-done.10.refs_7_
  78.9 10.9 %attend.1 = (bf16[16,16384]{1,0:T(8,128)(2,1)}, bf16[16,2048]{1,0:T(8,128)(2,1)}) custom-call(s32[4]{0:T(128)S(1)} %pad_add_fusion.refs_0_, s32[16]{0:T(128)S(1)} %copy-done, f32[16,128]{1,0:T(8,128)S(1)} %get-tuple-element.53.refs_2_, f32[16,128]{1,0:T(8,128)S(1)} %get-tuple-element.54.refs_3_, bf16[32,4608]{1,0:T(8,128)(2,1)S(1)} %pad_maximum_fusion.1.refs_4_, ...), custom_call_target="tpu_custom_call" | custom-call | tf_op jit(solution)/shard_map/attend/pallas_call | solution.py:203
  (13 shorter events, 0.2 us)
Async XLA Ops:
  0.6 3.8 %collective-permute-start = (bf16[64,4096]{1,0:T(8,128)(2,1)}, bf16[64,4096]{1,0:T(8,128)(2,1)S(1)}, u32[]{:S(2)}, u32[]{:S(2)}) collective-permute-start(bf16[64,4096]{1,0:T(8,128)(2,1)} %a0_ref.2), channel_id=1, source_target_pairs={{4,0},{0,4},{12,8},{8,12},{5,1},{1,5},{13,9},{9,13},{6,2},{2,6},{1... | collective-permute-start | bytes 1572872 | tf_op jit(solution)/shard_map/ppermute | solution.py:252
  1.1 21.5 %collective-permute-start.3 = (bf16[64,4096]{1,0:T(8,128)(2,1)}, bf16[64,4096]{1,0:T(8,128)(2,1)S(1)}, u32[]{:S(2)}, u32[]{:S(2)}) collective-permute-start(bf16[64,4096]{1,0:T(8,128)(2,1)} %a0_ref.2), channel_id=1, source_target_pairs={{8,0},{12,4},{0,8},{4,12},{9,1},{13,5},{1,9},{5,13},{10,2},{14,6},... | collective-permute-start | bytes 1572872 | tf_op jit(solution)/shard_map/ppermute | solution.py:252
  12.7 10.5 %collective-permute-start.1 = (bf16[64,2560]{1,0:T(8,128)(2,1)S(1)}, bf16[64,2560]{1,0:T(8,128)(2,1)S(1)}, u32[]{:S(2)}, u32[]{:S(2)}) collective-permute-start(bf16[64,2560]{1,0:T(8,128)(2,1)S(1)} %get-tuple-element.18), channel_id=1, source_target_pairs={{0,1},{1,0},{2,3},{3,2},{4,5},{5,4},{6,7},{7,6},{8,9},{9,8},{10,11... | collective-permute-start | bytes 983048 | tf_op jit(solution)/shard_map/ppermute | solution.py:255
  14.4 8.9 %copy-start = (s32[16]{0:T(128)S(1)}, s32[16]{0:T(128)}, u32[]{:S(2)}) copy-start(s32[16]{0:T(128)} %refs_1_.1) | copy-start | bytes 196
  22.7 2.0 %collective-permute-start.4 = (bf16[64,4096]{1,0:T(8,128)(2,1)S(1)}, bf16[64,4096]{1,0:T(8,128)(2,1)S(1)}, u32[]{:S(2)}, u32[]{:S(2)}) collective-permute-start(bf16[64,4096]{1,0:T(8,128)(2,1)S(1)} %collective-permute-done.3.a0_ref), channel_id=1, source_target_pairs={{4,0},{0,4},{12,8},{8,12},{5,1},{1,5},{13,9},{9,13},{6,2},{2,6},{1... | collective-permute-start | bytes 1572872 | tf_op jit(solution)/shard_map/ppermute | solution.py:252
  22.8 12.0 %collective-permute-start.2 = (bf16[64,2304]{1,0:T(8,128)(2,1)S(1)}, bf16[64,2304]{1,0:T(8,128)(2,1)S(1)}, u32[]{:S(2)}, u32[]{:S(2)}) collective-permute-start(bf16[64,2304]{1,0:T(8,128)(2,1)S(1)} %get-tuple-element.21), channel_id=1, source_target_pairs={{0,1},{1,0},{2,3},{3,2},{4,5},{5,4},{6,7},{7,6},{8,9},{9,8},{10,11... | collective-permute-start | bytes 884744 | tf_op jit(solution)/shard_map/ppermute | solution.py:255
  34.9 17.0 %collective-permute-start.5 = (bf16[32,4864]{1,0:T(8,128)(2,1)S(1)}, bf16[32,4864]{1,0:T(8,128)(2,1)S(1)}, u32[]{:S(2)}, u32[]{:S(2)}) collective-permute-start(bf16[32,4864]{1,0:T(8,128)(2,1)S(1)} %pad_maximum_fusion), channel_id=1, source_target_pairs={{0,2},{1,3},{2,0},{3,1},{4,6},{5,7},{6,4},{7,5},{8,10},{9,11},{10,... | collective-permute-start | bytes 933896 | tf_op jit(solution)/shard_map/ppermute | solution.py:255
  37.6 18.6 %collective-permute-start.7 = (bf16[64,3072]{1,0:T(8,128)(2,1)S(1)}, bf16[64,3072]{1,0:T(8,128)(2,1)S(1)}, u32[]{:S(2)}, u32[]{:S(2)}) collective-permute-start(bf16[64,3072]{1,0:T(8,128)(2,1)S(1)} %get-tuple-element.29), channel_id=1, source_target_pairs={{0,1},{1,0},{2,3},{3,2},{4,5},{5,4},{6,7},{7,6},{8,9},{9,8},{10,11... | collective-permute-start | bytes 1179656 | tf_op jit(solution)/shard_map/ppermute | solution.py:255
  45.8 15.1 %collective-permute-start.11 = (bf16[64,1792]{1,0:T(8,128)(2,1)S(1)}, bf16[64,1792]{1,0:T(8,128)(2,1)S(1)}, u32[]{:S(2)}, u32[]{:S(2)}) collective-permute-start(bf16[64,1792]{1,0:T(8,128)(2,1)S(1)} %get-tuple-element.30), channel_id=1, source_target_pairs={{0,1},{1,0},{2,3},{3,2},{4,5},{5,4},{6,7},{7,6},{8,9},{9,8},{10,11... | collective-permute-start | bytes 688136 | tf_op jit(solution)/shard_map/ppermute | solution.py:255
  52.2 25.8 %collective-permute-start.6 = (bf16[32,4608]{1,0:T(8,128)(2,1)S(1)}, bf16[32,4608]{1,0:T(8,128)(2,1)S(1)}, u32[]{:S(2)}, u32[]{:S(2)}) collective-permute-start(bf16[32,4608]{1,0:T(8,128)(2,1)S(1)} %pad_maximum_fusion.1.refs_4_), channel_id=1, source_target_pairs={{4,0},{0,4},{12,8},{8,12},{5,1},{1,5},{13,9},{9,13},{6,2},{2,6},{1... | collective-permute-start | bytes 884744 | tf_op jit(solution)/shard_map/ppermute | solution.py:252
  56.3 13.3 %collective-permute-start.8 = (bf16[32,3072]{1,0:T(8,128)(2,1)S(1)}, bf16[32,3072]{1,0:T(8,128)(2,1)S(1)}, u32[]{:S(2)}, u32[]{:S(2)}) collective-permute-start(bf16[32,3072]{1,0:T(8,128)(2,1)S(1)} %pad_maximum_fusion.2), channel_id=1, source_target_pairs={{0,2},{1,3},{2,0},{3,1},{4,6},{5,7},{6,4},{7,5},{8,10},{9,11},{10,... | collective-permute-start | bytes 589832 | tf_op jit(solution)/shard_map/ppermute | solution.py:255
  61.0 10.2 %collective-permute-start.12 = (bf16[32,1792]{1,0:T(8,128)(2,1)S(1)}, bf16[32,1792]{1,0:T(8,128)(2,1)S(1)}, u32[]{:S(2)}, u32[]{:S(2)}) collective-permute-start(bf16[32,1792]{1,0:T(8,128)(2,1)S(1)} %add_convert_fusion.3), channel_id=1, source_target_pairs={{0,2},{1,3},{2,0},{3,1},{4,6},{5,7},{6,4},{7,5},{8,10},{9,11},{10,... | collective-permute-start | bytes 344072 | tf_op jit(solution)/shard_map/ppermute | solution.py:255
  69.8 7.5 %collective-permute-start.9 = (bf16[32,2816]{1,0:T(8,128)(2,1)S(1)}, bf16[32,2816]{1,0:T(8,128)(2,1)S(1)}, u32[]{:S(2)}, u32[]{:S(2)}) collective-permute-start(bf16[32,2816]{1,0:T(8,128)(2,1)S(1)} %multiply_convert_fusion), channel_id=1, source_target_pairs={{8,0},{12,4},{0,8},{4,12},{9,1},{13,5},{1,9},{5,13},{10,2},{14,6},... | collective-permute-start | bytes 540680 | tf_op jit(solution)/shard_map/ppermute | solution.py:252
  71.2 6.1 %collective-permute-start.13 = (bf16[32,1792]{1,0:T(8,128)(2,1)S(1)}, bf16[32,1792]{1,0:T(8,128)(2,1)S(1)}, u32[]{:S(2)}, u32[]{:S(2)}) collective-permute-start(bf16[32,1792]{1,0:T(8,128)(2,1)S(1)} %multiply_convert_fusion.3), channel_id=1, source_target_pairs={{8,0},{12,4},{0,8},{4,12},{9,1},{13,5},{1,9},{5,13},{10,2},{14,6},... | collective-permute-start | bytes 344072 | tf_op jit(solution)/shard_map/ppermute | solution.py:252
  77.3 1.3 %collective-permute-start.14 = (bf16[32,1792]{1,0:T(8,128)(2,1)S(1)}, bf16[32,1792]{1,0:T(8,128)(2,1)S(1)}, u32[]{:S(2)}, u32[]{:S(2)}) collective-permute-start(bf16[32,1792]{1,0:T(8,128)(2,1)S(1)} %collective-permute-done.13.refs_8_), channel_id=1, source_target_pairs={{4,0},{0,4},{12,8},{8,12},{5,1},{1,5},{13,9},{9,13},{6,2},{2,6},{1... | collective-permute-start | bytes 344072 | tf_op jit(solution)/shard_map/ppermute | solution.py:252
  77.3 1.6 %collective-permute-start.10 = (bf16[32,2816]{1,0:T(8,128)(2,1)S(1)}, bf16[32,2816]{1,0:T(8,128)(2,1)S(1)}, u32[]{:S(2)}, u32[]{:S(2)}) collective-permute-start(bf16[32,2816]{1,0:T(8,128)(2,1)S(1)} %collective-permute-done.9.refs_6_), channel_id=1, source_target_pairs={{4,0},{0,4},{12,8},{8,12},{5,1},{1,5},{13,9},{9,13},{6,2},{2,6},{1... | collective-permute-start | bytes 540680 | tf_op jit(solution)/shard_map/ppermute | solution.py:252

commit v5 on v4

--- a/solution.py
+++ b/solution.py
@@ -115,42 +115,36 @@
     count = len(plan)
     places_ref, lengths_ref, cosine_ref, sine_ref = refs[:4]
     pieces = refs[4 : 4 + count]
-    keys_hbm, values_hbm, attended_ref, cache_rows_ref = refs[4 + count : 8 + count]
-    keys, values, table, heads, mixed, piece_sems, sems = refs[8 + count :]
-    fills = []
-    for at, ((source, first, width, start), piece) in enumerate(zip(plan, pieces)):
-        fill = pltpu.make_async_copy(
-            piece.at[pl.ds(start, rows), :], table.at[places_ref[source], :, pl.ds(first, width)], piece_sems.at[at]
-        )
-        fill.start()
-        fills.append(fill)
-    batch = 4
-    copies = []
-    for at in range(0, rows, batch):
-        span = pl.ds(at, batch)
-        copies.append(pltpu.make_async_copy(keys_hbm.at[span], keys.at[span], sems.at[0, at // batch]))
-        copies.append(pltpu.make_async_copy(values_hbm.at[span], values.at[span], sems.at[1, at // batch]))
-    for copy in copies:
-        copy.start()
-    for fill in fills:
-        fill.wait()
+    keys, values, _, attended_ref, cache_rows_ref = refs[4 + count : 9 + count]
+    heads, scores_ref, weights_ref, mixed = refs[9 + count :]
     cosine = cosine_ref[...]
     sine = sine_ref[...]
-    for h in range(HEADS + 2 * KV_HEADS):
-        column = (h % per_source) * HEAD_DIM
-        head = table[h // per_source, :, pl.ds(column, HEAD_DIM)].astype(f32)
-        if h < HEADS + KV_HEADS:
-            head = head * cosine + pltpu.roll(head, HEAD_DIM // 2, 1) * sine
-        head = head.astype(bf16)
-        if h >= HEADS:
-            cache_rows_ref[:, pl.ds((h - HEADS) * HEAD_DIM, HEAD_DIM)] = head
-        heads[pl.ds(h * rows, rows), :] = head.astype(f32)
+    rotated = HEADS + KV_HEADS
+    for (source, first, width, start), piece in zip(plan, pieces):
+        for column in range(0, width, HEAD_DIM):
+            local = (first + column) // HEAD_DIM
+            h = places_ref[source] * per_source + local
+            head = piece[pl.ds(start, rows), pl.ds(column, HEAD_DIM)].astype(f32)
+            turned = head * cosine + pltpu.roll(head, HEAD_DIM // 2, 1) * sine
+            if local + KV_HEADS >= per_source:
+                turned = jnp.where(h < rotated, turned, head)
+            heads[pl.ds(pl.multiple_of(h * rows, rows), rows), :] = turned.astype(bf16).astype(f32)
+    for h in range(2 * KV_HEADS):
+        cache_rows_ref[:, pl.ds(h * HEAD_DIM, HEAD_DIM)] = heads[pl.ds((HEADS + h) * rows, rows), :].astype(bf16)
     span = keys.shape[1]
     position = lax.broadcasted_iota(jnp.int32, (HEADS, span), 1)
-    for r in range(rows):
-        if r % batch == 0:
-            copies[r // batch * 2].wait()
-            copies[r // batch * 2 + 1].wait()
+
+    def score(r):
+        query = heads[pl.ds(r, HEADS, stride=rows), :].astype(bf16)
+        for k in range(KV_HEADS):
+            scores_ref[r, pl.ds(k * GROUP, GROUP), :] = lax.dot_general(
+                query[k * GROUP : (k + 1) * GROUP],
+                keys[r, :, pl.ds(k * HEAD_DIM, HEAD_DIM)],
+                (((1,), (1,)), ((), ())),
+                preferred_element_type=f32,
+            )
+
+    def soften(r):
         query = heads[pl.ds(r, HEADS, stride=rows), :]
         own_key = heads[pl.ds(HEADS * rows + r, KV_HEADS, stride=rows), :]
         own_value = heads[pl.ds((HEADS + KV_HEADS) * rows + r, KV_HEADS, stride=rows), :]
@@ -158,68 +152,87 @@
             [jnp.broadcast_to(own_key[k : k + 1], (GROUP, HEAD_DIM)) for k in range(KV_HEADS)], axis=0
         )
         own_score = jnp.sum(query * spread, axis=1, keepdims=True) * HEAD_DIM ** (-0.5)
-        query = query.astype(bf16)
-        scores = jnp.concatenate(
-            [
-                lax.dot_general(
-                    query[k * GROUP : (k + 1) * GROUP],
-                    keys[r, :, pl.ds(k * HEAD_DIM, HEAD_DIM)],
-                    (((1,), (1,)), ((), ())),
-                    preferred_element_type=f32,
-                )
-                for k in range(KV_HEADS)
-            ],
-            axis=0,
-        ) * HEAD_DIM ** (-0.5)
-        masked = jnp.where(position < lengths_ref[r], scores, -jnp.inf)
+        masked = jnp.where(position < lengths_ref[r], scores_ref[r] * HEAD_DIM ** (-0.5), -jnp.inf)
         top = jnp.maximum(jnp.max(masked, axis=1, keepdims=True), own_score)
         raised = jnp.exp(masked - top)
         raised_own = jnp.exp(own_score - top)
         inverse = 1.0 / (jnp.sum(raised, axis=1, keepdims=True) + raised_own)
-        weights = (raised * inverse).astype(bf16)
+        weights_ref[r] = (raised * inverse).astype(bf16)
         own_weight = (raised_own * inverse).astype(bf16).astype(f32)
-        result = jnp.concatenate(
-            [
+        spread = jnp.concatenate(
+            [jnp.broadcast_to(own_value[k : k + 1], (GROUP, HEAD_DIM)) for k in range(KV_HEADS)], axis=0
+        )
+        scores_ref[r] = own_weight * spread
+
+    def mix(r):
+        for k in range(KV_HEADS):
+            mixed[pl.ds(k * GROUP * rows + r, GROUP, stride=rows), :] = (
                 jnp.dot(
-                    weights[k * GROUP : (k + 1) * GROUP],
+                    weights_ref[r, pl.ds(k * GROUP, GROUP), :],
                     values[r, :, pl.ds(k * HEAD_DIM, HEAD_DIM)],
                     preferred_element_type=f32,
                 )
-                + own_weight[k * GROUP : (k + 1) * GROUP] * own_value[k : k + 1]
-                for k in range(KV_HEADS)
-            ],
-            axis=0,
-        )
-        mixed[pl.ds(r, HEADS, stride=rows), :] = result
+                + scores_ref[r, pl.ds(k * GROUP, GROUP), :]
+            )
+
+    for r in range(rows):
+        score(r)
+    for r in range(rows):
+        soften(r)
+    for r in range(rows):
+        mix(r)
     for h in range(HEADS):
         attended_ref[:, pl.ds(h * HEAD_DIM, HEAD_DIM)] = mixed[pl.ds(h * rows, rows), :].astype(bf16)
 
 
-def attend(plan, pieces, places, lengths, cosine, sine, key_cache, value_cache, sources, width):
+def attend(plan, pieces, places, lengths, cosine, sine, key_cache, value_cache, fetched, width):
     rows, span, kv_width = key_cache.shape
     smem = pl.BlockSpec(memory_space=pltpu.SMEM)
     vmem = pl.BlockSpec(memory_space=pltpu.VMEM)
-    hbm = pl.BlockSpec(memory_space=pltpu.HBM)
     return pl.pallas_call(
         functools.partial(attend_kernel, plan, rows, width // HEAD_DIM),
         out_shape=(
             jax.ShapeDtypeStruct((rows, HEADS * HEAD_DIM), bf16),
             jax.ShapeDtypeStruct((rows, 2 * KV_HEADS * HEAD_DIM), bf16),
         ),
-        in_specs=[smem, smem, vmem, vmem] + [hbm] * len(pieces) + [hbm, hbm],
+        in_specs=[smem, smem] + [vmem] * (len(pieces) + 5),
         out_specs=(vmem, vmem),
         scratch_shapes=[
-            pltpu.VMEM((rows, span, kv_width), bf16),
-            pltpu.VMEM((rows, span, kv_width), bf16),
-            pltpu.VMEM((sources, rows, width), bf16),
             pltpu.VMEM(((HEADS + 2 * KV_HEADS) * rows, HEAD_DIM), f32),
+            pltpu.VMEM((rows, HEADS, span), f32),
+            pltpu.VMEM((rows, HEADS, span), bf16),
             pltpu.VMEM((HEADS * rows, HEAD_DIM), f32),
-            pltpu.SemaphoreType.DMA((len(pieces),)),
-            pltpu.SemaphoreType.DMA((2, rows // 4)),
         ],
-        compiler_params=pltpu.CompilerParams(vmem_limit_bytes=24 * 2**20),
+        compiler_params=pltpu.CompilerParams(vmem_limit_bytes=12 * 2**20),
         name="attend",
-    )(places, lengths, cosine, sine, *pieces, key_cache, value_cache)
+    )(places, lengths, cosine, sine, *pieces, key_cache, value_cache, fetched)
+
+
+def fetch_kernel(keys_hbm, values_hbm, keys, values, fetched, sems):
+    loads = [
+        pltpu.make_async_copy(keys_hbm, keys, sems.at[0]),
+        pltpu.make_async_copy(values_hbm, values, sems.at[1]),
+    ]
+    for load in loads:
+        load.start()
+    for load in loads:
+        load.wait()
+    fetched[...] = jnp.zeros_like(fetched)
+
+
+def fetch(key_cache, value_cache):
+    vmem = pl.BlockSpec(memory_space=pltpu.VMEM)
+    hbm = pl.BlockSpec(memory_space=pltpu.HBM)
+    shape = jax.ShapeDtypeStruct(key_cache.shape, bf16)
+    return pl.pallas_call(
+        fetch_kernel,
+        out_shape=(shape, shape, jax.ShapeDtypeStruct((8, 128), f32)),
+        in_specs=[hbm, hbm],
+        out_specs=(vmem, vmem, vmem),
+        scratch_shapes=[pltpu.SemaphoreType.DMA((2,))],
+        compiler_params=pltpu.CompilerParams(vmem_limit_bytes=16 * 2**20),
+        name="fetch",
+    )(key_cache, value_cache)
 
 
 def rotation(lengths):
@@ -352,9 +365,11 @@
             done.append((total * scale).astype(bf16))
             first += chunk
         first = 0
-        for projected in [jnp.concatenate(done, axis=1)] if k == 0 else done:
-            if k:
-                projected = on_gx(projected, chips - k, 0)
+        sent = [jnp.concatenate(done, axis=1)] if k == 0 else [on_gx(part, chips - k, 0) for part in done]
+        if k + 1 == chips:
+            keys, values, fetched = fetch(in_hbm(after(key_cache, done)), in_hbm(value_cache))
+            sent, fetched = lax.optimization_barrier((sent, fetched))
+        for projected in sent:
             size = projected.shape[1]
             plan.append((k * CORES, first, size, 0))
             pieces.append(projected)
@@ -370,7 +385,7 @@
         ]
     ).astype(jnp.int32)
     return attend(
-        plan, pieces, places, lengths, cosine, sine, in_hbm(key_cache), in_hbm(value_cache), along_x, width
+        plan, pieces, places, lengths, cosine, sine, keys, values, fetched, width
     )
 
 

time: 90.2 us -> 97.5 us (1.081)
  waiting for transfers between devices: 27.8 us -> 35.5 us
  Pallas kernels: 45.4 us -> 43.2 us
  starting transfers between devices: 14 us -> 15.8 us
    ppermute x7, waiting for transfers between devices: 20.9 us -> 30.2 us  [on_z(): return lax.ppermute(array, 'gy', [(s, s ^ flip) for s in range(along_z)])]
    pallas_call x1, Pallas kernels: 10.9 us -> 5.29 us  [attend(): pl.pallas_call(functools.partial(attend_kernel, plan, rows, width // HEAD...]
    pallas_call x0 -> x1, Pallas kernels: none -> 3.49 us  [fetch(): pl.pallas_call(fetch_kernel, out_shape=(shape, shape, jax.ShapeDtypeStruc...]
    ppermute x7, starting transfers between devices: 7.73 us -> 9.94 us  [on_z(): return lax.ppermute(array, 'gy', [(s, s ^ flip) for s in range(along_z)])]
    ppermute x8, waiting for transfers between devices: 6.92 us -> 5.35 us  [on_gx(): return lax.ppermute(array, 'gx', pairs)]
  transfers between devices with their start and end apart: 15 -> 15, of which waited for: 8 -> 8; matrix products, arithmetic and copies ran while one was open for 2% -> 2% of each run, Pallas kernels for 38% -> 39%
where the time goes in v5:
time: 97.5 us; the launch traced here: 97.3 us
  Pallas kernels  43.2 us (44%)
  waiting for transfers between devices  35.5 us (36%)
  starting transfers between devices  15.8 us (16%)
  other arithmetic  1.04 us (1%)
    pallas_call x4, Pallas kernels, project(): pl.pallas_call(functools.partial(project_kernel, rows, kept, first, tiles...  34.5 us
    ppermute x7, waiting for transfers between devices, on_z(): return lax.ppermute(array, 'gy', [(s, s ^ flip) for s in range(along_z)])  30.2 us
    ppermute x7, starting transfers between devices, on_z(): return lax.ppermute(array, 'gy', [(s, s ^ flip) for s in range(along_z)])  9.94 us
    ppermute x8, starting transfers between devices, on_gx(): return lax.ppermute(array, 'gx', pairs)  5.89 us
    ppermute x8, waiting for transfers between devices, on_gx(): return lax.ppermute(array, 'gx', pairs)  5.35 us
    pallas_call x1, Pallas kernels, attend(): pl.pallas_call(functools.partial(attend_kernel, plan, rows, width // HEAD...  5.29 us
    pallas_call x1, Pallas kernels, fetch(): pl.pallas_call(fetch_kernel, out_shape=(shape, shape, jax.ShapeDtypeStruc...  3.49 us
  transfers between devices with their start and end apart: 15, of which 8 were waited for; matrix products, arithmetic and copies ran while one was open for 2% of the time, Pallas kernels for 39%

profile of v5, /device:TPU:0, one launch (start us, length us, event | category | flops | bytes accessed | tf_op | source)
XLA Modules:
  0.0 97.3 jit_solution(18129846691162233696)
XLA Ops:
  0.6 0.5 collective-permute-start
  1.1 2.6 %collective-permute-start.3 = (bf16[64,4096]{1,0:T(8,128)(2,1)}, bf16[64,4096]{1,0:T(8,128)(2,1)S(1)}, u32[]{:S(2)}, u32[]{:S(2)}) collective-permute-start(bf16[64,4096]{1,0:T(8,128)(2,1)} %a0_ref.2), channel_id=1, source_target_pairs={{8,0},{12,4},{0,8},{4,12},{9,1},{13,5},{1,9},{5,13},{10,2},{14,6},... | collective-permute-start | bytes 1572872 | tf_op jit(solution)/shard_map/ppermute | solution.py:265
  3.7 0.7 reshape.17.gain_ref
  4.4 0.0 collective-permute-done.a1_ref
  4.4 8.3 %project.4 = (f32[64,2432]{1,0:T(8,128)S(1)}, bf16[64,2560]{1,0:T(8,128)(2,1)S(1)}) custom-call(s32[1]{0:T(128)} %bitcast.4.z_ref, bf16[64,4096]{1,0:T(8,128)(2,1)} %a0_ref.2, bf16[64,4096]{1,0:T(8,128)(2,1)S(1)} %collective-permute-done.a1_ref, bf16[1,4096]{1,0:T(2,128)(2,1)S(1)} %reshape.17.gain_ref, bf16[4096,4608]{1,0:T(8,128)(2,1)} %w_hbm.7), custom_call_target="tpu_custom_call" | custom-call | tf_op jit(solution)/shard_map/project/pallas_call | solution.py:92
  12.7 1.6 %collective-permute-start.1 = (bf16[64,2560]{1,0:T(8,128)(2,1)S(1)}, bf16[64,2560]{1,0:T(8,128)(2,1)S(1)}, u32[]{:S(2)}, u32[]{:S(2)}) collective-permute-start(bf16[64,2560]{1,0:T(8,128)(2,1)S(1)} %get-tuple-element.25), channel_id=1, source_target_pairs={{0,1},{1,0},{2,3},{3,2},{4,5},{5,4},{6,7},{7,6},{8,9},{9,8},{10,11... | collective-permute-start | bytes 983048 | tf_op jit(solution)/shard_map/ppermute | solution.py:268
  14.4 0.0 copy-start
  14.4 8.3 %project.5 = (f32[64,2304]{1,0:T(8,128)S(1)}, bf16[64,2304]{1,0:T(8,128)(2,1)S(1)}) custom-call(s32[1]{0:T(128)} %bitcast.4.z_ref, bf16[64,4096]{1,0:T(8,128)(2,1)} %a0_ref.2, bf16[64,4096]{1,0:T(8,128)(2,1)S(1)} %collective-permute-done.a1_ref, bf16[1,4096]{1,0:T(2,128)(2,1)S(1)} %reshape.17.gain_ref, bf16[4096,4608]{1,0:T(8,128)(2,1)} %w_hbm.7), custom_call_target="tpu_custom_call" | custom-call | tf_op jit(solution)/shard_map/project/pallas_call | solution.py:92
  22.7 0.0 collective-permute-done.3.a0_ref
  22.7 0.1 collective-permute-start.4
  22.8 0.5 collective-permute-start.2
  23.3 0.0 copy-done
  23.3 0.0 collective-permute-done.1
  23.3 1.3 %collective-permute-done.4.a1_ref = bf16[64,4096]{1,0:T(8,128)(2,1)S(1)} collective-permute-done((bf16[64,4096]{1,0:T(8,128)(2,1)S(1)}, bf16[64,4096]{1,0:T(8,128)(2,1)S(1)}, u32[]{:S(2)}, u32[]{:S(2)}) %collective-permute-start.4) | collective-permute-done | bytes 524320 | tf_op jit(solution)/shard_map/ppermute | solution.py:265
  24.7 10.1 %project.6 = (f32[64,2944]{1,0:T(8,128)S(1)}, bf16[64,3072]{1,0:T(8,128)(2,1)S(1)}) custom-call(s32[1]{0:T(128)} %bitcast.4.z_ref, bf16[64,4096]{1,0:T(8,128)(2,1)S(1)} %collective-permute-done.3.a0_ref, bf16[64,4096]{1,0:T(8,128)(2,1)S(1)} %collective-permute-done.4.a1_ref, bf16[1,4096]{1,0:T(2,128)(2,1)S(1)} %reshape.17.gain_ref, bf16[4096,4608]{1,0:T(8,128)(2,1)} %w_hbm.7), custom_call_target="tpu_custom_call" | custom-call | tf_op jit(solution)/shard_map/project/pallas_call | solution.py:92
  34.8 0.0 collective-permute-done.2
  34.8 0.1 add_convert_fusion.1
  34.9 2.6 %collective-permute-start.5 = (bf16[32,4864]{1,0:T(8,128)(2,1)S(1)}, bf16[32,4864]{1,0:T(8,128)(2,1)S(1)}, u32[]{:S(2)}, u32[]{:S(2)}) collective-permute-start(bf16[32,4864]{1,0:T(8,128)(2,1)S(1)} %pad_maximum_fusion), channel_id=1, source_target_pairs={{0,2},{1,3},{2,0},{3,1},{4,6},{5,7},{6,4},{7,5},{8,10},{9,11},{10,... | collective-permute-start | bytes 933896 | tf_op jit(solution)/shard_map/ppermute | solution.py:268
  37.6 7.8 %project.7 = (f32[64,1792]{1,0:T(8,128)S(1)}, bf16[64,1792]{1,0:T(8,128)(2,1)S(1)}) custom-call(s32[1]{0:T(128)} %bitcast.4.z_ref, bf16[64,4096]{1,0:T(8,128)(2,1)S(1)} %collective-permute-done.3.a0_ref, bf16[64,4096]{1,0:T(8,128)(2,1)S(1)} %collective-permute-done.4.a1_ref, bf16[1,4096]{1,0:T(2,128)(2,1)S(1)} %reshape.17.gain_ref, bf16[4096,4608]{1,0:T(8,128)(2,1)} %w_hbm.7), custom_call_target="tpu_custom_call" | custom-call | tf_op jit(solution)/shard_map/project/pallas_call | solution.py:92
  45.3 0.5 collective-permute-start.10
  45.8 1.6 %collective-permute-start.7 = (bf16[64,3072]{1,0:T(8,128)(2,1)S(1)}, bf16[64,3072]{1,0:T(8,128)(2,1)S(1)}, u32[]{:S(2)}, u32[]{:S(2)}) collective-permute-start(bf16[64,3072]{1,0:T(8,128)(2,1)S(1)} %get-tuple-element.36), channel_id=1, source_target_pairs={{0,1},{1,0},{2,3},{3,2},{4,5},{5,4},{6,7},{7,6},{8,9},{9,8},{10,11... | collective-permute-start | bytes 1179656 | tf_op jit(solution)/shard_map/ppermute | solution.py:268
  47.4 4.5 %collective-permute-done.5 = bf16[32,4864]{1,0:T(8,128)(2,1)S(1)} collective-permute-done((bf16[32,4864]{1,0:T(8,128)(2,1)S(1)}, bf16[32,4864]{1,0:T(8,128)(2,1)S(1)}, u32[]{:S(2)}, u32[]{:S(2)}) %collective-permute-start.5) | collective-permute-done | bytes 311328 | tf_op jit(solution)/shard_map/ppermute | solution.py:268
  51.9 0.1 fusion.15
  52.0 0.1 multiply_convert_fusion.2
  52.2 0.1 collective-permute-start.6
  52.3 12.9 %collective-permute-done.7 = bf16[64,3072]{1,0:T(8,128)(2,1)S(1)} collective-permute-done((bf16[64,3072]{1,0:T(8,128)(2,1)S(1)}, bf16[64,3072]{1,0:T(8,128)(2,1)S(1)}, u32[]{:S(2)}, u32[]{:S(2)}) %collective-permute-start.7) | collective-permute-done | bytes 393248 | tf_op jit(solution)/shard_map/ppermute | solution.py:268
  65.2 0.0 collective-permute-done.10
  65.3 0.1 collective-permute-start.11
  65.4 3.0 %collective-permute-start.8 = (bf16[32,3072]{1,0:T(8,128)(2,1)S(1)}, bf16[32,3072]{1,0:T(8,128)(2,1)S(1)}, u32[]{:S(2)}, u32[]{:S(2)}) collective-permute-start(bf16[32,3072]{1,0:T(8,128)(2,1)S(1)} %pad_maximum_fusion.2), channel_id=1, source_target_pairs={{0,2},{1,3},{2,0},{3,1},{4,6},{5,7},{6,4},{7,5},{8,10},{9,11},{10,... | collective-permute-start | bytes 589832 | tf_op jit(solution)/shard_map/ppermute | solution.py:268
  68.4 12.8 %collective-permute-done.8 = bf16[32,3072]{1,0:T(8,128)(2,1)S(1)} collective-permute-done((bf16[32,3072]{1,0:T(8,128)(2,1)S(1)}, bf16[32,3072]{1,0:T(8,128)(2,1)S(1)}, u32[]{:S(2)}, u32[]{:S(2)}) %collective-permute-start.8) | collective-permute-done | bytes 196640 | tf_op jit(solution)/shard_map/ppermute | solution.py:268
  81.2 0.1 fusion.8
  81.3 0.0 collective-permute-done.11
  81.3 0.1 multiply_convert_fusion.3
  81.4 1.3 %collective-permute-start.12 = (bf16[32,1792]{1,0:T(8,128)(2,1)S(1)}, bf16[32,1792]{1,0:T(8,128)(2,1)S(1)}, u32[]{:S(2)}, u32[]{:S(2)}) collective-permute-start(bf16[32,1792]{1,0:T(8,128)(2,1)S(1)} %multiply_convert_fusion.3), channel_id=1, source_target_pairs={{8,0},{12,4},{0,8},{4,12},{9,1},{13,5},{1,9},{5,13},{10,2},{14,6},... | collective-permute-start | bytes 344072 | tf_op jit(solution)/shard_map/ppermute | solution.py:265
  82.7 0.1 multiply_convert_fusion
  82.8 0.8 collective-permute-start.9
  83.6 0.1 fusion.16
  83.8 3.5 %fetch.1 = (bf16[16,128,1024]{2,1,0:T(8,128)(2,1)S(1)}, bf16[16,128,1024]{2,1,0:T(8,128)(2,1)S(1)}, f32[8,128]{1,0:T(8,128)S(1)}) custom-call(bf16[16,128,1024]{2,1,0:T(8,128)(2,1)} %keys_hbm, bf16[16,128,1024]{2,1,0:T(8,128)(2,1)} %values_hbm.1), custom_call_target="tpu_custom_call" | custom-call | tf_op jit(solution)/shard_map/fetch/pallas_call | solution.py:227
  87.3 0.1 collective-permute-done.12.refs_8_
  87.5 2.9 %collective-permute-done.9.refs_6_ = bf16[32,2816]{1,0:T(8,128)(2,1)S(1)} collective-permute-done((bf16[32,2816]{1,0:T(8,128)(2,1)S(1)}, bf16[32,2816]{1,0:T(8,128)(2,1)S(1)}, u32[]{:S(2)}, u32[]{:S(2)}) %collective-permute-start.9) | collective-permute-done | bytes 180256 | tf_op jit(solution)/shard_map/ppermute | solution.py:265
  90.4 0.0 collective-permute-start.14
  90.4 0.5 collective-permute-start.13
  90.9 0.1 pad_add_fusion.refs_0_
  91.0 0.1 pad_maximum_fusion.3
  91.0 0.0 collective-permute-done.6.refs_5_
  91.0 0.7 collective-permute-done.14.refs_9_
  91.7 0.3 collective-permute-done.13.refs_7_
  92.0 5.3 %attend.1 = (bf16[16,16384]{1,0:T(8,128)(2,1)}, bf16[16,2048]{1,0:T(8,128)(2,1)}) custom-call(s32[4]{0:T(128)S(1)} %pad_add_fusion.refs_0_, s32[16]{0:T(128)S(1)} %copy-done, f32[16,128]{1,0:T(8,128)S(1)} %get-tuple-element.67.refs_2_, f32[16,128]{1,0:T(8,128)S(1)} %get-tuple-element.68.refs_3_, bf16[32,4608]{1,0:T(8,128)(2,1)S(1)} %pad_maximum_fusion.1.refs_4_, ...), custom_call_target="tpu_custom_call" | custom-call | tf_op jit(solution)/shard_map/attend/pallas_call | solution.py:192
  (13 shorter events, 0.2 us)
Async XLA Ops:
  0.6 3.8 %collective-permute-start = (bf16[64,4096]{1,0:T(8,128)(2,1)}, bf16[64,4096]{1,0:T(8,128)(2,1)S(1)}, u32[]{:S(2)}, u32[]{:S(2)}) collective-permute-start(bf16[64,4096]{1,0:T(8,128)(2,1)} %a0_ref.2), channel_id=1, source_target_pairs={{4,0},{0,4},{12,8},{8,12},{5,1},{1,5},{13,9},{9,13},{6,2},{2,6},{1... | collective-permute-start | bytes 1572872 | tf_op jit(solution)/shard_map/ppermute | solution.py:265
  1.1 21.5 %collective-permute-start.3 = (bf16[64,4096]{1,0:T(8,128)(2,1)}, bf16[64,4096]{1,0:T(8,128)(2,1)S(1)}, u32[]{:S(2)}, u32[]{:S(2)}) collective-permute-start(bf16[64,4096]{1,0:T(8,128)(2,1)} %a0_ref.2), channel_id=1, source_target_pairs={{8,0},{12,4},{0,8},{4,12},{9,1},{13,5},{1,9},{5,13},{10,2},{14,6},... | collective-permute-start | bytes 1572872 | tf_op jit(solution)/shard_map/ppermute | solution.py:265
  12.7 10.5 %collective-permute-start.1 = (bf16[64,2560]{1,0:T(8,128)(2,1)S(1)}, bf16[64,2560]{1,0:T(8,128)(2,1)S(1)}, u32[]{:S(2)}, u32[]{:S(2)}) collective-permute-start(bf16[64,2560]{1,0:T(8,128)(2,1)S(1)} %get-tuple-element.25), channel_id=1, source_target_pairs={{0,1},{1,0},{2,3},{3,2},{4,5},{5,4},{6,7},{7,6},{8,9},{9,8},{10,11... | collective-permute-start | bytes 983048 | tf_op jit(solution)/shard_map/ppermute | solution.py:268
  14.4 8.9 %copy-start = (s32[16]{0:T(128)S(1)}, s32[16]{0:T(128)}, u32[]{:S(2)}) copy-start(s32[16]{0:T(128)} %refs_1_.1) | copy-start | bytes 196
  22.7 2.0 %collective-permute-start.4 = (bf16[64,4096]{1,0:T(8,128)(2,1)S(1)}, bf16[64,4096]{1,0:T(8,128)(2,1)S(1)}, u32[]{:S(2)}, u32[]{:S(2)}) collective-permute-start(bf16[64,4096]{1,0:T(8,128)(2,1)S(1)} %collective-permute-done.3.a0_ref), channel_id=1, source_target_pairs={{4,0},{0,4},{12,8},{8,12},{5,1},{1,5},{13,9},{9,13},{6,2},{2,6},{1... | collective-permute-start | bytes 1572872 | tf_op jit(solution)/shard_map/ppermute | solution.py:265
  22.8 12.0 %collective-permute-start.2 = (bf16[64,2304]{1,0:T(8,128)(2,1)S(1)}, bf16[64,2304]{1,0:T(8,128)(2,1)S(1)}, u32[]{:S(2)}, u32[]{:S(2)}) collective-permute-start(bf16[64,2304]{1,0:T(8,128)(2,1)S(1)} %get-tuple-element.28), channel_id=1, source_target_pairs={{0,1},{1,0},{2,3},{3,2},{4,5},{5,4},{6,7},{7,6},{8,9},{9,8},{10,11... | collective-permute-start | bytes 884744 | tf_op jit(solution)/shard_map/ppermute | solution.py:268
  34.9 17.0 %collective-permute-start.5 = (bf16[32,4864]{1,0:T(8,128)(2,1)S(1)}, bf16[32,4864]{1,0:T(8,128)(2,1)S(1)}, u32[]{:S(2)}, u32[]{:S(2)}) collective-permute-start(bf16[32,4864]{1,0:T(8,128)(2,1)S(1)} %pad_maximum_fusion), channel_id=1, source_target_pairs={{0,2},{1,3},{2,0},{3,1},{4,6},{5,7},{6,4},{7,5},{8,10},{9,11},{10,... | collective-permute-start | bytes 933896 | tf_op jit(solution)/shard_map/ppermute | solution.py:268
  45.3 19.9 %collective-permute-start.10 = (bf16[64,1792]{1,0:T(8,128)(2,1)S(1)}, bf16[64,1792]{1,0:T(8,128)(2,1)S(1)}, u32[]{:S(2)}, u32[]{:S(2)}) collective-permute-start(bf16[64,1792]{1,0:T(8,128)(2,1)S(1)} %get-tuple-element.37), channel_id=1, source_target_pairs={{0,1},{1,0},{2,3},{3,2},{4,5},{5,4},{6,7},{7,6},{8,9},{9,8},{10,11... | collective-permute-start | bytes 688136 | tf_op jit(solution)/shard_map/ppermute | solution.py:268
  45.8 19.3 %collective-permute-start.7 = (bf16[64,3072]{1,0:T(8,128)(2,1)S(1)}, bf16[64,3072]{1,0:T(8,128)(2,1)S(1)}, u32[]{:S(2)}, u32[]{:S(2)}) collective-permute-start(bf16[64,3072]{1,0:T(8,128)(2,1)S(1)} %get-tuple-element.36), channel_id=1, source_target_pairs={{0,1},{1,0},{2,3},{3,2},{4,5},{5,4},{6,7},{7,6},{8,9},{9,8},{10,11... | collective-permute-start | bytes 1179656 | tf_op jit(solution)/shard_map/ppermute | solution.py:268
  52.2 38.8 %collective-permute-start.6 = (bf16[32,4608]{1,0:T(8,128)(2,1)S(1)}, bf16[32,4608]{1,0:T(8,128)(2,1)S(1)}, u32[]{:S(2)}, u32[]{:S(2)}) collective-permute-start(bf16[32,4608]{1,0:T(8,128)(2,1)S(1)} %pad_maximum_fusion.1.refs_4_), channel_id=1, source_target_pairs={{4,0},{0,4},{12,8},{8,12},{5,1},{1,5},{13,9},{9,13},{6,2},{2,6},{1... | collective-permute-start | bytes 884744 | tf_op jit(solution)/shard_map/ppermute | solution.py:265
  65.3 16.0 %collective-permute-start.11 = (bf16[32,1792]{1,0:T(8,128)(2,1)S(1)}, bf16[32,1792]{1,0:T(8,128)(2,1)S(1)}, u32[]{:S(2)}, u32[]{:S(2)}) collective-permute-start(bf16[32,1792]{1,0:T(8,128)(2,1)S(1)} %add_convert_fusion.3), channel_id=1, source_target_pairs={{0,2},{1,3},{2,0},{3,1},{4,6},{5,7},{6,4},{7,5},{8,10},{9,11},{10,... | collective-permute-start | bytes 344072 | tf_op jit(solution)/shard_map/ppermute | solution.py:268
  65.4 15.8 %collective-permute-start.8 = (bf16[32,3072]{1,0:T(8,128)(2,1)S(1)}, bf16[32,3072]{1,0:T(8,128)(2,1)S(1)}, u32[]{:S(2)}, u32[]{:S(2)}) collective-permute-start(bf16[32,3072]{1,0:T(8,128)(2,1)S(1)} %pad_maximum_fusion.2), channel_id=1, source_target_pairs={{0,2},{1,3},{2,0},{3,1},{4,6},{5,7},{6,4},{7,5},{8,10},{9,11},{10,... | collective-permute-start | bytes 589832 | tf_op jit(solution)/shard_map/ppermute | solution.py:268
  81.4 6.1 %collective-permute-start.12 = (bf16[32,1792]{1,0:T(8,128)(2,1)S(1)}, bf16[32,1792]{1,0:T(8,128)(2,1)S(1)}, u32[]{:S(2)}, u32[]{:S(2)}) collective-permute-start(bf16[32,1792]{1,0:T(8,128)(2,1)S(1)} %multiply_convert_fusion.3), channel_id=1, source_target_pairs={{8,0},{12,4},{0,8},{4,12},{9,1},{13,5},{1,9},{5,13},{10,2},{14,6},... | collective-permute-start | bytes 344072 | tf_op jit(solution)/shard_map/ppermute | solution.py:265
  82.8 7.6 %collective-permute-start.9 = (bf16[32,2816]{1,0:T(8,128)(2,1)S(1)}, bf16[32,2816]{1,0:T(8,128)(2,1)S(1)}, u32[]{:S(2)}, u32[]{:S(2)}) collective-permute-start(bf16[32,2816]{1,0:T(8,128)(2,1)S(1)} %multiply_convert_fusion), channel_id=1, source_target_pairs={{8,0},{12,4},{0,8},{4,12},{9,1},{13,5},{1,9},{5,13},{10,2},{14,6},... | collective-permute-start | bytes 540680 | tf_op jit(solution)/shard_map/ppermute | solution.py:265
  90.4 1.3 %collective-permute-start.14 = (bf16[32,1792]{1,0:T(8,128)(2,1)S(1)}, bf16[32,1792]{1,0:T(8,128)(2,1)S(1)}, u32[]{:S(2)}, u32[]{:S(2)}) collective-permute-start(bf16[32,1792]{1,0:T(8,128)(2,1)S(1)} %collective-permute-done.12.refs_8_), channel_id=1, source_target_pairs={{4,0},{0,4},{12,8},{8,12},{5,1},{1,5},{13,9},{9,13},{6,2},{2,6},{1... | collective-permute-start | bytes 344072 | tf_op jit(solution)/shard_map/ppermute | solution.py:265
  90.4 1.6 %collective-permute-start.13 = (bf16[32,2816]{1,0:T(8,128)(2,1)S(1)}, bf16[32,2816]{1,0:T(8,128)(2,1)S(1)}, u32[]{:S(2)}, u32[]{:S(2)}) collective-permute-start(bf16[32,2816]{1,0:T(8,128)(2,1)S(1)} %collective-permute-done.9.refs_6_), channel_id=1, source_target_pairs={{4,0},{0,4},{12,8},{8,12},{5,1},{1,5},{13,9},{9,13},{6,2},{2,6},{1... | collective-permute-start | bytes 540680 | tf_op jit(solution)/shard_map/ppermute | solution.py:265

commit v6 on v5

--- a/solution.py
+++ b/solution.py
@@ -284,98 +284,110 @@
     plan = []
     pieces = []
 
-    def after(array, other):
-        return lax.optimization_barrier((array, other))[0]
-
-    kinds = range(chips)
-    chunks = {k: cuts[min(k, 1)] for k in kinds}
-    keeps = {k: [] for k in kinds}
-    receiveds = {k: [] for k in kinds}
-    aways = {}
-
-    def add_pairs(k):
-        owns, away = [], []
-        for c, chunk in enumerate(chunks[k]):
-            keep, received = keeps[k][c], receiveds[k][c]
-            if k and c:
-                received = after(received, away[2])
-            for part, start in ((owns, 0), (away, first_rows)):
-                span = slice(start, start + first_rows) if start == 0 else slice(start, None)
-                if c == 0:
-                    square = (
-                        keep[span, :HEAD_DIM]
-                        + received[span, :HEAD_DIM].astype(f32)
-                        + received[span, HEAD_DIM : 2 * HEAD_DIM].astype(f32)
-                    )
-                    if start:
-                        upper = lax.reduce_precision(square, 8, 7)
-                        part.append(upper.astype(bf16))
-                        part.append((square - upper).astype(bf16))
-                    else:
-                        part.append(square)
-                skip = HEAD_DIM if c == 0 else 0
-                total = keep[span, skip:] + received[span, 2 * skip :].astype(f32)
-                part.append(total.astype(bf16) if start else total)
-        if k == 0:
-            return owns, [jnp.concatenate(away, axis=1)]
-        return owns, [jnp.concatenate(away[:3], axis=1), *away[3:]]
-
-    owns = {}
-    arrived = {}
-    for k in kinds:
+    def tie(*arrays):
+        return lax.optimization_barrier(arrays)
+
+    units = [
+        (k, sum(cuts[min(k, 1)][:c]), chunk, c == 0)
+        for k in range(chips)
+        for c, chunk in enumerate(cuts[min(k, 1)])
+    ]
+    count = len(units)
+    keeps, receiveds, owns, aways, arrived = [], [], [], [], []
+
+    def add_pair(keep, received, squared):
+        results = []
+        for rest in (False, True):
+            span = slice(first_rows, None) if rest else slice(0, first_rows)
+            skip = HEAD_DIM if squared else 0
+            parts = []
+            if squared:
+                square = (
+                    keep[span, :HEAD_DIM]
+                    + received[span, :HEAD_DIM].astype(f32)
+                    + received[span, HEAD_DIM : 2 * HEAD_DIM].astype(f32)
+                )
+                upper = lax.reduce_precision(square, 8, 7)
+                parts = [upper.astype(bf16), (square - upper).astype(bf16)] if rest else [square]
+            total = keep[span, skip:] + received[span, 2 * skip :].astype(f32)
+            results.append(parts + [total.astype(bf16) if rest else total])
+        return results
+
+    def step_one(u):
+        own, away = add_pair(keeps[u], receiveds[u], units[u][3])
+        owns.append(own)
+        aways.append(jnp.concatenate(away, axis=1) if len(away) > 1 else away[0])
+
+    def step_two(u):
+        away = aways[u]
+        arrived.append([on_z(away[(i - 1) * first_rows : i * first_rows], 2 * i) for i in range(1, kept)])
+
+    for u, (k, first, chunk, squared) in enumerate(units):
+        if u > 1:
+            receiveds[u - 2], keeps[u - 1] = tie(receiveds[u - 2], keeps[u - 1])
+        if squared and k:
+            array, keeps[u - 1] = tie(there[k - 1], keeps[u - 1])
+            a0, a1 = array, on_gx(array, 0, 1)
+        elif squared:
+            a0, a1 = here[0]
+        else:
+            a0, keeps[u - 1] = tie(a0, keeps[u - 1])
+        if u > 1:
+            step_one(u - 2)
+            a0, aways[u - 2] = tie(a0, aways[u - 2])
+            step_two(u - 2)
+        if u > 2:
+            a0, arrived[u - 3] = tie(a0, arrived[u - 3])
+        keep, send = project(z, a0, a1, gain, weight, rows, first, chunk, squared)
+        keeps.append(keep)
+        receiveds.append(on_z(send, 1))
+    plan, pieces, scales, projecteds = [], [], {}, []
+
+    def finish(u):
+        k, first, chunk, squared = units[u]
+        own, others = owns[u], arrived[u]
+        skip = 2 * HEAD_DIM if squared else 0
+        if squared:
+            square = own[0]
+            for other in others:
+                square = square + other[:, :HEAD_DIM].astype(f32) + other[:, HEAD_DIM:skip].astype(f32)
+            scales[k] = lax.rsqrt(square[:, :1] * (1.0 / D) + norm_eps)
+        total = own[-1]
+        for other in others:
+            total = total + other[:, skip:].astype(f32)
+        projecteds.append((total * scales[k]).astype(bf16))
+
+    def hand_out(u):
+        k, first, chunk, squared = units[u]
+        projected = projecteds[u]
         if k:
-            a0 = after(there[k - 1], keeps[k - 1])
-            a1 = on_gx(a0, 0, 1)
-            if len(chunks[0]) > 1:
-                a0 = after(a0, receiveds[k - 1][0])
-        else:
-            a0, a1 = here[0]
-        first = 0
-        for c, chunk in enumerate(chunks[k]):
-            if k == 0 and c:
-                a0 = after(a0, keeps[0][0])
-            keep, send = project(z, a0, a1, gain, weight, rows, first, chunk, c == 0)
-            first += chunk
-            keeps[k].append(keep)
-            receiveds[k].append(on_z(send, 1))
-            if k and c == 0:
-                receiveds[k - 1][-1] = after(receiveds[k - 1][-1], keep)
-                owns[k - 1], aways[k - 1] = add_pairs(k - 1)
-                a0 = after(a0, aways[k - 1])
-    owns[chips - 1], aways[chips - 1] = add_pairs(chips - 1)
-    for k in kinds:
-        arrived[k] = [
-            [on_z(away[(i - 1) * first_rows : i * first_rows], 2 * i) for i in range(1, kept)]
-            for away in aways[k]
-        ]
-        if k + 1 < chips:
-            arrived[k] = after(arrived[k], keeps[k + 1][-1])
-    for k in kinds:
-        square = owns[k][0]
-        for other in arrived[k][0]:
-            square = square + other[:, :HEAD_DIM].astype(f32) + other[:, HEAD_DIM : 2 * HEAD_DIM].astype(f32)
-        scale = lax.rsqrt(square[:, :1] * (1.0 / D) + norm_eps)
-        done = []
-        first = 0
-        for c, chunk in enumerate(chunks[k]):
-            total = owns[k][c + 1]
-            for other in arrived[k][0 if k == 0 else c]:
-                skip = 2 * HEAD_DIM + first if k == 0 else (2 * HEAD_DIM if c == 0 else 0)
-                total = total + other[:, skip : skip + chunk].astype(f32)
-            done.append((total * scale).astype(bf16))
-            first += chunk
-        first = 0
-        sent = [jnp.concatenate(done, axis=1)] if k == 0 else [on_gx(part, chips - k, 0) for part in done]
-        if k + 1 == chips:
-            keys, values, fetched = fetch(in_hbm(after(key_cache, done)), in_hbm(value_cache))
-            sent, fetched = lax.optimization_barrier((sent, fetched))
-        for projected in sent:
-            size = projected.shape[1]
-            plan.append((k * CORES, first, size, 0))
-            pieces.append(projected)
-            plan.append((k * CORES + 1, first, size, rows))
-            pieces.append(on_gx(projected, 0, 1))
-            first += size
+            projected = on_gx(projected, chips - k, 0)
+        plan.append((k * CORES, first, chunk, 0))
+        plan.append((k * CORES + 1, first, chunk, rows))
+        return projected
+
+    for u in range(max(count - 2, 0), count):
+        if u + 1 < count and u:
+            receiveds[u], keeps[u + 1], arrived[u - 1] = tie(receiveds[u], keeps[u + 1], arrived[u - 1])
+        elif u:
+            *arrived[:], aways[u - 1] = tie(*arrived, aways[u - 1])
+            step_two(u - 1)
+            for before in range(u - 1):
+                finish(before)
+            if projecteds:
+                receiveds[u], projecteds[-1], aways[u - 1] = tie(receiveds[u], projecteds[-1], aways[u - 1])
+        step_one(u)
+    step_two(count - 1)
+    if count > 1:
+        finish(count - 2)
+    finish(count - 1)
+    projecteds[-1], key_cache = tie(projecteds[-1], key_cache)
+    keys, values, fetched = fetch(in_hbm(key_cache), in_hbm(value_cache))
+    held = [hand_out(u) for u in range(count)]
+    held[-1], fetched = tie(held[-1], fetched)
+    for projected in held:
+        pieces.append(projected)
+        pieces.append(on_gx(projected, 0, 1))
     x, core = gx // CORES, gx % CORES
     places = jnp.stack(
         [

time: 97.5 us -> 82.2 us (0.84)
  waiting for transfers between devices: 35.5 us -> 18.4 us
  starting transfers between devices: 15.8 us -> 17.8 us
    ppermute x7 -> x8, waiting for transfers between devices: 30.2 us -> 15.6 us  [on_z(): return lax.ppermute(array, 'gy', [(s, s ^ flip) for s in range(along_z)])]
    ppermute x8 -> x9, waiting for transfers between devices: 5.35 us -> 2.74 us  [on_gx(): return lax.ppermute(array, 'gx', pairs)]
    ppermute x7 -> x8, starting transfers between devices: 9.94 us -> 11.8 us  [on_z(): return lax.ppermute(array, 'gy', [(s, s ^ flip) for s in range(along_z)])]
    ppermute x8 -> x9, starting transfers between devices: 5.89 us -> 5.96 us  [on_gx(): return lax.ppermute(array, 'gx', pairs)]
  transfers between devices with their start and end apart: 15 -> 17, of which waited for: 8 -> 7; matrix products, arithmetic and copies ran while one was open for 2% -> 2% of each run, Pallas kernels for 39% -> 46%
where the time goes in v6:
time: 82.2 us; the launch traced here: 82 us
  Pallas kernels  43.3 us (53%)
  waiting for transfers between devices  18.4 us (22%)
  starting transfers between devices  17.8 us (22%)
  other arithmetic  1.01 us (1%)
    pallas_call x4, Pallas kernels, project(): pl.pallas_call(functools.partial(project_kernel, rows, kept, first, tiles...  34.5 us
    ppermute x8, waiting for transfers between devices, on_z(): return lax.ppermute(array, 'gy', [(s, s ^ flip) for s in range(along_z)])  15.6 us
    ppermute x8, starting transfers between devices, on_z(): return lax.ppermute(array, 'gy', [(s, s ^ flip) for s in range(along_z)])  11.8 us
    ppermute x9, starting transfers between devices, on_gx(): return lax.ppermute(array, 'gx', pairs)  5.96 us
    pallas_call x1, Pallas kernels, attend(): pl.pallas_call(functools.partial(attend_kernel, plan, rows, width // HEAD...  5.29 us
    pallas_call x1, Pallas kernels, fetch(): pl.pallas_call(fetch_kernel, out_shape=(shape, shape, jax.ShapeDtypeStruc...  3.48 us
    ppermute x9, waiting for transfers between devices, on_gx(): return lax.ppermute(array, 'gx', pairs)  2.74 us
  transfers between devices with their start and end apart: 17, of which 7 were waited for; matrix products, arithmetic and copies ran while one was open for 2% of the time, Pallas kernels for 46%

profile of v6, /device:TPU:0, one launch (start us, length us, event | category | flops | bytes accessed | tf_op | source)
XLA Modules:
  0.0 82.0 jit_solution(2781876281427495393)
XLA Ops:
  0.6 0.5 collective-permute-start
  1.1 2.6 %collective-permute-start.2 = (bf16[64,4096]{1,0:T(8,128)(2,1)}, bf16[64,4096]{1,0:T(8,128)(2,1)S(1)}, u32[]{:S(2)}, u32[]{:S(2)}) collective-permute-start(bf16[64,4096]{1,0:T(8,128)(2,1)} %a0_ref.2), channel_id=1, source_target_pairs={{8,0},{12,4},{0,8},{4,12},{9,1},{13,5},{1,9},{5,13},{10,2},{14,6},... | collective-permute-start | bytes 1572872 | tf_op jit(solution)/shard_map/ppermute | solution.py:265
  3.7 0.7 reshape.17.gain_ref
  4.4 0.0 collective-permute-done.a1_ref
  4.4 0.0 copy-start
  4.4 8.3 %project.4 = (f32[64,2432]{1,0:T(8,128)S(1)}, bf16[64,2560]{1,0:T(8,128)(2,1)S(1)}) custom-call(s32[1]{0:T(128)} %bitcast.4.z_ref, bf16[64,4096]{1,0:T(8,128)(2,1)} %a0_ref.2, bf16[64,4096]{1,0:T(8,128)(2,1)S(1)} %collective-permute-done.a1_ref, bf16[1,4096]{1,0:T(2,128)(2,1)S(1)} %reshape.17.gain_ref, bf16[4096,4608]{1,0:T(8,128)(2,1)} %w_hbm.7), custom_call_target="tpu_custom_call" | custom-call | tf_op jit(solution)/shard_map/project/pallas_call | solution.py:92
  12.8 1.6 %collective-permute-start.1 = (bf16[64,2560]{1,0:T(8,128)(2,1)S(1)}, bf16[64,2560]{1,0:T(8,128)(2,1)S(1)}, u32[]{:S(2)}, u32[]{:S(2)}) collective-permute-start(bf16[64,2560]{1,0:T(8,128)(2,1)S(1)} %get-tuple-element.43), channel_id=1, source_target_pairs={{0,1},{1,0},{2,3},{3,2},{4,5},{5,4},{6,7},{7,6},{8,9},{9,8},{10,11... | collective-permute-start | bytes 983048 | tf_op jit(solution)/shard_map/ppermute | solution.py:268
  14.4 8.3 %project.5 = (f32[64,2304]{1,0:T(8,128)S(1)}, bf16[64,2304]{1,0:T(8,128)(2,1)S(1)}) custom-call(s32[1]{0:T(128)} %bitcast.4.z_ref, bf16[64,4096]{1,0:T(8,128)(2,1)} %a0_ref.2, bf16[64,4096]{1,0:T(8,128)(2,1)S(1)} %collective-permute-done.a1_ref, bf16[1,4096]{1,0:T(2,128)(2,1)S(1)} %reshape.17.gain_ref, bf16[4096,4608]{1,0:T(8,128)(2,1)} %w_hbm.7), custom_call_target="tpu_custom_call" | custom-call | tf_op jit(solution)/shard_map/project/pallas_call | solution.py:92
  22.7 0.5 collective-permute-start.3
  23.2 0.0 collective-permute-done.1
  23.2 0.0 collective-permute-done.2.a0_ref
  23.2 0.0 collective-permute-start.4
  23.3 2.7 %collective-permute-start.5 = (bf16[32,2560]{1,0:T(8,128)(2,1)S(1)}, bf16[32,2560]{1,0:T(8,128)(2,1)S(1)}, u32[]{:S(2)}, u32[]{:S(2)}) collective-permute-start(bf16[32,2560]{1,0:T(8,128)(2,1)S(1)} %pad_maximum_fusion.1), channel_id=1, source_target_pairs={{0,2},{1,3},{2,0},{3,1},{4,6},{5,7},{6,4},{7,5},{8,10},{9,11},{10,... | collective-permute-start | bytes 491528 | tf_op jit(solution)/shard_map/ppermute | solution.py:268
  26.0 0.0 collective-permute-done.4.a1_ref
  26.0 10.1 %project.6 = (f32[64,2944]{1,0:T(8,128)S(1)}, bf16[64,3072]{1,0:T(8,128)(2,1)S(1)}) custom-call(s32[1]{0:T(128)} %bitcast.4.z_ref, bf16[64,4096]{1,0:T(8,128)(2,1)S(1)} %collective-permute-done.2.a0_ref, bf16[64,4096]{1,0:T(8,128)(2,1)S(1)} %collective-permute-done.4.a1_ref, bf16[1,4096]{1,0:T(2,128)(2,1)S(1)} %reshape.17.gain_ref, bf16[4096,4608]{1,0:T(8,128)(2,1)} %w_hbm.7), custom_call_target="tpu_custom_call" | custom-call | tf_op jit(solution)/shard_map/project/pallas_call | solution.py:92
  36.1 0.0 collective-permute-done.3
  36.2 1.6 %collective-permute-start.6 = (bf16[64,3072]{1,0:T(8,128)(2,1)S(1)}, bf16[64,3072]{1,0:T(8,128)(2,1)S(1)}, u32[]{:S(2)}, u32[]{:S(2)}) collective-permute-start(bf16[64,3072]{1,0:T(8,128)(2,1)S(1)} %get-tuple-element.59), channel_id=1, source_target_pairs={{0,1},{1,0},{2,3},{3,2},{4,5},{5,4},{6,7},{7,6},{8,9},{9,8},{10,11... | collective-permute-start | bytes 1179656 | tf_op jit(solution)/shard_map/ppermute | solution.py:268
  37.8 1.8 %collective-permute-start.7 = (bf16[32,2304]{1,0:T(8,128)(2,1)S(1)}, bf16[32,2304]{1,0:T(8,128)(2,1)S(1)}, u32[]{:S(2)}, u32[]{:S(2)}) collective-permute-start(bf16[32,2304]{1,0:T(8,128)(2,1)S(1)} %add_convert_fusion.1), channel_id=1, source_target_pairs={{0,2},{1,3},{2,0},{3,1},{4,6},{5,7},{6,4},{7,5},{8,10},{9,11},{10,... | collective-permute-start | bytes 442376 | tf_op jit(solution)/shard_map/ppermute | solution.py:268
  39.6 7.7 %project.7 = (f32[64,1792]{1,0:T(8,128)S(1)}, bf16[64,1792]{1,0:T(8,128)(2,1)S(1)}) custom-call(s32[1]{0:T(128)} %bitcast.4.z_ref, bf16[64,4096]{1,0:T(8,128)(2,1)S(1)} %collective-permute-done.2.a0_ref, bf16[64,4096]{1,0:T(8,128)(2,1)S(1)} %collective-permute-done.4.a1_ref, bf16[1,4096]{1,0:T(2,128)(2,1)S(1)} %reshape.17.gain_ref, bf16[4096,4608]{1,0:T(8,128)(2,1)} %w_hbm.7), custom_call_target="tpu_custom_call" | custom-call | tf_op jit(solution)/shard_map/project/pallas_call | solution.py:92
  47.4 0.5 collective-permute-start.9
  47.9 2.5 %collective-permute-done.7 = bf16[32,2304]{1,0:T(8,128)(2,1)S(1)} collective-permute-done((bf16[32,2304]{1,0:T(8,128)(2,1)S(1)}, bf16[32,2304]{1,0:T(8,128)(2,1)S(1)}, u32[]{:S(2)}, u32[]{:S(2)}) %collective-permute-start.7) | collective-permute-done | bytes 147488 | tf_op jit(solution)/shard_map/ppermute | solution.py:268
  50.4 0.9 %collective-permute-done.6 = bf16[64,3072]{1,0:T(8,128)(2,1)S(1)} collective-permute-done((bf16[64,3072]{1,0:T(8,128)(2,1)S(1)}, bf16[64,3072]{1,0:T(8,128)(2,1)S(1)}, u32[]{:S(2)}, u32[]{:S(2)}) %collective-permute-start.6) | collective-permute-done | bytes 393248 | tf_op jit(solution)/shard_map/ppermute | solution.py:268
  51.4 2.5 %collective-permute-start.11 = (bf16[32,3072]{1,0:T(8,128)(2,1)S(1)}, bf16[32,3072]{1,0:T(8,128)(2,1)S(1)}, u32[]{:S(2)}, u32[]{:S(2)}) collective-permute-start(bf16[32,3072]{1,0:T(8,128)(2,1)S(1)} %pad_maximum_fusion), channel_id=1, source_target_pairs={{0,2},{1,3},{2,0},{3,1},{4,6},{5,7},{6,4},{7,5},{8,10},{9,11},{10,... | collective-permute-start | bytes 589832 | tf_op jit(solution)/shard_map/ppermute | solution.py:268
  54.0 0.1 fusion.15
  54.1 0.1 multiply_convert_fusion.1
  54.2 4.3 %collective-permute-done.9 = bf16[64,1792]{1,0:T(8,128)(2,1)S(1)} collective-permute-done((bf16[64,1792]{1,0:T(8,128)(2,1)S(1)}, bf16[64,1792]{1,0:T(8,128)(2,1)S(1)}, u32[]{:S(2)}, u32[]{:S(2)}) %collective-permute-start.9) | collective-permute-done | bytes 229408 | tf_op jit(solution)/shard_map/ppermute | solution.py:268
  58.5 0.5 collective-permute-start.14
  59.0 6.6 %collective-permute-done.11 = bf16[32,3072]{1,0:T(8,128)(2,1)S(1)} collective-permute-done((bf16[32,3072]{1,0:T(8,128)(2,1)S(1)}, bf16[32,3072]{1,0:T(8,128)(2,1)S(1)}, u32[]{:S(2)}, u32[]{:S(2)}) %collective-permute-start.11) | collective-permute-done | bytes 196640 | tf_op jit(solution)/shard_map/ppermute | solution.py:268
  65.7 0.1 fusion.8
  65.8 1.3 %collective-permute-done.14 = bf16[32,1792]{1,0:T(8,128)(2,1)S(1)} collective-permute-done((bf16[32,1792]{1,0:T(8,128)(2,1)S(1)}, bf16[32,1792]{1,0:T(8,128)(2,1)S(1)}, u32[]{:S(2)}, u32[]{:S(2)}) %collective-permute-start.14) | collective-permute-done | bytes 114720 | tf_op jit(solution)/shard_map/ppermute | solution.py:268
  67.1 0.1 multiply_convert_fusion.3
  67.2 1.3 %collective-permute-start.15 = (bf16[32,1792]{1,0:T(8,128)(2,1)S(1)}, bf16[32,1792]{1,0:T(8,128)(2,1)S(1)}, u32[]{:S(2)}, u32[]{:S(2)}) collective-permute-start(bf16[32,1792]{1,0:T(8,128)(2,1)S(1)} %multiply_convert_fusion.3), channel_id=1, source_target_pairs={{8,0},{12,4},{0,8},{4,12},{9,1},{13,5},{1,9},{5,13},{10,2},{14,6},... | collective-permute-start | bytes 344072 | tf_op jit(solution)/shard_map/ppermute | solution.py:265
  68.6 0.1 multiply_convert_fusion
  68.6 0.8 collective-permute-start.12
  69.5 0.1 fusion.16
  69.6 0.1 collective-permute-start.10
  69.7 0.5 collective-permute-start.8
  70.2 3.5 %fetch.1 = (bf16[16,128,1024]{2,1,0:T(8,128)(2,1)S(1)}, bf16[16,128,1024]{2,1,0:T(8,128)(2,1)S(1)}, f32[8,128]{1,0:T(8,128)S(1)}) custom-call(bf16[16,128,1024]{2,1,0:T(8,128)(2,1)} %keys_hbm, bf16[16,128,1024]{2,1,0:T(8,128)(2,1)} %values_hbm.1), custom_call_target="tpu_custom_call" | custom-call | tf_op jit(solution)/shard_map/fetch/pallas_call | solution.py:227
  73.7 0.1 collective-permute-start.16
  73.8 1.5 %collective-permute-done.12.refs_8_ = bf16[32,2816]{1,0:T(8,128)(2,1)S(1)} collective-permute-done((bf16[32,2816]{1,0:T(8,128)(2,1)S(1)}, bf16[32,2816]{1,0:T(8,128)(2,1)S(1)}, u32[]{:S(2)}, u32[]{:S(2)}) %collective-permute-start.12) | collective-permute-done | bytes 180256 | tf_op jit(solution)/shard_map/ppermute | solution.py:265
  75.3 0.0 collective-permute-start.13
  75.3 0.1 pad_add_fusion.refs_0_
  75.4 0.1 pad_maximum_fusion.2
  75.4 0.0 collective-permute-done.10.refs_7_
  75.4 0.0 collective-permute-done.8.refs_5_
  75.4 0.0 collective-permute-done.16.refs_11_
  75.4 1.2 %collective-permute-done.13.refs_9_ = bf16[32,2816]{1,0:T(8,128)(2,1)S(1)} collective-permute-done((bf16[32,2816]{1,0:T(8,128)(2,1)S(1)}, bf16[32,2816]{1,0:T(8,128)(2,1)S(1)}, u32[]{:S(2)}, u32[]{:S(2)}) %collective-permute-start.13) | collective-permute-done | bytes 180256 | tf_op jit(solution)/shard_map/ppermute | solution.py:265
  76.7 5.3 %attend.1 = (bf16[16,16384]{1,0:T(8,128)(2,1)}, bf16[16,2048]{1,0:T(8,128)(2,1)}) custom-call(s32[4]{0:T(128)S(1)} %pad_add_fusion.refs_0_, s32[16]{0:T(128)S(1)} %copy-done, f32[16,128]{1,0:T(8,128)S(1)} %get-tuple-element.99.refs_2_, f32[16,128]{1,0:T(8,128)S(1)} %get-tuple-element.100.refs_3_, bf16[32,2304]{1,0:T(8,128)(2,1)S(1)} %get-tuple-element.98.refs_4_, ...), custom_call_target="tpu_custom_call" | custom-call | tf_op jit(solution)/shard_map/attend/pallas_call | solution.py:192
  (17 shorter events, 0.2 us)
Async XLA Ops:
  0.6 3.8 %collective-permute-start = (bf16[64,4096]{1,0:T(8,128)(2,1)}, bf16[64,4096]{1,0:T(8,128)(2,1)S(1)}, u32[]{:S(2)}, u32[]{:S(2)}) collective-permute-start(bf16[64,4096]{1,0:T(8,128)(2,1)} %a0_ref.2), channel_id=1, source_target_pairs={{4,0},{0,4},{12,8},{8,12},{5,1},{1,5},{13,9},{9,13},{6,2},{2,6},{1... | collective-permute-start | bytes 1572872 | tf_op jit(solution)/shard_map/ppermute | solution.py:265
  1.1 22.1 %collective-permute-start.2 = (bf16[64,4096]{1,0:T(8,128)(2,1)}, bf16[64,4096]{1,0:T(8,128)(2,1)S(1)}, u32[]{:S(2)}, u32[]{:S(2)}) collective-permute-start(bf16[64,4096]{1,0:T(8,128)(2,1)} %a0_ref.2), channel_id=1, source_target_pairs={{8,0},{12,4},{0,8},{4,12},{9,1},{13,5},{1,9},{5,13},{10,2},{14,6},... | collective-permute-start | bytes 1572872 | tf_op jit(solution)/shard_map/ppermute | solution.py:265
  4.4 10.0 %copy-start = (s32[16]{0:T(128)S(1)}, s32[16]{0:T(128)}, u32[]{:S(2)}) copy-start(s32[16]{0:T(128)} %refs_1_.1) | copy-start | bytes 196
  12.8 10.5 %collective-permute-start.1 = (bf16[64,2560]{1,0:T(8,128)(2,1)S(1)}, bf16[64,2560]{1,0:T(8,128)(2,1)S(1)}, u32[]{:S(2)}, u32[]{:S(2)}) collective-permute-start(bf16[64,2560]{1,0:T(8,128)(2,1)S(1)} %get-tuple-element.43), channel_id=1, source_target_pairs={{0,1},{1,0},{2,3},{3,2},{4,5},{5,4},{6,7},{7,6},{8,9},{9,8},{10,11... | collective-permute-start | bytes 983048 | tf_op jit(solution)/shard_map/ppermute | solution.py:268
  22.7 13.4 %collective-permute-start.3 = (bf16[64,2304]{1,0:T(8,128)(2,1)S(1)}, bf16[64,2304]{1,0:T(8,128)(2,1)S(1)}, u32[]{:S(2)}, u32[]{:S(2)}) collective-permute-start(bf16[64,2304]{1,0:T(8,128)(2,1)S(1)} %get-tuple-element.50), channel_id=1, source_target_pairs={{0,1},{1,0},{2,3},{3,2},{4,5},{5,4},{6,7},{7,6},{8,9},{9,8},{10,11... | collective-permute-start | bytes 884744 | tf_op jit(solution)/shard_map/ppermute | solution.py:268
  23.2 2.8 %collective-permute-start.4 = (bf16[64,4096]{1,0:T(8,128)(2,1)S(1)}, bf16[64,4096]{1,0:T(8,128)(2,1)S(1)}, u32[]{:S(2)}, u32[]{:S(2)}) collective-permute-start(bf16[64,4096]{1,0:T(8,128)(2,1)S(1)} %collective-permute-done.2.a0_ref), channel_id=1, source_target_pairs={{4,0},{0,4},{12,8},{8,12},{5,1},{1,5},{13,9},{9,13},{6,2},{2,6},{1... | collective-permute-start | bytes 1572872 | tf_op jit(solution)/shard_map/ppermute | solution.py:265
  23.3 16.3 %collective-permute-start.5 = (bf16[32,2560]{1,0:T(8,128)(2,1)S(1)}, bf16[32,2560]{1,0:T(8,128)(2,1)S(1)}, u32[]{:S(2)}, u32[]{:S(2)}) collective-permute-start(bf16[32,2560]{1,0:T(8,128)(2,1)S(1)} %pad_maximum_fusion.1), channel_id=1, source_target_pairs={{0,2},{1,3},{2,0},{3,1},{4,6},{5,7},{6,4},{7,5},{8,10},{9,11},{10,... | collective-permute-start | bytes 491528 | tf_op jit(solution)/shard_map/ppermute | solution.py:268
  36.2 15.2 %collective-permute-start.6 = (bf16[64,3072]{1,0:T(8,128)(2,1)S(1)}, bf16[64,3072]{1,0:T(8,128)(2,1)S(1)}, u32[]{:S(2)}, u32[]{:S(2)}) collective-permute-start(bf16[64,3072]{1,0:T(8,128)(2,1)S(1)} %get-tuple-element.59), channel_id=1, source_target_pairs={{0,1},{1,0},{2,3},{3,2},{4,5},{5,4},{6,7},{7,6},{8,9},{9,8},{10,11... | collective-permute-start | bytes 1179656 | tf_op jit(solution)/shard_map/ppermute | solution.py:268
  37.8 12.6 %collective-permute-start.7 = (bf16[32,2304]{1,0:T(8,128)(2,1)S(1)}, bf16[32,2304]{1,0:T(8,128)(2,1)S(1)}, u32[]{:S(2)}, u32[]{:S(2)}) collective-permute-start(bf16[32,2304]{1,0:T(8,128)(2,1)S(1)} %add_convert_fusion.1), channel_id=1, source_target_pairs={{0,2},{1,3},{2,0},{3,1},{4,6},{5,7},{6,4},{7,5},{8,10},{9,11},{10,... | collective-permute-start | bytes 442376 | tf_op jit(solution)/shard_map/ppermute | solution.py:268
  47.4 11.1 %collective-permute-start.9 = (bf16[64,1792]{1,0:T(8,128)(2,1)S(1)}, bf16[64,1792]{1,0:T(8,128)(2,1)S(1)}, u32[]{:S(2)}, u32[]{:S(2)}) collective-permute-start(bf16[64,1792]{1,0:T(8,128)(2,1)S(1)} %get-tuple-element.67), channel_id=1, source_target_pairs={{0,1},{1,0},{2,3},{3,2},{4,5},{5,4},{6,7},{7,6},{8,9},{9,8},{10,11... | collective-permute-start | bytes 688136 | tf_op jit(solution)/shard_map/ppermute | solution.py:268
  51.4 14.3 %collective-permute-start.11 = (bf16[32,3072]{1,0:T(8,128)(2,1)S(1)}, bf16[32,3072]{1,0:T(8,128)(2,1)S(1)}, u32[]{:S(2)}, u32[]{:S(2)}) collective-permute-start(bf16[32,3072]{1,0:T(8,128)(2,1)S(1)} %pad_maximum_fusion), channel_id=1, source_target_pairs={{0,2},{1,3},{2,0},{3,1},{4,6},{5,7},{6,4},{7,5},{8,10},{9,11},{10,... | collective-permute-start | bytes 589832 | tf_op jit(solution)/shard_map/ppermute | solution.py:268
  58.5 8.6 %collective-permute-start.14 = (bf16[32,1792]{1,0:T(8,128)(2,1)S(1)}, bf16[32,1792]{1,0:T(8,128)(2,1)S(1)}, u32[]{:S(2)}, u32[]{:S(2)}) collective-permute-start(bf16[32,1792]{1,0:T(8,128)(2,1)S(1)} %add_convert_fusion.3), channel_id=1, source_target_pairs={{0,2},{1,3},{2,0},{3,1},{4,6},{5,7},{6,4},{7,5},{8,10},{9,11},{10,... | collective-permute-start | bytes 344072 | tf_op jit(solution)/shard_map/ppermute | solution.py:268
  67.2 6.4 %collective-permute-start.15 = (bf16[32,1792]{1,0:T(8,128)(2,1)S(1)}, bf16[32,1792]{1,0:T(8,128)(2,1)S(1)}, u32[]{:S(2)}, u32[]{:S(2)}) collective-permute-start(bf16[32,1792]{1,0:T(8,128)(2,1)S(1)} %multiply_convert_fusion.3), channel_id=1, source_target_pairs={{8,0},{12,4},{0,8},{4,12},{9,1},{13,5},{1,9},{5,13},{10,2},{14,6},... | collective-permute-start | bytes 344072 | tf_op jit(solution)/shard_map/ppermute | solution.py:265
  68.6 6.6 %collective-permute-start.12 = (bf16[32,2816]{1,0:T(8,128)(2,1)S(1)}, bf16[32,2816]{1,0:T(8,128)(2,1)S(1)}, u32[]{:S(2)}, u32[]{:S(2)}) collective-permute-start(bf16[32,2816]{1,0:T(8,128)(2,1)S(1)} %multiply_convert_fusion), channel_id=1, source_target_pairs={{8,0},{12,4},{0,8},{4,12},{9,1},{13,5},{1,9},{5,13},{10,2},{14,6},... | collective-permute-start | bytes 540680 | tf_op jit(solution)/shard_map/ppermute | solution.py:265
  69.6 5.9 %collective-permute-start.10 = (bf16[32,2304]{1,0:T(8,128)(2,1)S(1)}, bf16[32,2304]{1,0:T(8,128)(2,1)S(1)}, u32[]{:S(2)}, u32[]{:S(2)}) collective-permute-start(bf16[32,2304]{1,0:T(8,128)(2,1)S(1)} %get-tuple-element.70.refs_6_), channel_id=1, source_target_pairs={{4,0},{0,4},{12,8},{8,12},{5,1},{1,5},{13,9},{9,13},{6,2},{2,6},{1... | collective-permute-start | bytes 442376 | tf_op jit(solution)/shard_map/ppermute | solution.py:265
  69.7 5.8 %collective-permute-start.8 = (bf16[32,2304]{1,0:T(8,128)(2,1)S(1)}, bf16[32,2304]{1,0:T(8,128)(2,1)S(1)}, u32[]{:S(2)}, u32[]{:S(2)}) collective-permute-start(bf16[32,2304]{1,0:T(8,128)(2,1)S(1)} %get-tuple-element.98.refs_4_), channel_id=1, source_target_pairs={{4,0},{0,4},{12,8},{8,12},{5,1},{1,5},{13,9},{9,13},{6,2},{2,6},{1... | collective-permute-start | bytes 442376 | tf_op jit(solution)/shard_map/ppermute | solution.py:265
  73.7 1.8 %collective-permute-start.16 = (bf16[32,1792]{1,0:T(8,128)(2,1)S(1)}, bf16[32,1792]{1,0:T(8,128)(2,1)S(1)}, u32[]{:S(2)}, u32[]{:S(2)}) collective-permute-start(bf16[32,1792]{1,0:T(8,128)(2,1)S(1)} %collective-permute-done.15.refs_10_), channel_id=1, source_target_pairs={{4,0},{0,4},{12,8},{8,12},{5,1},{1,5},{13,9},{9,13},{6,2},{2,6},{1... | collective-permute-start | bytes 344072 | tf_op jit(solution)/shard_map/ppermute | solution.py:265
  75.3 1.4 %collective-permute-start.13 = (bf16[32,2816]{1,0:T(8,128)(2,1)S(1)}, bf16[32,2816]{1,0:T(8,128)(2,1)S(1)}, u32[]{:S(2)}, u32[]{:S(2)}) collective-permute-start(bf16[32,2816]{1,0:T(8,128)(2,1)S(1)} %collective-permute-done.12.refs_8_), channel_id=1, source_target_pairs={{4,0},{0,4},{12,8},{8,12},{5,1},{1,5},{13,9},{9,13},{6,2},{2,6},{1... | collective-permute-start | bytes 540680 | tf_op jit(solution)/shard_map/ppermute | solution.py:265

commit v7 on v6

--- a/solution.py
+++ b/solution.py
@@ -15,6 +15,8 @@
 GROUP = HEADS // KV_HEADS
 CORES = 2
 IN_FLIGHT = 3
+OWN_SHARE = 2 / 3
+OTHER_SHARE = 0.5
 
 norm_eps = 1e-05
 rope_base = 500000.0
@@ -278,20 +280,18 @@
 
     unit = HEAD_DIM * 2
     if width % unit == 0 and width >= 4 * unit:
-        cuts = {0: split_at(width, unit, 0.5), 1: split_at(width, unit, 0.6)}
+        own_cut, other_cut = split_at(width, unit, OWN_SHARE), split_at(width, unit, OTHER_SHARE)
     else:
-        cuts = {0: (width,), 1: (width,)}
-    plan = []
-    pieces = []
+        own_cut = other_cut = (width,)
+    units = [(0, 0, own_cut[0], True)]
+    for k in range(1, chips):
+        units.append((k, 0, other_cut[0], True))
+        units += [(k, other_cut[0], rest, False) for rest in other_cut[1:]]
+    units += [(0, own_cut[0], rest, False) for rest in own_cut[1:]]
 
     def tie(*arrays):
         return lax.optimization_barrier(arrays)
 
-    units = [
-        (k, sum(cuts[min(k, 1)][:c]), chunk, c == 0)
-        for k in range(chips)
-        for c, chunk in enumerate(cuts[min(k, 1)])
-    ]
     count = len(units)
     keeps, receiveds, owns, aways, arrived = [], [], [], [], []
 
@@ -322,15 +322,15 @@
         away = aways[u]
         arrived.append([on_z(away[(i - 1) * first_rows : i * first_rows], 2 * i) for i in range(1, kept)])
 
+    sides = {0: here[0]}
     for u, (k, first, chunk, squared) in enumerate(units):
         if u > 1:
             receiveds[u - 2], keeps[u - 1] = tie(receiveds[u - 2], keeps[u - 1])
-        if squared and k:
+        if k not in sides:
             array, keeps[u - 1] = tie(there[k - 1], keeps[u - 1])
-            a0, a1 = array, on_gx(array, 0, 1)
-        elif squared:
-            a0, a1 = here[0]
-        else:
+            sides[k] = (array, on_gx(array, 0, 1))
+        a0, a1 = sides[k]
+        if u:
             a0, keeps[u - 1] = tie(a0, keeps[u - 1])
         if u > 1:
             step_one(u - 2)
@@ -338,6 +338,7 @@
             step_two(u - 2)
         if u > 2:
             a0, arrived[u - 3] = tie(a0, arrived[u - 3])
+        sides[k] = (a0, a1)
         keep, send = project(z, a0, a1, gain, weight, rows, first, chunk, squared)
         keeps.append(keep)
         receiveds.append(on_z(send, 1))
@@ -358,33 +359,37 @@
         projecteds.append((total * scales[k]).astype(bf16))
 
     def hand_out(u):
-        k, first, chunk, squared = units[u]
-        projected = projecteds[u]
-        if k:
-            projected = on_gx(projected, chips - k, 0)
+        k, first, chunk, _ = units[u]
         plan.append((k * CORES, first, chunk, 0))
         plan.append((k * CORES + 1, first, chunk, rows))
-        return projected
-
-    for u in range(max(count - 2, 0), count):
-        if u + 1 < count and u:
-            receiveds[u], keeps[u + 1], arrived[u - 1] = tie(receiveds[u], keeps[u + 1], arrived[u - 1])
-        elif u:
-            *arrived[:], aways[u - 1] = tie(*arrived, aways[u - 1])
-            step_two(u - 1)
-            for before in range(u - 1):
-                finish(before)
-            if projecteds:
-                receiveds[u], projecteds[-1], aways[u - 1] = tie(receiveds[u], projecteds[-1], aways[u - 1])
+        held.append(on_gx(projecteds[u], chips - k, 0) if k else projecteds[u])
+
+    held = []
+    last = count - 1
+    if count > 1:
+        u = last - 1
+        if u:
+            receiveds[u], keeps[last], arrived[u - 1] = tie(receiveds[u], keeps[last], arrived[u - 1])
         step_one(u)
-    step_two(count - 1)
+        *arrived[:], aways[u] = tie(*arrived, aways[u])
+        step_two(u)
+        for before in range(u):
+            finish(before)
+            hand_out(before)
+        if u:
+            receiveds[last], projecteds[-1], aways[u] = tie(receiveds[last], projecteds[-1], aways[u])
+    step_one(last)
     if count > 1:
-        finish(count - 2)
-    finish(count - 1)
-    projecteds[-1], key_cache = tie(projecteds[-1], key_cache)
+        arrived[last - 1], aways[last] = tie(arrived[last - 1], aways[last])
+    step_two(last)
+    if count > 1:
+        finish(last - 1)
+        hand_out(last - 1)
+        projecteds[-1], key_cache = tie(projecteds[-1], key_cache)
     keys, values, fetched = fetch(in_hbm(key_cache), in_hbm(value_cache))
-    held = [hand_out(u) for u in range(count)]
-    held[-1], fetched = tie(held[-1], fetched)
+    *held[: last - 1], arrived[last], fetched = tie(*held[: last - 1], arrived[last], fetched)
+    finish(last)
+    hand_out(last)
     for projected in held:
         pieces.append(projected)
         pieces.append(on_gx(projected, 0, 1))

time: 82.2 us -> 80 us (0.973)
  waiting for transfers between devices: 18.4 us -> 13.5 us
  starting transfers between devices: 17.8 us -> 20.2 us
    ppermute x8, waiting for transfers between devices: 15.6 us -> 10.9 us  [on_z(): return lax.ppermute(array, 'gy', [(s, s ^ flip) for s in range(along_z)])]
    ppermute x8, starting transfers between devices: 11.8 us -> 13.6 us  [on_z(): return lax.ppermute(array, 'gy', [(s, s ^ flip) for s in range(along_z)])]
  transfers between devices with their start and end apart: 17 -> 17, of which waited for: 7 -> 7; matrix products, arithmetic and copies ran while one was open for 2% -> 2% of each run, Pallas kernels for 46% -> 48%
where the time goes in v7:
time: 80 us; the launch traced here: 79.8 us
  Pallas kernels  43.5 us (54%)
  starting transfers between devices  20.2 us (25%)
  waiting for transfers between devices  13.5 us (17%)
  other arithmetic  1.07 us (1%)
  between operations  0.82 us (1%)
    pallas_call x4, Pallas kernels, project(): pl.pallas_call(functools.partial(project_kernel, rows, kept, first, tiles...  34.7 us
    ppermute x8, starting transfers between devices, on_z(): return lax.ppermute(array, 'gy', [(s, s ^ flip) for s in range(along_z)])  13.6 us
    ppermute x8, waiting for transfers between devices, on_z(): return lax.ppermute(array, 'gy', [(s, s ^ flip) for s in range(along_z)])  10.9 us
    ppermute x9, starting transfers between devices, on_gx(): return lax.ppermute(array, 'gx', pairs)  6.61 us
    pallas_call x1, Pallas kernels, attend(): pl.pallas_call(functools.partial(attend_kernel, plan, rows, width // HEAD...  5.29 us
    pallas_call x1, Pallas kernels, fetch(): pl.pallas_call(fetch_kernel, out_shape=(shape, shape, jax.ShapeDtypeStruc...  3.49 us
    ppermute x9, waiting for transfers between devices, on_gx(): return lax.ppermute(array, 'gx', pairs)  2.66 us
  transfers between devices with their start and end apart: 17, of which 7 were waited for; matrix products, arithmetic and copies ran while one was open for 2% of the time, Pallas kernels for 48%

profile of v7, /device:TPU:0, one launch (start us, length us, event | category | flops | bytes accessed | tf_op | source)
XLA Modules:
  0.0 79.8 jit_solution(3311955497041719855)
XLA Ops:
  0.6 0.5 collective-permute-start.1
  1.1 2.6 %collective-permute-start = (bf16[64,4096]{1,0:T(8,128)(2,1)}, bf16[64,4096]{1,0:T(8,128)(2,1)S(1)}, u32[]{:S(2)}, u32[]{:S(2)}) collective-permute-start(bf16[64,4096]{1,0:T(8,128)(2,1)} %a0_ref.2), channel_id=1, source_target_pairs={{8,0},{12,4},{0,8},{4,12},{9,1},{13,5},{1,9},{5,13},{10,2},{14,6},... | collective-permute-start | bytes 1572872 | tf_op jit(solution)/shard_map/ppermute | solution.py:267
  3.7 0.7 reshape.17.gain_ref
  4.4 0.0 collective-permute-done.1.a1_ref
  4.4 0.0 copy-start
  4.4 10.2 %project.4 = (f32[64,3200]{1,0:T(8,128)S(1)}, bf16[64,3328]{1,0:T(8,128)(2,1)S(1)}) custom-call(s32[1]{0:T(128)} %bitcast.4.z_ref, bf16[64,4096]{1,0:T(8,128)(2,1)} %a0_ref.2, bf16[64,4096]{1,0:T(8,128)(2,1)S(1)} %collective-permute-done.1.a1_ref, bf16[1,4096]{1,0:T(2,128)(2,1)S(1)} %reshape.17.gain_ref, bf16[4096,4608]{1,0:T(8,128)(2,1)} %w_hbm.7), custom_call_target="tpu_custom_call" | custom-call | tf_op jit(solution)/shard_map/project/pallas_call | solution.py:94
  14.7 1.8 %collective-permute-done.a0_ref = bf16[64,4096]{1,0:T(8,128)(2,1)S(1)} collective-permute-done((bf16[64,4096]{1,0:T(8,128)(2,1)}, bf16[64,4096]{1,0:T(8,128)(2,1)S(1)}, u32[]{:S(2)}, u32[]{:S(2)}) %collective-permute-start) | collective-permute-done | bytes 524320 | tf_op jit(solution)/shard_map/ppermute | solution.py:267
  16.4 0.0 collective-permute-start.3
  16.5 1.9 %collective-permute-start.2 = (bf16[64,3328]{1,0:T(8,128)(2,1)S(1)}, bf16[64,3328]{1,0:T(8,128)(2,1)S(1)}, u32[]{:S(2)}, u32[]{:S(2)}) collective-permute-start(bf16[64,3328]{1,0:T(8,128)(2,1)S(1)} %get-tuple-element.46), channel_id=1, source_target_pairs={{0,1},{1,0},{2,3},{3,2},{4,5},{5,4},{6,7},{7,6},{8,9},{9,8},{10,11... | collective-permute-start | bytes 1277960 | tf_op jit(solution)/shard_map/ppermute | solution.py:270
  18.4 0.1 fusion.16
  18.5 0.1 pad_maximum_fusion.2
  18.6 0.0 collective-permute-done.3.a1_ref
  18.6 9.0 %project.5 = (f32[64,2432]{1,0:T(8,128)S(1)}, bf16[64,2560]{1,0:T(8,128)(2,1)S(1)}) custom-call(s32[1]{0:T(128)} %bitcast.4.z_ref, bf16[64,4096]{1,0:T(8,128)(2,1)S(1)} %collective-permute-done.a0_ref, bf16[64,4096]{1,0:T(8,128)(2,1)S(1)} %collective-permute-done.3.a1_ref, bf16[1,4096]{1,0:T(2,128)(2,1)S(1)} %reshape.17.gain_ref, bf16[4096,4608]{1,0:T(8,128)(2,1)} %w_hbm.7), custom_call_target="tpu_custom_call" | custom-call | tf_op jit(solution)/shard_map/project/pallas_call | solution.py:94
  27.6 1.2 %collective-permute-done.2 = bf16[64,3328]{1,0:T(8,128)(2,1)S(1)} collective-permute-done((bf16[64,3328]{1,0:T(8,128)(2,1)S(1)}, bf16[64,3328]{1,0:T(8,128)(2,1)S(1)}, u32[]{:S(2)}, u32[]{:S(2)}) %collective-permute-start.2) | collective-permute-done | bytes 426016 | tf_op jit(solution)/shard_map/ppermute | solution.py:270
  28.8 1.8 %collective-permute-start.4 = (bf16[64,2560]{1,0:T(8,128)(2,1)S(1)}, bf16[64,2560]{1,0:T(8,128)(2,1)S(1)}, u32[]{:S(2)}, u32[]{:S(2)}) collective-permute-start(bf16[64,2560]{1,0:T(8,128)(2,1)S(1)} %get-tuple-element.51), channel_id=1, source_target_pairs={{0,1},{1,0},{2,3},{3,2},{4,5},{5,4},{6,7},{7,6},{8,9},{9,8},{10,11... | collective-permute-start | bytes 983048 | tf_op jit(solution)/shard_map/ppermute | solution.py:270
  30.7 2.7 %collective-permute-start.5 = (bf16[32,3328]{1,0:T(8,128)(2,1)S(1)}, bf16[32,3328]{1,0:T(8,128)(2,1)S(1)}, u32[]{:S(2)}, u32[]{:S(2)}) collective-permute-start(bf16[32,3328]{1,0:T(8,128)(2,1)S(1)} %pad_maximum_fusion), channel_id=1, source_target_pairs={{0,2},{1,3},{2,0},{3,1},{4,6},{5,7},{6,4},{7,5},{8,10},{9,11},{10,... | collective-permute-start | bytes 638984 | tf_op jit(solution)/shard_map/ppermute | solution.py:270
  33.3 8.9 %project.6 = (f32[64,2304]{1,0:T(8,128)S(1)}, bf16[64,2304]{1,0:T(8,128)(2,1)S(1)}) custom-call(s32[1]{0:T(128)} %bitcast.4.z_ref, bf16[64,4096]{1,0:T(8,128)(2,1)S(1)} %collective-permute-done.a0_ref, bf16[64,4096]{1,0:T(8,128)(2,1)S(1)} %collective-permute-done.3.a1_ref, bf16[1,4096]{1,0:T(2,128)(2,1)S(1)} %reshape.17.gain_ref, bf16[4096,4608]{1,0:T(8,128)(2,1)} %w_hbm.7), custom_call_target="tpu_custom_call" | custom-call | tf_op jit(solution)/shard_map/project/pallas_call | solution.py:94
  42.3 0.5 collective-permute-start.6
  42.8 0.1 collective-permute-done.4
  42.9 0.0 collective-permute-done.5
  42.9 3.1 %collective-permute-start.7 = (bf16[32,2560]{1,0:T(8,128)(2,1)S(1)}, bf16[32,2560]{1,0:T(8,128)(2,1)S(1)}, u32[]{:S(2)}, u32[]{:S(2)}) collective-permute-start(bf16[32,2560]{1,0:T(8,128)(2,1)S(1)} %pad_maximum_fusion.1), channel_id=1, source_target_pairs={{0,2},{1,3},{2,0},{3,1},{4,6},{5,7},{6,4},{7,5},{8,10},{9,11},{10,... | collective-permute-start | bytes 491528 | tf_op jit(solution)/shard_map/ppermute | solution.py:270
  46.0 6.6 %project.7 = (f32[64,1536]{1,0:T(8,128)S(1)}, bf16[64,1536]{1,0:T(8,128)(2,1)S(1)}) custom-call(s32[1]{0:T(128)} %bitcast.4.z_ref, bf16[64,4096]{1,0:T(8,128)(2,1)} %a0_ref.2, bf16[64,4096]{1,0:T(8,128)(2,1)S(1)} %collective-permute-done.1.a1_ref, bf16[1,4096]{1,0:T(2,128)(2,1)S(1)} %reshape.17.gain_ref, bf16[4096,4608]{1,0:T(8,128)(2,1)} %w_hbm.7), custom_call_target="tpu_custom_call" | custom-call | tf_op jit(solution)/shard_map/project/pallas_call | solution.py:94
  52.6 2.5 %collective-permute-start.10 = (bf16[64,1536]{1,0:T(8,128)(2,1)S(1)}, bf16[64,1536]{1,0:T(8,128)(2,1)S(1)}, u32[]{:S(2)}, u32[]{:S(2)}) collective-permute-start(bf16[64,1536]{1,0:T(8,128)(2,1)S(1)} %get-tuple-element.74), channel_id=1, source_target_pairs={{0,1},{1,0},{2,3},{3,2},{4,5},{5,4},{6,7},{7,6},{8,9},{9,8},{10,11... | collective-permute-start | bytes 589832 | tf_op jit(solution)/shard_map/ppermute | solution.py:270
  55.2 0.0 collective-permute-done.6
  55.2 0.0 collective-permute-done.7
  55.2 0.1 fusion.8
  55.3 0.1 multiply_convert_fusion.2
  55.5 1.6 %collective-permute-start.8 = (bf16[32,2304]{1,0:T(8,128)(2,1)S(1)}, bf16[32,2304]{1,0:T(8,128)(2,1)S(1)}, u32[]{:S(2)}, u32[]{:S(2)}) collective-permute-start(bf16[32,2304]{1,0:T(8,128)(2,1)S(1)} %multiply_convert_fusion.2), channel_id=1, source_target_pairs={{8,0},{12,4},{0,8},{4,12},{9,1},{13,5},{1,9},{5,13},{10,2},{14,6},... | collective-permute-start | bytes 442376 | tf_op jit(solution)/shard_map/ppermute | solution.py:267
  57.0 1.0 %collective-permute-start.9 = (bf16[32,2304]{1,0:T(8,128)(2,1)S(1)}, bf16[32,2304]{1,0:T(8,128)(2,1)S(1)}, u32[]{:S(2)}, u32[]{:S(2)}) collective-permute-start(bf16[32,2304]{1,0:T(8,128)(2,1)S(1)} %add_convert_fusion.1), channel_id=1, source_target_pairs={{0,2},{1,3},{2,0},{3,1},{4,6},{5,7},{6,4},{7,5},{8,10},{9,11},{10,... | collective-permute-start | bytes 442376 | tf_op jit(solution)/shard_map/ppermute | solution.py:270
  58.0 0.1 fusion.15
  58.1 2.3 %collective-permute-done.10 = bf16[64,1536]{1,0:T(8,128)(2,1)S(1)} collective-permute-done((bf16[64,1536]{1,0:T(8,128)(2,1)S(1)}, bf16[64,1536]{1,0:T(8,128)(2,1)S(1)}, u32[]{:S(2)}, u32[]{:S(2)}) %collective-permute-start.10) | collective-permute-done | bytes 196640 | tf_op jit(solution)/shard_map/ppermute | solution.py:270
  60.4 6.3 %collective-permute-done.9 = bf16[32,2304]{1,0:T(8,128)(2,1)S(1)} collective-permute-done((bf16[32,2304]{1,0:T(8,128)(2,1)S(1)}, bf16[32,2304]{1,0:T(8,128)(2,1)S(1)}, u32[]{:S(2)}, u32[]{:S(2)}) %collective-permute-start.9) | collective-permute-done | bytes 147488 | tf_op jit(solution)/shard_map/ppermute | solution.py:270
  66.7 0.1 multiply_convert_fusion.1
  66.8 0.1 collective-permute-start.11
  66.9 0.9 %collective-permute-start.14 = (bf16[32,2304]{1,0:T(8,128)(2,1)S(1)}, bf16[32,2304]{1,0:T(8,128)(2,1)S(1)}, u32[]{:S(2)}, u32[]{:S(2)}) collective-permute-start(bf16[32,2304]{1,0:T(8,128)(2,1)S(1)} %multiply_convert_fusion.1), channel_id=1, source_target_pairs={{8,0},{12,4},{0,8},{4,12},{9,1},{13,5},{1,9},{5,13},{10,2},{14,6},... | collective-permute-start | bytes 442376 | tf_op jit(solution)/shard_map/ppermute | solution.py:267
  67.8 0.1 multiply_convert_fusion.refs_4_
  67.9 3.5 %fetch.1 = (bf16[16,128,1024]{2,1,0:T(8,128)(2,1)S(1)}, bf16[16,128,1024]{2,1,0:T(8,128)(2,1)S(1)}, f32[8,128]{1,0:T(8,128)S(1)}) custom-call(bf16[16,128,1024]{2,1,0:T(8,128)(2,1)} %keys_hbm, bf16[16,128,1024]{2,1,0:T(8,128)(2,1)} %values_hbm.1), custom_call_target="tpu_custom_call" | custom-call | tf_op jit(solution)/shard_map/fetch/pallas_call | solution.py:229
  71.4 0.0 collective-permute-done.8.refs_6_
  71.4 1.0 %collective-permute-done.11 = bf16[32,1536]{1,0:T(8,128)(2,1)S(1)} collective-permute-done((bf16[32,1536]{1,0:T(8,128)(2,1)S(1)}, bf16[32,1536]{1,0:T(8,128)(2,1)S(1)}, u32[]{:S(2)}, u32[]{:S(2)}) %collective-permute-start.11) | collective-permute-done | bytes 98336 | tf_op jit(solution)/shard_map/ppermute | solution.py:270
  72.4 0.0 collective-permute-start.13
  72.4 0.5 collective-permute-start.12
  72.9 0.0 collective-permute-done.14.refs_8_
  72.9 0.0 collective-permute-start.15
  72.9 0.1 multiply_convert_fusion.3.refs_10_
  73.0 0.6 collective-permute-start.16
  73.6 0.1 pad_add_fusion.refs_0_
  73.6 0.9 %collective-permute-done.16.refs_11_ = bf16[32,1536]{1,0:T(8,128)(2,1)S(1)} collective-permute-done((bf16[32,1536]{1,0:T(8,128)(2,1)S(1)}, bf16[32,1536]{1,0:T(8,128)(2,1)S(1)}, u32[]{:S(2)}, u32[]{:S(2)}) %collective-permute-start.16) | collective-permute-done | bytes 98336 | tf_op jit(solution)/shard_map/ppermute | solution.py:267
  74.5 5.3 %attend.1 = (bf16[16,16384]{1,0:T(8,128)(2,1)}, bf16[16,2048]{1,0:T(8,128)(2,1)}) custom-call(s32[4]{0:T(128)S(1)} %pad_add_fusion.refs_0_, s32[16]{0:T(128)S(1)} %copy-done, f32[16,128]{1,0:T(8,128)S(1)} %get-tuple-element.103.refs_2_, f32[16,128]{1,0:T(8,128)S(1)} %get-tuple-element.104.refs_3_, bf16[32,3072]{1,0:T(8,128)(2,1)S(1)} %multiply_convert_fusion.refs_4_, ...), custom_call_target="tpu_custom_call" | custom-call | tf_op jit(solution)/shard_map/attend/pallas_call | solution.py:194
  (18 shorter events, 0.2 us)
Async XLA Ops:
  0.6 3.8 %collective-permute-start.1 = (bf16[64,4096]{1,0:T(8,128)(2,1)}, bf16[64,4096]{1,0:T(8,128)(2,1)S(1)}, u32[]{:S(2)}, u32[]{:S(2)}) collective-permute-start(bf16[64,4096]{1,0:T(8,128)(2,1)} %a0_ref.2), channel_id=1, source_target_pairs={{4,0},{0,4},{12,8},{8,12},{5,1},{1,5},{13,9},{9,13},{6,2},{2,6},{1... | collective-permute-start | bytes 1572872 | tf_op jit(solution)/shard_map/ppermute | solution.py:267
  1.1 15.3 %collective-permute-start = (bf16[64,4096]{1,0:T(8,128)(2,1)}, bf16[64,4096]{1,0:T(8,128)(2,1)S(1)}, u32[]{:S(2)}, u32[]{:S(2)}) collective-permute-start(bf16[64,4096]{1,0:T(8,128)(2,1)} %a0_ref.2), channel_id=1, source_target_pairs={{8,0},{12,4},{0,8},{4,12},{9,1},{13,5},{1,9},{5,13},{10,2},{14,6},... | collective-permute-start | bytes 1572872 | tf_op jit(solution)/shard_map/ppermute | solution.py:267
  4.4 12.0 %copy-start = (s32[16]{0:T(128)S(1)}, s32[16]{0:T(128)}, u32[]{:S(2)}) copy-start(s32[16]{0:T(128)} %refs_1_.1) | copy-start | bytes 196
  16.4 2.1 %collective-permute-start.3 = (bf16[64,4096]{1,0:T(8,128)(2,1)S(1)}, bf16[64,4096]{1,0:T(8,128)(2,1)S(1)}, u32[]{:S(2)}, u32[]{:S(2)}) collective-permute-start(bf16[64,4096]{1,0:T(8,128)(2,1)S(1)} %collective-permute-done.a0_ref), channel_id=1, source_target_pairs={{4,0},{0,4},{12,8},{8,12},{5,1},{1,5},{13,9},{9,13},{6,2},{2,6},{1... | collective-permute-start | bytes 1572872 | tf_op jit(solution)/shard_map/ppermute | solution.py:267
  16.5 12.3 %collective-permute-start.2 = (bf16[64,3328]{1,0:T(8,128)(2,1)S(1)}, bf16[64,3328]{1,0:T(8,128)(2,1)S(1)}, u32[]{:S(2)}, u32[]{:S(2)}) collective-permute-start(bf16[64,3328]{1,0:T(8,128)(2,1)S(1)} %get-tuple-element.46), channel_id=1, source_target_pairs={{0,1},{1,0},{2,3},{3,2},{4,5},{5,4},{6,7},{7,6},{8,9},{9,8},{10,11... | collective-permute-start | bytes 1277960 | tf_op jit(solution)/shard_map/ppermute | solution.py:270
  28.8 14.0 %collective-permute-start.4 = (bf16[64,2560]{1,0:T(8,128)(2,1)S(1)}, bf16[64,2560]{1,0:T(8,128)(2,1)S(1)}, u32[]{:S(2)}, u32[]{:S(2)}) collective-permute-start(bf16[64,2560]{1,0:T(8,128)(2,1)S(1)} %get-tuple-element.51), channel_id=1, source_target_pairs={{0,1},{1,0},{2,3},{3,2},{4,5},{5,4},{6,7},{7,6},{8,9},{9,8},{10,11... | collective-permute-start | bytes 983048 | tf_op jit(solution)/shard_map/ppermute | solution.py:270
  30.7 12.3 %collective-permute-start.5 = (bf16[32,3328]{1,0:T(8,128)(2,1)S(1)}, bf16[32,3328]{1,0:T(8,128)(2,1)S(1)}, u32[]{:S(2)}, u32[]{:S(2)}) collective-permute-start(bf16[32,3328]{1,0:T(8,128)(2,1)S(1)} %pad_maximum_fusion), channel_id=1, source_target_pairs={{0,2},{1,3},{2,0},{3,1},{4,6},{5,7},{6,4},{7,5},{8,10},{9,11},{10,... | collective-permute-start | bytes 638984 | tf_op jit(solution)/shard_map/ppermute | solution.py:270
  42.3 12.9 %collective-permute-start.6 = (bf16[64,2304]{1,0:T(8,128)(2,1)S(1)}, bf16[64,2304]{1,0:T(8,128)(2,1)S(1)}, u32[]{:S(2)}, u32[]{:S(2)}) collective-permute-start(bf16[64,2304]{1,0:T(8,128)(2,1)S(1)} %get-tuple-element.63), channel_id=1, source_target_pairs={{0,1},{1,0},{2,3},{3,2},{4,5},{5,4},{6,7},{7,6},{8,9},{9,8},{10,11... | collective-permute-start | bytes 884744 | tf_op jit(solution)/shard_map/ppermute | solution.py:270
  42.9 12.2 %collective-permute-start.7 = (bf16[32,2560]{1,0:T(8,128)(2,1)S(1)}, bf16[32,2560]{1,0:T(8,128)(2,1)S(1)}, u32[]{:S(2)}, u32[]{:S(2)}) collective-permute-start(bf16[32,2560]{1,0:T(8,128)(2,1)S(1)} %pad_maximum_fusion.1), channel_id=1, source_target_pairs={{0,2},{1,3},{2,0},{3,1},{4,6},{5,7},{6,4},{7,5},{8,10},{9,11},{10,... | collective-permute-start | bytes 491528 | tf_op jit(solution)/shard_map/ppermute | solution.py:270
  52.6 7.8 %collective-permute-start.10 = (bf16[64,1536]{1,0:T(8,128)(2,1)S(1)}, bf16[64,1536]{1,0:T(8,128)(2,1)S(1)}, u32[]{:S(2)}, u32[]{:S(2)}) collective-permute-start(bf16[64,1536]{1,0:T(8,128)(2,1)S(1)} %get-tuple-element.74), channel_id=1, source_target_pairs={{0,1},{1,0},{2,3},{3,2},{4,5},{5,4},{6,7},{7,6},{8,9},{9,8},{10,11... | collective-permute-start | bytes 589832 | tf_op jit(solution)/shard_map/ppermute | solution.py:270
  55.5 15.9 %collective-permute-start.8 = (bf16[32,2304]{1,0:T(8,128)(2,1)S(1)}, bf16[32,2304]{1,0:T(8,128)(2,1)S(1)}, u32[]{:S(2)}, u32[]{:S(2)}) collective-permute-start(bf16[32,2304]{1,0:T(8,128)(2,1)S(1)} %multiply_convert_fusion.2), channel_id=1, source_target_pairs={{8,0},{12,4},{0,8},{4,12},{9,1},{13,5},{1,9},{5,13},{10,2},{14,6},... | collective-permute-start | bytes 442376 | tf_op jit(solution)/shard_map/ppermute | solution.py:267
  57.0 9.7 %collective-permute-start.9 = (bf16[32,2304]{1,0:T(8,128)(2,1)S(1)}, bf16[32,2304]{1,0:T(8,128)(2,1)S(1)}, u32[]{:S(2)}, u32[]{:S(2)}) collective-permute-start(bf16[32,2304]{1,0:T(8,128)(2,1)S(1)} %add_convert_fusion.1), channel_id=1, source_target_pairs={{0,2},{1,3},{2,0},{3,1},{4,6},{5,7},{6,4},{7,5},{8,10},{9,11},{10,... | collective-permute-start | bytes 442376 | tf_op jit(solution)/shard_map/ppermute | solution.py:270
  66.8 5.6 %collective-permute-start.11 = (bf16[32,1536]{1,0:T(8,128)(2,1)S(1)}, bf16[32,1536]{1,0:T(8,128)(2,1)S(1)}, u32[]{:S(2)}, u32[]{:S(2)}) collective-permute-start(bf16[32,1536]{1,0:T(8,128)(2,1)S(1)} %add_convert_fusion.3), channel_id=1, source_target_pairs={{0,2},{1,3},{2,0},{3,1},{4,6},{5,7},{6,4},{7,5},{8,10},{9,11},{10,... | collective-permute-start | bytes 294920 | tf_op jit(solution)/shard_map/ppermute | solution.py:270
  66.9 6.0 %collective-permute-start.14 = (bf16[32,2304]{1,0:T(8,128)(2,1)S(1)}, bf16[32,2304]{1,0:T(8,128)(2,1)S(1)}, u32[]{:S(2)}, u32[]{:S(2)}) collective-permute-start(bf16[32,2304]{1,0:T(8,128)(2,1)S(1)} %multiply_convert_fusion.1), channel_id=1, source_target_pairs={{8,0},{12,4},{0,8},{4,12},{9,1},{13,5},{1,9},{5,13},{10,2},{14,6},... | collective-permute-start | bytes 442376 | tf_op jit(solution)/shard_map/ppermute | solution.py:267
  72.4 2.1 %collective-permute-start.13 = (bf16[32,2304]{1,0:T(8,128)(2,1)S(1)}, bf16[32,2304]{1,0:T(8,128)(2,1)S(1)}, u32[]{:S(2)}, u32[]{:S(2)}) collective-permute-start(bf16[32,2304]{1,0:T(8,128)(2,1)S(1)} %collective-permute-done.8.refs_6_), channel_id=1, source_target_pairs={{4,0},{0,4},{12,8},{8,12},{5,1},{1,5},{13,9},{9,13},{6,2},{2,6},{1... | collective-permute-start | bytes 442376 | tf_op jit(solution)/shard_map/ppermute | solution.py:267
  72.4 2.1 %collective-permute-start.12 = (bf16[32,3072]{1,0:T(8,128)(2,1)S(1)}, bf16[32,3072]{1,0:T(8,128)(2,1)S(1)}, u32[]{:S(2)}, u32[]{:S(2)}) collective-permute-start(bf16[32,3072]{1,0:T(8,128)(2,1)S(1)} %multiply_convert_fusion.refs_4_), channel_id=1, source_target_pairs={{4,0},{0,4},{12,8},{8,12},{5,1},{1,5},{13,9},{9,13},{6,2},{2,6},{1... | collective-permute-start | bytes 589832 | tf_op jit(solution)/shard_map/ppermute | solution.py:267
  72.9 1.6 %collective-permute-start.15 = (bf16[32,2304]{1,0:T(8,128)(2,1)S(1)}, bf16[32,2304]{1,0:T(8,128)(2,1)S(1)}, u32[]{:S(2)}, u32[]{:S(2)}) collective-permute-start(bf16[32,2304]{1,0:T(8,128)(2,1)S(1)} %collective-permute-done.14.refs_8_), channel_id=1, source_target_pairs={{4,0},{0,4},{12,8},{8,12},{5,1},{1,5},{13,9},{9,13},{6,2},{2,6},{1... | collective-permute-start | bytes 442376 | tf_op jit(solution)/shard_map/ppermute | solution.py:267
  73.0 1.5 %collective-permute-start.16 = (bf16[32,1536]{1,0:T(8,128)(2,1)S(1)}, bf16[32,1536]{1,0:T(8,128)(2,1)S(1)}, u32[]{:S(2)}, u32[]{:S(2)}) collective-permute-start(bf16[32,1536]{1,0:T(8,128)(2,1)S(1)} %multiply_convert_fusion.3.refs_10_), channel_id=1, source_target_pairs={{4,0},{0,4},{12,8},{8,12},{5,1},{1,5},{13,9},{9,13},{6,2},{2,6},{1... | collective-permute-start | bytes 294920 | tf_op jit(solution)/shard_map/ppermute | solution.py:267

commit v8 on v7

--- a/solution.py
+++ b/solution.py
@@ -15,7 +15,7 @@
 GROUP = HEADS // KV_HEADS
 CORES = 2
 IN_FLIGHT = 3
-OWN_SHARE = 2 / 3
+OWN_SHARE = 0.56
 OTHER_SHARE = 0.5
 
 norm_eps = 1e-05
@@ -138,10 +138,13 @@
 
     def score(r):
         query = heads[pl.ds(r, HEADS, stride=rows), :].astype(bf16)
-        for k in range(KV_HEADS):
-            scores_ref[r, pl.ds(k * GROUP, GROUP), :] = lax.dot_general(
-                query[k * GROUP : (k + 1) * GROUP],
-                keys[r, :, pl.ds(k * HEAD_DIM, HEAD_DIM)],
+        empty = jnp.zeros((GROUP, HEAD_DIM), bf16)
+        for k in range(0, KV_HEADS, 2):
+            front = jnp.concatenate([query[k * GROUP : (k + 1) * GROUP], empty], axis=1)
+            second = jnp.concatenate([empty, query[(k + 1) * GROUP : (k + 2) * GROUP]], axis=1)
+            scores_ref[r, pl.ds(k * GROUP, 2 * GROUP), :] = lax.dot_general(
+                jnp.concatenate([front, second], axis=0),
+                keys[r, :, pl.ds(k * HEAD_DIM, 2 * HEAD_DIM)],
                 (((1,), (1,)), ((), ())),
                 preferred_element_type=f32,
             )
@@ -167,15 +170,17 @@
         scores_ref[r] = own_weight * spread
 
     def mix(r):
-        for k in range(KV_HEADS):
-            mixed[pl.ds(k * GROUP * rows + r, GROUP, stride=rows), :] = (
-                jnp.dot(
-                    weights_ref[r, pl.ds(k * GROUP, GROUP), :],
-                    values[r, :, pl.ds(k * HEAD_DIM, HEAD_DIM)],
-                    preferred_element_type=f32,
+        for k in range(0, KV_HEADS, 2):
+            both = jnp.dot(
+                weights_ref[r, pl.ds(k * GROUP, 2 * GROUP), :],
+                values[r, :, pl.ds(k * HEAD_DIM, 2 * HEAD_DIM)],
+                preferred_element_type=f32,
+            )
+            for i in range(2):
+                mixed[pl.ds((k + i) * GROUP * rows + r, GROUP, stride=rows), :] = (
+                    both[i * GROUP : (i + 1) * GROUP, i * HEAD_DIM : (i + 1) * HEAD_DIM]
+                    + scores_ref[r, pl.ds((k + i) * GROUP, GROUP), :]
                 )
-                + scores_ref[r, pl.ds(k * GROUP, GROUP), :]
-            )
 
     for r in range(rows):
         score(r)

time: 80 us -> 77 us (0.963)
  waiting for transfers between devices: 13.5 us -> 10.9 us
  Pallas kernels: 43.5 us -> 42.6 us
    ppermute x8, waiting for transfers between devices: 10.9 us -> 7.01 us  [on_z(): return lax.ppermute(array, 'gy', [(s, s ^ flip) for s in range(along_z)])]
    ppermute x9, waiting for transfers between devices: 2.66 us -> 3.91 us  [on_gx(): return lax.ppermute(array, 'gx', pairs)]
    pallas_call x1, Pallas kernels: 5.29 us -> 4.42 us  [attend(): pl.pallas_call(functools.partial(attend_kernel, plan, rows, width // HEAD...]
  transfers between devices with their start and end apart: 17 -> 17, of which waited for: 7 -> 7; matrix products, arithmetic and copies ran while one was open for 2% -> 2% of each run, Pallas kernels for 48% -> 50%
where the time goes in v8:
time: 77 us; the launch traced here: 76.8 us
  Pallas kernels  42.6 us (55%)
  starting transfers between devices  20.6 us (27%)
  waiting for transfers between devices  10.9 us (14%)
  other arithmetic  1.08 us (1%)
  between operations  0.83 us (1%)
    pallas_call x4, Pallas kernels, project(): pl.pallas_call(functools.partial(project_kernel, rows, kept, first, tiles...  34.7 us
    ppermute x8, starting transfers between devices, on_z(): return lax.ppermute(array, 'gy', [(s, s ^ flip) for s in range(along_z)])  13.3 us
    ppermute x9, starting transfers between devices, on_gx(): return lax.ppermute(array, 'gx', pairs)  7.31 us
    ppermute x8, waiting for transfers between devices, on_z(): return lax.ppermute(array, 'gy', [(s, s ^ flip) for s in range(along_z)])  7.01 us
    pallas_call x1, Pallas kernels, attend(): pl.pallas_call(functools.partial(attend_kernel, plan, rows, width // HEAD...  4.42 us
    ppermute x9, waiting for transfers between devices, on_gx(): return lax.ppermute(array, 'gx', pairs)  3.91 us
    pallas_call x1, Pallas kernels, fetch(): pl.pallas_call(fetch_kernel, out_shape=(shape, shape, jax.ShapeDtypeStruc...  3.48 us
  transfers between devices with their start and end apart: 17, of which 7 were waited for; matrix products, arithmetic and copies ran while one was open for 2% of the time, Pallas kernels for 50%

profile of v8, /device:TPU:0, one launch (start us, length us, event | category | flops | bytes accessed | tf_op | source)
XLA Modules:
  0.0 76.8 jit_solution(4926841116075677187)
XLA Ops:
  0.6 0.5 collective-permute-start.1
  1.1 2.6 %collective-permute-start = (bf16[64,4096]{1,0:T(8,128)(2,1)}, bf16[64,4096]{1,0:T(8,128)(2,1)S(1)}, u32[]{:S(2)}, u32[]{:S(2)}) collective-permute-start(bf16[64,4096]{1,0:T(8,128)(2,1)} %a0_ref.2), channel_id=1, source_target_pairs={{8,0},{12,4},{0,8},{4,12},{9,1},{13,5},{1,9},{5,13},{10,2},{14,6},... | collective-permute-start | bytes 1572872 | tf_op jit(solution)/shard_map/ppermute | solution.py:272
  3.7 0.7 reshape.17.gain_ref
  4.4 0.0 collective-permute-done.1.a1_ref
  4.4 0.0 copy-start
  4.4 9.0 %project.4 = (f32[64,2688]{1,0:T(8,128)S(1)}, bf16[64,2816]{1,0:T(8,128)(2,1)S(1)}) custom-call(s32[1]{0:T(128)} %bitcast.4.z_ref, bf16[64,4096]{1,0:T(8,128)(2,1)} %a0_ref.2, bf16[64,4096]{1,0:T(8,128)(2,1)S(1)} %collective-permute-done.1.a1_ref, bf16[1,4096]{1,0:T(2,128)(2,1)S(1)} %reshape.17.gain_ref, bf16[4096,4608]{1,0:T(8,128)(2,1)} %w_hbm.7), custom_call_target="tpu_custom_call" | custom-call | tf_op jit(solution)/shard_map/project/pallas_call | solution.py:94
  13.5 3.0 %collective-permute-done.a0_ref = bf16[64,4096]{1,0:T(8,128)(2,1)S(1)} collective-permute-done((bf16[64,4096]{1,0:T(8,128)(2,1)}, bf16[64,4096]{1,0:T(8,128)(2,1)S(1)}, u32[]{:S(2)}, u32[]{:S(2)}) %collective-permute-start) | collective-permute-done | bytes 524320 | tf_op jit(solution)/shard_map/ppermute | solution.py:272
  16.4 0.0 collective-permute-start.3
  16.4 1.8 %collective-permute-start.2 = (bf16[64,2816]{1,0:T(8,128)(2,1)S(1)}, bf16[64,2816]{1,0:T(8,128)(2,1)S(1)}, u32[]{:S(2)}, u32[]{:S(2)}) collective-permute-start(bf16[64,2816]{1,0:T(8,128)(2,1)S(1)} %get-tuple-element.46), channel_id=1, source_target_pairs={{0,1},{1,0},{2,3},{3,2},{4,5},{5,4},{6,7},{7,6},{8,9},{9,8},{10,11... | collective-permute-start | bytes 1081352 | tf_op jit(solution)/shard_map/ppermute | solution.py:275
  18.3 0.1 fusion.16
  18.4 0.0 collective-permute-done.3.a1_ref
  18.4 9.0 %project.5 = (f32[64,2432]{1,0:T(8,128)S(1)}, bf16[64,2560]{1,0:T(8,128)(2,1)S(1)}) custom-call(s32[1]{0:T(128)} %bitcast.4.z_ref, bf16[64,4096]{1,0:T(8,128)(2,1)S(1)} %collective-permute-done.a0_ref, bf16[64,4096]{1,0:T(8,128)(2,1)S(1)} %collective-permute-done.3.a1_ref, bf16[1,4096]{1,0:T(2,128)(2,1)S(1)} %reshape.17.gain_ref, bf16[4096,4608]{1,0:T(8,128)(2,1)} %w_hbm.7), custom_call_target="tpu_custom_call" | custom-call | tf_op jit(solution)/shard_map/project/pallas_call | solution.py:94
  27.4 0.0 collective-permute-done.2
  27.5 1.8 %collective-permute-start.4 = (bf16[64,2560]{1,0:T(8,128)(2,1)S(1)}, bf16[64,2560]{1,0:T(8,128)(2,1)S(1)}, u32[]{:S(2)}, u32[]{:S(2)}) collective-permute-start(bf16[64,2560]{1,0:T(8,128)(2,1)S(1)} %get-tuple-element.51), channel_id=1, source_target_pairs={{0,1},{1,0},{2,3},{3,2},{4,5},{5,4},{6,7},{7,6},{8,9},{9,8},{10,11... | collective-permute-start | bytes 983048 | tf_op jit(solution)/shard_map/ppermute | solution.py:275
  29.3 2.7 %collective-permute-start.5 = (bf16[32,2816]{1,0:T(8,128)(2,1)S(1)}, bf16[32,2816]{1,0:T(8,128)(2,1)S(1)}, u32[]{:S(2)}, u32[]{:S(2)}) collective-permute-start(bf16[32,2816]{1,0:T(8,128)(2,1)S(1)} %pad_maximum_fusion), channel_id=1, source_target_pairs={{0,2},{1,3},{2,0},{3,1},{4,6},{5,7},{6,4},{7,5},{8,10},{9,11},{10,... | collective-permute-start | bytes 540680 | tf_op jit(solution)/shard_map/ppermute | solution.py:275
  32.0 8.9 %project.6 = (f32[64,2304]{1,0:T(8,128)S(1)}, bf16[64,2304]{1,0:T(8,128)(2,1)S(1)}) custom-call(s32[1]{0:T(128)} %bitcast.4.z_ref, bf16[64,4096]{1,0:T(8,128)(2,1)S(1)} %collective-permute-done.a0_ref, bf16[64,4096]{1,0:T(8,128)(2,1)S(1)} %collective-permute-done.3.a1_ref, bf16[1,4096]{1,0:T(2,128)(2,1)S(1)} %reshape.17.gain_ref, bf16[4096,4608]{1,0:T(8,128)(2,1)} %w_hbm.7), custom_call_target="tpu_custom_call" | custom-call | tf_op jit(solution)/shard_map/project/pallas_call | solution.py:94
  40.9 0.5 collective-permute-start.6
  41.5 0.0 collective-permute-done.5
  41.5 2.4 %collective-permute-start.7 = (bf16[32,2560]{1,0:T(8,128)(2,1)S(1)}, bf16[32,2560]{1,0:T(8,128)(2,1)S(1)}, u32[]{:S(2)}, u32[]{:S(2)}) collective-permute-start(bf16[32,2560]{1,0:T(8,128)(2,1)S(1)} %pad_maximum_fusion.1), channel_id=1, source_target_pairs={{0,2},{1,3},{2,0},{3,1},{4,6},{5,7},{6,4},{7,5},{8,10},{9,11},{10,... | collective-permute-start | bytes 491528 | tf_op jit(solution)/shard_map/ppermute | solution.py:275
  44.0 7.8 %project.7 = (f32[64,2048]{1,0:T(8,128)S(1)}, bf16[64,2048]{1,0:T(8,128)(2,1)S(1)}) custom-call(s32[1]{0:T(128)} %bitcast.4.z_ref, bf16[64,4096]{1,0:T(8,128)(2,1)} %a0_ref.2, bf16[64,4096]{1,0:T(8,128)(2,1)S(1)} %collective-permute-done.1.a1_ref, bf16[1,4096]{1,0:T(2,128)(2,1)S(1)} %reshape.17.gain_ref, bf16[4096,4608]{1,0:T(8,128)(2,1)} %w_hbm.7), custom_call_target="tpu_custom_call" | custom-call | tf_op jit(solution)/shard_map/project/pallas_call | solution.py:94
  51.7 2.5 %collective-permute-start.10 = (bf16[64,2048]{1,0:T(8,128)(2,1)S(1)}, bf16[64,2048]{1,0:T(8,128)(2,1)S(1)}, u32[]{:S(2)}, u32[]{:S(2)}) collective-permute-start(bf16[64,2048]{1,0:T(8,128)(2,1)S(1)} %get-tuple-element.74), channel_id=1, source_target_pairs={{0,1},{1,0},{2,3},{3,2},{4,5},{5,4},{6,7},{7,6},{8,9},{9,8},{10,11... | collective-permute-start | bytes 786440 | tf_op jit(solution)/shard_map/ppermute | solution.py:275
  54.3 0.0 collective-permute-done.6
  54.3 0.1 fusion.15
  54.5 0.1 multiply_convert_fusion.refs_4_
  54.6 0.1 fusion.8
  54.7 0.1 multiply_convert_fusion.2
  54.8 1.6 %collective-permute-start.8 = (bf16[32,2304]{1,0:T(8,128)(2,1)S(1)}, bf16[32,2304]{1,0:T(8,128)(2,1)S(1)}, u32[]{:S(2)}, u32[]{:S(2)}) collective-permute-start(bf16[32,2304]{1,0:T(8,128)(2,1)S(1)} %multiply_convert_fusion.2), channel_id=1, source_target_pairs={{8,0},{12,4},{0,8},{4,12},{9,1},{13,5},{1,9},{5,13},{10,2},{14,6},... | collective-permute-start | bytes 442376 | tf_op jit(solution)/shard_map/ppermute | solution.py:272
  56.4 0.8 collective-permute-start.9
  57.1 3.4 %collective-permute-done.10 = bf16[64,2048]{1,0:T(8,128)(2,1)S(1)} collective-permute-done((bf16[64,2048]{1,0:T(8,128)(2,1)S(1)}, bf16[64,2048]{1,0:T(8,128)(2,1)S(1)}, u32[]{:S(2)}, u32[]{:S(2)}) %collective-permute-start.10) | collective-permute-done | bytes 262176 | tf_op jit(solution)/shard_map/ppermute | solution.py:275
  60.6 3.5 %collective-permute-done.9 = bf16[32,2304]{1,0:T(8,128)(2,1)S(1)} collective-permute-done((bf16[32,2304]{1,0:T(8,128)(2,1)S(1)}, bf16[32,2304]{1,0:T(8,128)(2,1)S(1)}, u32[]{:S(2)}, u32[]{:S(2)}) %collective-permute-start.9) | collective-permute-done | bytes 147488 | tf_op jit(solution)/shard_map/ppermute | solution.py:275
  64.0 0.8 %collective-permute-start.11 = (bf16[32,2048]{1,0:T(8,128)(2,1)S(1)}, bf16[32,2048]{1,0:T(8,128)(2,1)S(1)}, u32[]{:S(2)}, u32[]{:S(2)}) collective-permute-start(bf16[32,2048]{1,0:T(8,128)(2,1)S(1)} %add_convert_fusion.3), channel_id=1, source_target_pairs={{0,2},{1,3},{2,0},{3,1},{4,6},{5,7},{6,4},{7,5},{8,10},{9,11},{10,... | collective-permute-start | bytes 393224 | tf_op jit(solution)/shard_map/ppermute | solution.py:275
  64.8 0.1 multiply_convert_fusion.1
  64.9 1.6 %collective-permute-start.14 = (bf16[32,2304]{1,0:T(8,128)(2,1)S(1)}, bf16[32,2304]{1,0:T(8,128)(2,1)S(1)}, u32[]{:S(2)}, u32[]{:S(2)}) collective-permute-start(bf16[32,2304]{1,0:T(8,128)(2,1)S(1)} %multiply_convert_fusion.1), channel_id=1, source_target_pairs={{8,0},{12,4},{0,8},{4,12},{9,1},{13,5},{1,9},{5,13},{10,2},{14,6},... | collective-permute-start | bytes 442376 | tf_op jit(solution)/shard_map/ppermute | solution.py:272
  66.5 3.5 %fetch.1 = (bf16[16,128,1024]{2,1,0:T(8,128)(2,1)S(1)}, bf16[16,128,1024]{2,1,0:T(8,128)(2,1)S(1)}, f32[8,128]{1,0:T(8,128)S(1)}) custom-call(bf16[16,128,1024]{2,1,0:T(8,128)(2,1)} %keys_hbm, bf16[16,128,1024]{2,1,0:T(8,128)(2,1)} %values_hbm.1), custom_call_target="tpu_custom_call" | custom-call | tf_op jit(solution)/shard_map/fetch/pallas_call | solution.py:234
  70.0 0.1 collective-permute-done.11
  70.1 0.1 multiply_convert_fusion.3.refs_10_
  70.2 0.1 collective-permute-start.16
  70.3 0.5 collective-permute-start.13
  70.8 0.1 collective-permute-start.12
  70.9 0.0 collective-permute-done.14.refs_8_
  70.9 0.4 collective-permute-start.15
  71.3 0.1 pad_add_fusion.refs_0_
  71.4 0.1 pad_maximum_fusion.2
  71.5 0.2 collective-permute-done.16.refs_11_
  71.6 0.2 collective-permute-done.13.refs_7_
  71.9 0.6 collective-permute-done.15.refs_9_
  72.4 0.0 collective-permute-done.12.refs_5_
  72.4 4.4 %attend.1 = (bf16[16,16384]{1,0:T(8,128)(2,1)}, bf16[16,2048]{1,0:T(8,128)(2,1)}) custom-call(s32[4]{0:T(128)S(1)} %pad_add_fusion.refs_0_, s32[16]{0:T(128)S(1)} %copy-done, f32[16,128]{1,0:T(8,128)S(1)} %get-tuple-element.103.refs_2_, f32[16,128]{1,0:T(8,128)S(1)} %get-tuple-element.104.refs_3_, bf16[32,2560]{1,0:T(8,128)(2,1)S(1)} %multiply_convert_fusion.refs_4_, ...), custom_call_target="tpu_custom_call" | custom-call | tf_op jit(solution)/shard_map/attend/pallas_call | solution.py:199
  (18 shorter events, 0.2 us)
Async XLA Ops:
  0.6 3.8 %collective-permute-start.1 = (bf16[64,4096]{1,0:T(8,128)(2,1)}, bf16[64,4096]{1,0:T(8,128)(2,1)S(1)}, u32[]{:S(2)}, u32[]{:S(2)}) collective-permute-start(bf16[64,4096]{1,0:T(8,128)(2,1)} %a0_ref.2), channel_id=1, source_target_pairs={{4,0},{0,4},{12,8},{8,12},{5,1},{1,5},{13,9},{9,13},{6,2},{2,6},{1... | collective-permute-start | bytes 1572872 | tf_op jit(solution)/shard_map/ppermute | solution.py:272
  1.1 15.3 %collective-permute-start = (bf16[64,4096]{1,0:T(8,128)(2,1)}, bf16[64,4096]{1,0:T(8,128)(2,1)S(1)}, u32[]{:S(2)}, u32[]{:S(2)}) collective-permute-start(bf16[64,4096]{1,0:T(8,128)(2,1)} %a0_ref.2), channel_id=1, source_target_pairs={{8,0},{12,4},{0,8},{4,12},{9,1},{13,5},{1,9},{5,13},{10,2},{14,6},... | collective-permute-start | bytes 1572872 | tf_op jit(solution)/shard_map/ppermute | solution.py:272
  4.4 13.9 %copy-start = (s32[16]{0:T(128)S(1)}, s32[16]{0:T(128)}, u32[]{:S(2)}) copy-start(s32[16]{0:T(128)} %refs_1_.1) | copy-start | bytes 196
  16.4 2.0 %collective-permute-start.3 = (bf16[64,4096]{1,0:T(8,128)(2,1)S(1)}, bf16[64,4096]{1,0:T(8,128)(2,1)S(1)}, u32[]{:S(2)}, u32[]{:S(2)}) collective-permute-start(bf16[64,4096]{1,0:T(8,128)(2,1)S(1)} %collective-permute-done.a0_ref), channel_id=1, source_target_pairs={{4,0},{0,4},{12,8},{8,12},{5,1},{1,5},{13,9},{9,13},{6,2},{2,6},{1... | collective-permute-start | bytes 1572872 | tf_op jit(solution)/shard_map/ppermute | solution.py:272
  16.4 11.0 %collective-permute-start.2 = (bf16[64,2816]{1,0:T(8,128)(2,1)S(1)}, bf16[64,2816]{1,0:T(8,128)(2,1)S(1)}, u32[]{:S(2)}, u32[]{:S(2)}) collective-permute-start(bf16[64,2816]{1,0:T(8,128)(2,1)S(1)} %get-tuple-element.46), channel_id=1, source_target_pairs={{0,1},{1,0},{2,3},{3,2},{4,5},{5,4},{6,7},{7,6},{8,9},{9,8},{10,11... | collective-permute-start | bytes 1081352 | tf_op jit(solution)/shard_map/ppermute | solution.py:275
  27.5 13.9 %collective-permute-start.4 = (bf16[64,2560]{1,0:T(8,128)(2,1)S(1)}, bf16[64,2560]{1,0:T(8,128)(2,1)S(1)}, u32[]{:S(2)}, u32[]{:S(2)}) collective-permute-start(bf16[64,2560]{1,0:T(8,128)(2,1)S(1)} %get-tuple-element.51), channel_id=1, source_target_pairs={{0,1},{1,0},{2,3},{3,2},{4,5},{5,4},{6,7},{7,6},{8,9},{9,8},{10,11... | collective-permute-start | bytes 983048 | tf_op jit(solution)/shard_map/ppermute | solution.py:275
  29.3 12.2 %collective-permute-start.5 = (bf16[32,2816]{1,0:T(8,128)(2,1)S(1)}, bf16[32,2816]{1,0:T(8,128)(2,1)S(1)}, u32[]{:S(2)}, u32[]{:S(2)}) collective-permute-start(bf16[32,2816]{1,0:T(8,128)(2,1)S(1)} %pad_maximum_fusion), channel_id=1, source_target_pairs={{0,2},{1,3},{2,0},{3,1},{4,6},{5,7},{6,4},{7,5},{8,10},{9,11},{10,... | collective-permute-start | bytes 540680 | tf_op jit(solution)/shard_map/ppermute | solution.py:275
  40.9 13.4 %collective-permute-start.6 = (bf16[64,2304]{1,0:T(8,128)(2,1)S(1)}, bf16[64,2304]{1,0:T(8,128)(2,1)S(1)}, u32[]{:S(2)}, u32[]{:S(2)}) collective-permute-start(bf16[64,2304]{1,0:T(8,128)(2,1)S(1)} %get-tuple-element.63), channel_id=1, source_target_pairs={{0,1},{1,0},{2,3},{3,2},{4,5},{5,4},{6,7},{7,6},{8,9},{9,8},{10,11... | collective-permute-start | bytes 884744 | tf_op jit(solution)/shard_map/ppermute | solution.py:275
  41.5 12.8 %collective-permute-start.7 = (bf16[32,2560]{1,0:T(8,128)(2,1)S(1)}, bf16[32,2560]{1,0:T(8,128)(2,1)S(1)}, u32[]{:S(2)}, u32[]{:S(2)}) collective-permute-start(bf16[32,2560]{1,0:T(8,128)(2,1)S(1)} %pad_maximum_fusion.1), channel_id=1, source_target_pairs={{0,2},{1,3},{2,0},{3,1},{4,6},{5,7},{6,4},{7,5},{8,10},{9,11},{10,... | collective-permute-start | bytes 491528 | tf_op jit(solution)/shard_map/ppermute | solution.py:275
  51.7 8.8 %collective-permute-start.10 = (bf16[64,2048]{1,0:T(8,128)(2,1)S(1)}, bf16[64,2048]{1,0:T(8,128)(2,1)S(1)}, u32[]{:S(2)}, u32[]{:S(2)}) collective-permute-start(bf16[64,2048]{1,0:T(8,128)(2,1)S(1)} %get-tuple-element.74), channel_id=1, source_target_pairs={{0,1},{1,0},{2,3},{3,2},{4,5},{5,4},{6,7},{7,6},{8,9},{9,8},{10,11... | collective-permute-start | bytes 786440 | tf_op jit(solution)/shard_map/ppermute | solution.py:275
  54.8 15.2 %collective-permute-start.8 = (bf16[32,2304]{1,0:T(8,128)(2,1)S(1)}, bf16[32,2304]{1,0:T(8,128)(2,1)S(1)}, u32[]{:S(2)}, u32[]{:S(2)}) collective-permute-start(bf16[32,2304]{1,0:T(8,128)(2,1)S(1)} %multiply_convert_fusion.2), channel_id=1, source_target_pairs={{8,0},{12,4},{0,8},{4,12},{9,1},{13,5},{1,9},{5,13},{10,2},{14,6},... | collective-permute-start | bytes 442376 | tf_op jit(solution)/shard_map/ppermute | solution.py:272
  56.4 7.7 %collective-permute-start.9 = (bf16[32,2304]{1,0:T(8,128)(2,1)S(1)}, bf16[32,2304]{1,0:T(8,128)(2,1)S(1)}, u32[]{:S(2)}, u32[]{:S(2)}) collective-permute-start(bf16[32,2304]{1,0:T(8,128)(2,1)S(1)} %add_convert_fusion.1), channel_id=1, source_target_pairs={{0,2},{1,3},{2,0},{3,1},{4,6},{5,7},{6,4},{7,5},{8,10},{9,11},{10,... | collective-permute-start | bytes 442376 | tf_op jit(solution)/shard_map/ppermute | solution.py:275
  64.0 6.1 %collective-permute-start.11 = (bf16[32,2048]{1,0:T(8,128)(2,1)S(1)}, bf16[32,2048]{1,0:T(8,128)(2,1)S(1)}, u32[]{:S(2)}, u32[]{:S(2)}) collective-permute-start(bf16[32,2048]{1,0:T(8,128)(2,1)S(1)} %add_convert_fusion.3), channel_id=1, source_target_pairs={{0,2},{1,3},{2,0},{3,1},{4,6},{5,7},{6,4},{7,5},{8,10},{9,11},{10,... | collective-permute-start | bytes 393224 | tf_op jit(solution)/shard_map/ppermute | solution.py:275
  64.9 6.0 %collective-permute-start.14 = (bf16[32,2304]{1,0:T(8,128)(2,1)S(1)}, bf16[32,2304]{1,0:T(8,128)(2,1)S(1)}, u32[]{:S(2)}, u32[]{:S(2)}) collective-permute-start(bf16[32,2304]{1,0:T(8,128)(2,1)S(1)} %multiply_convert_fusion.1), channel_id=1, source_target_pairs={{8,0},{12,4},{0,8},{4,12},{9,1},{13,5},{1,9},{5,13},{10,2},{14,6},... | collective-permute-start | bytes 442376 | tf_op jit(solution)/shard_map/ppermute | solution.py:272
  70.2 1.4 %collective-permute-start.16 = (bf16[32,2048]{1,0:T(8,128)(2,1)S(1)}, bf16[32,2048]{1,0:T(8,128)(2,1)S(1)}, u32[]{:S(2)}, u32[]{:S(2)}) collective-permute-start(bf16[32,2048]{1,0:T(8,128)(2,1)S(1)} %multiply_convert_fusion.3.refs_10_), channel_id=1, source_target_pairs={{4,0},{0,4},{12,8},{8,12},{5,1},{1,5},{13,9},{9,13},{6,2},{2,6},{1... | collective-permute-start | bytes 393224 | tf_op jit(solution)/shard_map/ppermute | solution.py:272
  70.3 1.5 %collective-permute-start.13 = (bf16[32,2304]{1,0:T(8,128)(2,1)S(1)}, bf16[32,2304]{1,0:T(8,128)(2,1)S(1)}, u32[]{:S(2)}, u32[]{:S(2)}) collective-permute-start(bf16[32,2304]{1,0:T(8,128)(2,1)S(1)} %collective-permute-done.8.refs_6_), channel_id=1, source_target_pairs={{4,0},{0,4},{12,8},{8,12},{5,1},{1,5},{13,9},{9,13},{6,2},{2,6},{1... | collective-permute-start | bytes 442376 | tf_op jit(solution)/shard_map/ppermute | solution.py:272
  70.8 1.6 %collective-permute-start.12 = (bf16[32,2560]{1,0:T(8,128)(2,1)S(1)}, bf16[32,2560]{1,0:T(8,128)(2,1)S(1)}, u32[]{:S(2)}, u32[]{:S(2)}) collective-permute-start(bf16[32,2560]{1,0:T(8,128)(2,1)S(1)} %multiply_convert_fusion.refs_4_), channel_id=1, source_target_pairs={{4,0},{0,4},{12,8},{8,12},{5,1},{1,5},{13,9},{9,13},{6,2},{2,6},{1... | collective-permute-start | bytes 491528 | tf_op jit(solution)/shard_map/ppermute | solution.py:272
  70.9 1.5 %collective-permute-start.15 = (bf16[32,2304]{1,0:T(8,128)(2,1)S(1)}, bf16[32,2304]{1,0:T(8,128)(2,1)S(1)}, u32[]{:S(2)}, u32[]{:S(2)}) collective-permute-start(bf16[32,2304]{1,0:T(8,128)(2,1)S(1)} %collective-permute-done.14.refs_8_), channel_id=1, source_target_pairs={{4,0},{0,4},{12,8},{8,12},{5,1},{1,5},{13,9},{9,13},{6,2},{2,6},{1... | collective-permute-start | bytes 442376 | tf_op jit(solution)/shard_map/ppermute | solution.py:272

commit v9 on v8

--- a/solution.py
+++ b/solution.py
@@ -381,8 +381,10 @@
         for before in range(u):
             finish(before)
             hand_out(before)
+        aways[u], key_cache = tie(aways[u], key_cache)
+        keys, values, fetched = fetch(in_hbm(key_cache), in_hbm(value_cache))
         if u:
-            receiveds[last], projecteds[-1], aways[u] = tie(receiveds[last], projecteds[-1], aways[u])
+            receiveds[last], projecteds[-1], aways[u], fetched = tie(receiveds[last], projecteds[-1], aways[u], fetched)
     step_one(last)
     if count > 1:
         arrived[last - 1], aways[last] = tie(arrived[last - 1], aways[last])
@@ -390,8 +392,8 @@
     if count > 1:
         finish(last - 1)
         hand_out(last - 1)
-        projecteds[-1], key_cache = tie(projecteds[-1], key_cache)
-    keys, values, fetched = fetch(in_hbm(key_cache), in_hbm(value_cache))
+    else:
+        keys, values, fetched = fetch(in_hbm(key_cache), in_hbm(value_cache))
     *held[: last - 1], arrived[last], fetched = tie(*held[: last - 1], arrived[last], fetched)
     finish(last)
     hand_out(last)

time: 77 us -> 77 us (level)
  no operation moved by 1% of the time
where the time goes in v9:
time: 77 us; the launch traced here: 76.8 us
  Pallas kernels  42.6 us (55%)
  starting transfers between devices  21.3 us (28%)
  waiting for transfers between devices  10.3 us (13%)
  other arithmetic  1.08 us (1%)
  between operations  0.82 us (1%)
    pallas_call x4, Pallas kernels, project(): pl.pallas_call(functools.partial(project_kernel, rows, kept, first, tiles...  34.7 us
    ppermute x8, starting transfers between devices, on_z(): return lax.ppermute(array, 'gy', [(s, s ^ flip) for s in range(along_z)])  14 us
    ppermute x9, starting transfers between devices, on_gx(): return lax.ppermute(array, 'gx', pairs)  7.22 us
    ppermute x8, waiting for transfers between devices, on_z(): return lax.ppermute(array, 'gy', [(s, s ^ flip) for s in range(along_z)])  6.39 us
    pallas_call x1, Pallas kernels, attend(): pl.pallas_call(functools.partial(attend_kernel, plan, rows, width // HEAD...  4.42 us
    ppermute x9, waiting for transfers between devices, on_gx(): return lax.ppermute(array, 'gx', pairs)  3.91 us
    pallas_call x1, Pallas kernels, fetch(): pl.pallas_call(fetch_kernel, out_shape=(shape, shape, jax.ShapeDtypeStruc...  3.48 us
  transfers between devices with their start and end apart: 17, of which 7 were waited for; matrix products, arithmetic and copies ran while one was open for 2% of the time, Pallas kernels for 50%

profile of v9, /device:TPU:0, one launch (start us, length us, event | category | flops | bytes accessed | tf_op | source)
XLA Modules:
  0.0 76.8 jit_solution(8071719686797417616)
XLA Ops:
  0.6 0.5 collective-permute-start.1
  1.1 2.6 %collective-permute-start = (bf16[64,4096]{1,0:T(8,128)(2,1)}, bf16[64,4096]{1,0:T(8,128)(2,1)S(1)}, u32[]{:S(2)}, u32[]{:S(2)}) collective-permute-start(bf16[64,4096]{1,0:T(8,128)(2,1)} %a0_ref.2), channel_id=1, source_target_pairs={{8,0},{12,4},{0,8},{4,12},{9,1},{13,5},{1,9},{5,13},{10,2},{14,6},... | collective-permute-start | bytes 1572872 | tf_op jit(solution)/shard_map/ppermute | solution.py:272
  3.7 0.7 reshape.17.gain_ref
  4.4 0.0 collective-permute-done.1.a1_ref
  4.4 0.0 copy-start
  4.4 9.0 %project.4 = (f32[64,2688]{1,0:T(8,128)S(1)}, bf16[64,2816]{1,0:T(8,128)(2,1)S(1)}) custom-call(s32[1]{0:T(128)} %bitcast.4.z_ref, bf16[64,4096]{1,0:T(8,128)(2,1)} %a0_ref.2, bf16[64,4096]{1,0:T(8,128)(2,1)S(1)} %collective-permute-done.1.a1_ref, bf16[1,4096]{1,0:T(2,128)(2,1)S(1)} %reshape.17.gain_ref, bf16[4096,4608]{1,0:T(8,128)(2,1)} %w_hbm.7), custom_call_target="tpu_custom_call" | custom-call | tf_op jit(solution)/shard_map/project/pallas_call | solution.py:94
  13.5 3.0 %collective-permute-done.a0_ref = bf16[64,4096]{1,0:T(8,128)(2,1)S(1)} collective-permute-done((bf16[64,4096]{1,0:T(8,128)(2,1)}, bf16[64,4096]{1,0:T(8,128)(2,1)S(1)}, u32[]{:S(2)}, u32[]{:S(2)}) %collective-permute-start) | collective-permute-done | bytes 524320 | tf_op jit(solution)/shard_map/ppermute | solution.py:272
  16.4 0.0 collective-permute-start.3
  16.4 1.8 %collective-permute-start.2 = (bf16[64,2816]{1,0:T(8,128)(2,1)S(1)}, bf16[64,2816]{1,0:T(8,128)(2,1)S(1)}, u32[]{:S(2)}, u32[]{:S(2)}) collective-permute-start(bf16[64,2816]{1,0:T(8,128)(2,1)S(1)} %get-tuple-element.47), channel_id=1, source_target_pairs={{0,1},{1,0},{2,3},{3,2},{4,5},{5,4},{6,7},{7,6},{8,9},{9,8},{10,11... | collective-permute-start | bytes 1081352 | tf_op jit(solution)/shard_map/ppermute | solution.py:275
  18.3 0.1 fusion.16
  18.4 0.0 collective-permute-done.3.a1_ref
  18.4 9.0 %project.5 = (f32[64,2432]{1,0:T(8,128)S(1)}, bf16[64,2560]{1,0:T(8,128)(2,1)S(1)}) custom-call(s32[1]{0:T(128)} %bitcast.4.z_ref, bf16[64,4096]{1,0:T(8,128)(2,1)S(1)} %collective-permute-done.a0_ref, bf16[64,4096]{1,0:T(8,128)(2,1)S(1)} %collective-permute-done.3.a1_ref, bf16[1,4096]{1,0:T(2,128)(2,1)S(1)} %reshape.17.gain_ref, bf16[4096,4608]{1,0:T(8,128)(2,1)} %w_hbm.7), custom_call_target="tpu_custom_call" | custom-call | tf_op jit(solution)/shard_map/project/pallas_call | solution.py:94
  27.4 0.0 collective-permute-done.2
  27.5 1.8 %collective-permute-start.4 = (bf16[64,2560]{1,0:T(8,128)(2,1)S(1)}, bf16[64,2560]{1,0:T(8,128)(2,1)S(1)}, u32[]{:S(2)}, u32[]{:S(2)}) collective-permute-start(bf16[64,2560]{1,0:T(8,128)(2,1)S(1)} %get-tuple-element.52), channel_id=1, source_target_pairs={{0,1},{1,0},{2,3},{3,2},{4,5},{5,4},{6,7},{7,6},{8,9},{9,8},{10,11... | collective-permute-start | bytes 983048 | tf_op jit(solution)/shard_map/ppermute | solution.py:275
  29.3 2.7 %collective-permute-start.5 = (bf16[32,2816]{1,0:T(8,128)(2,1)S(1)}, bf16[32,2816]{1,0:T(8,128)(2,1)S(1)}, u32[]{:S(2)}, u32[]{:S(2)}) collective-permute-start(bf16[32,2816]{1,0:T(8,128)(2,1)S(1)} %pad_maximum_fusion), channel_id=1, source_target_pairs={{0,2},{1,3},{2,0},{3,1},{4,6},{5,7},{6,4},{7,5},{8,10},{9,11},{10,... | collective-permute-start | bytes 540680 | tf_op jit(solution)/shard_map/ppermute | solution.py:275
  32.0 8.9 %project.6 = (f32[64,2304]{1,0:T(8,128)S(1)}, bf16[64,2304]{1,0:T(8,128)(2,1)S(1)}) custom-call(s32[1]{0:T(128)} %bitcast.4.z_ref, bf16[64,4096]{1,0:T(8,128)(2,1)S(1)} %collective-permute-done.a0_ref, bf16[64,4096]{1,0:T(8,128)(2,1)S(1)} %collective-permute-done.3.a1_ref, bf16[1,4096]{1,0:T(2,128)(2,1)S(1)} %reshape.17.gain_ref, bf16[4096,4608]{1,0:T(8,128)(2,1)} %w_hbm.7), custom_call_target="tpu_custom_call" | custom-call | tf_op jit(solution)/shard_map/project/pallas_call | solution.py:94
  40.9 0.5 collective-permute-start.6
  41.4 0.0 collective-permute-done.4
  41.5 0.0 collective-permute-done.5
  41.5 2.4 %collective-permute-start.7 = (bf16[32,2560]{1,0:T(8,128)(2,1)S(1)}, bf16[32,2560]{1,0:T(8,128)(2,1)S(1)}, u32[]{:S(2)}, u32[]{:S(2)}) collective-permute-start(bf16[32,2560]{1,0:T(8,128)(2,1)S(1)} %pad_maximum_fusion.1), channel_id=1, source_target_pairs={{0,2},{1,3},{2,0},{3,1},{4,6},{5,7},{6,4},{7,5},{8,10},{9,11},{10,... | collective-permute-start | bytes 491528 | tf_op jit(solution)/shard_map/ppermute | solution.py:275
  44.0 7.8 %project.7 = (f32[64,2048]{1,0:T(8,128)S(1)}, bf16[64,2048]{1,0:T(8,128)(2,1)S(1)}) custom-call(s32[1]{0:T(128)} %bitcast.4.z_ref, bf16[64,4096]{1,0:T(8,128)(2,1)} %a0_ref.2, bf16[64,4096]{1,0:T(8,128)(2,1)S(1)} %collective-permute-done.1.a1_ref, bf16[1,4096]{1,0:T(2,128)(2,1)S(1)} %reshape.17.gain_ref, bf16[4096,4608]{1,0:T(8,128)(2,1)} %w_hbm.7), custom_call_target="tpu_custom_call" | custom-call | tf_op jit(solution)/shard_map/project/pallas_call | solution.py:94
  51.7 2.5 %collective-permute-start.10 = (bf16[64,2048]{1,0:T(8,128)(2,1)S(1)}, bf16[64,2048]{1,0:T(8,128)(2,1)S(1)}, u32[]{:S(2)}, u32[]{:S(2)}) collective-permute-start(bf16[64,2048]{1,0:T(8,128)(2,1)S(1)} %get-tuple-element.75), channel_id=1, source_target_pairs={{0,1},{1,0},{2,3},{3,2},{4,5},{5,4},{6,7},{7,6},{8,9},{9,8},{10,11... | collective-permute-start | bytes 786440 | tf_op jit(solution)/shard_map/ppermute | solution.py:275
  54.3 0.0 collective-permute-done.7
  54.3 0.1 fusion.15
  54.5 0.1 multiply_convert_fusion.refs_4_
  54.6 0.1 fusion.8
  54.7 0.1 multiply_convert_fusion.2
  54.8 0.8 %collective-permute-start.9 = (bf16[32,2304]{1,0:T(8,128)(2,1)S(1)}, bf16[32,2304]{1,0:T(8,128)(2,1)S(1)}, u32[]{:S(2)}, u32[]{:S(2)}) collective-permute-start(bf16[32,2304]{1,0:T(8,128)(2,1)S(1)} %add_convert_fusion.1), channel_id=1, source_target_pairs={{0,2},{1,3},{2,0},{3,1},{4,6},{5,7},{6,4},{7,5},{8,10},{9,11},{10,... | collective-permute-start | bytes 442376 | tf_op jit(solution)/shard_map/ppermute | solution.py:275
  55.6 1.5 %collective-permute-start.8 = (bf16[32,2304]{1,0:T(8,128)(2,1)S(1)}, bf16[32,2304]{1,0:T(8,128)(2,1)S(1)}, u32[]{:S(2)}, u32[]{:S(2)}) collective-permute-start(bf16[32,2304]{1,0:T(8,128)(2,1)S(1)} %multiply_convert_fusion.2), channel_id=1, source_target_pairs={{8,0},{12,4},{0,8},{4,12},{9,1},{13,5},{1,9},{5,13},{10,2},{14,6},... | collective-permute-start | bytes 442376 | tf_op jit(solution)/shard_map/ppermute | solution.py:272
  57.1 3.5 %fetch.1 = (bf16[16,128,1024]{2,1,0:T(8,128)(2,1)S(1)}, bf16[16,128,1024]{2,1,0:T(8,128)(2,1)S(1)}, f32[8,128]{1,0:T(8,128)S(1)}) custom-call(bf16[16,128,1024]{2,1,0:T(8,128)(2,1)} %keys_hbm, bf16[16,128,1024]{2,1,0:T(8,128)(2,1)} %values_hbm.1), custom_call_target="tpu_custom_call" | custom-call | tf_op jit(solution)/shard_map/fetch/pallas_call | solution.py:234
  60.6 1.2 %collective-permute-done.10 = bf16[64,2048]{1,0:T(8,128)(2,1)S(1)} collective-permute-done((bf16[64,2048]{1,0:T(8,128)(2,1)S(1)}, bf16[64,2048]{1,0:T(8,128)(2,1)S(1)}, u32[]{:S(2)}, u32[]{:S(2)}) %collective-permute-start.10) | collective-permute-done | bytes 262176 | tf_op jit(solution)/shard_map/ppermute | solution.py:275
  61.9 1.5 %collective-permute-done.9 = bf16[32,2304]{1,0:T(8,128)(2,1)S(1)} collective-permute-done((bf16[32,2304]{1,0:T(8,128)(2,1)S(1)}, bf16[32,2304]{1,0:T(8,128)(2,1)S(1)}, u32[]{:S(2)}, u32[]{:S(2)}) %collective-permute-start.9) | collective-permute-done | bytes 147488 | tf_op jit(solution)/shard_map/ppermute | solution.py:275
  63.4 1.5 %collective-permute-start.11 = (bf16[32,2048]{1,0:T(8,128)(2,1)S(1)}, bf16[32,2048]{1,0:T(8,128)(2,1)S(1)}, u32[]{:S(2)}, u32[]{:S(2)}) collective-permute-start(bf16[32,2048]{1,0:T(8,128)(2,1)S(1)} %add_convert_fusion.3), channel_id=1, source_target_pairs={{0,2},{1,3},{2,0},{3,1},{4,6},{5,7},{6,4},{7,5},{8,10},{9,11},{10,... | collective-permute-start | bytes 393224 | tf_op jit(solution)/shard_map/ppermute | solution.py:275
  64.9 0.1 multiply_convert_fusion.1
  65.0 1.6 %collective-permute-start.14 = (bf16[32,2304]{1,0:T(8,128)(2,1)S(1)}, bf16[32,2304]{1,0:T(8,128)(2,1)S(1)}, u32[]{:S(2)}, u32[]{:S(2)}) collective-permute-start(bf16[32,2304]{1,0:T(8,128)(2,1)S(1)} %multiply_convert_fusion.1), channel_id=1, source_target_pairs={{8,0},{12,4},{0,8},{4,12},{9,1},{13,5},{1,9},{5,13},{10,2},{14,6},... | collective-permute-start | bytes 442376 | tf_op jit(solution)/shard_map/ppermute | solution.py:272
  66.5 3.6 %collective-permute-done.11 = bf16[32,2048]{1,0:T(8,128)(2,1)S(1)} collective-permute-done((bf16[32,2048]{1,0:T(8,128)(2,1)S(1)}, bf16[32,2048]{1,0:T(8,128)(2,1)S(1)}, u32[]{:S(2)}, u32[]{:S(2)}) %collective-permute-start.11) | collective-permute-done | bytes 131104 | tf_op jit(solution)/shard_map/ppermute | solution.py:275
  70.1 0.1 multiply_convert_fusion.3.refs_10_
  70.2 0.1 collective-permute-start.16
  70.3 0.5 collective-permute-start.13
  70.8 0.1 collective-permute-start.12
  70.9 0.4 collective-permute-start.15
  71.3 0.1 pad_add_fusion.refs_0_
  71.4 0.1 pad_maximum_fusion.2
  71.5 0.2 collective-permute-done.16.refs_11_
  71.6 0.2 collective-permute-done.13.refs_7_
  71.9 0.6 collective-permute-done.15.refs_9_
  72.4 0.0 collective-permute-done.12.refs_5_
  72.4 4.4 %attend.1 = (bf16[16,16384]{1,0:T(8,128)(2,1)}, bf16[16,2048]{1,0:T(8,128)(2,1)}) custom-call(s32[4]{0:T(128)S(1)} %pad_add_fusion.refs_0_, s32[16]{0:T(128)S(1)} %copy-done, f32[16,128]{1,0:T(8,128)S(1)} %get-tuple-element.105.refs_2_, f32[16,128]{1,0:T(8,128)S(1)} %get-tuple-element.106.refs_3_, bf16[32,2560]{1,0:T(8,128)(2,1)S(1)} %multiply_convert_fusion.refs_4_, ...), custom_call_target="tpu_custom_call" | custom-call | tf_op jit(solution)/shard_map/attend/pallas_call | solution.py:199
  (18 shorter events, 0.2 us)
Async XLA Ops:
  0.6 3.8 %collective-permute-start.1 = (bf16[64,4096]{1,0:T(8,128)(2,1)}, bf16[64,4096]{1,0:T(8,128)(2,1)S(1)}, u32[]{:S(2)}, u32[]{:S(2)}) collective-permute-start(bf16[64,4096]{1,0:T(8,128)(2,1)} %a0_ref.2), channel_id=1, source_target_pairs={{4,0},{0,4},{12,8},{8,12},{5,1},{1,5},{13,9},{9,13},{6,2},{2,6},{1... | collective-permute-start | bytes 1572872 | tf_op jit(solution)/shard_map/ppermute | solution.py:272
  1.1 15.3 %collective-permute-start = (bf16[64,4096]{1,0:T(8,128)(2,1)}, bf16[64,4096]{1,0:T(8,128)(2,1)S(1)}, u32[]{:S(2)}, u32[]{:S(2)}) collective-permute-start(bf16[64,4096]{1,0:T(8,128)(2,1)} %a0_ref.2), channel_id=1, source_target_pairs={{8,0},{12,4},{0,8},{4,12},{9,1},{13,5},{1,9},{5,13},{10,2},{14,6},... | collective-permute-start | bytes 1572872 | tf_op jit(solution)/shard_map/ppermute | solution.py:272
  4.4 13.9 %copy-start = (s32[16]{0:T(128)S(1)}, s32[16]{0:T(128)}, u32[]{:S(2)}) copy-start(s32[16]{0:T(128)} %refs_1_.1) | copy-start | bytes 196
  16.4 2.0 %collective-permute-start.3 = (bf16[64,4096]{1,0:T(8,128)(2,1)S(1)}, bf16[64,4096]{1,0:T(8,128)(2,1)S(1)}, u32[]{:S(2)}, u32[]{:S(2)}) collective-permute-start(bf16[64,4096]{1,0:T(8,128)(2,1)S(1)} %collective-permute-done.a0_ref), channel_id=1, source_target_pairs={{4,0},{0,4},{12,8},{8,12},{5,1},{1,5},{13,9},{9,13},{6,2},{2,6},{1... | collective-permute-start | bytes 1572872 | tf_op jit(solution)/shard_map/ppermute | solution.py:272
  16.4 11.0 %collective-permute-start.2 = (bf16[64,2816]{1,0:T(8,128)(2,1)S(1)}, bf16[64,2816]{1,0:T(8,128)(2,1)S(1)}, u32[]{:S(2)}, u32[]{:S(2)}) collective-permute-start(bf16[64,2816]{1,0:T(8,128)(2,1)S(1)} %get-tuple-element.47), channel_id=1, source_target_pairs={{0,1},{1,0},{2,3},{3,2},{4,5},{5,4},{6,7},{7,6},{8,9},{9,8},{10,11... | collective-permute-start | bytes 1081352 | tf_op jit(solution)/shard_map/ppermute | solution.py:275
  27.5 13.9 %collective-permute-start.4 = (bf16[64,2560]{1,0:T(8,128)(2,1)S(1)}, bf16[64,2560]{1,0:T(8,128)(2,1)S(1)}, u32[]{:S(2)}, u32[]{:S(2)}) collective-permute-start(bf16[64,2560]{1,0:T(8,128)(2,1)S(1)} %get-tuple-element.52), channel_id=1, source_target_pairs={{0,1},{1,0},{2,3},{3,2},{4,5},{5,4},{6,7},{7,6},{8,9},{9,8},{10,11... | collective-permute-start | bytes 983048 | tf_op jit(solution)/shard_map/ppermute | solution.py:275
  29.3 12.2 %collective-permute-start.5 = (bf16[32,2816]{1,0:T(8,128)(2,1)S(1)}, bf16[32,2816]{1,0:T(8,128)(2,1)S(1)}, u32[]{:S(2)}, u32[]{:S(2)}) collective-permute-start(bf16[32,2816]{1,0:T(8,128)(2,1)S(1)} %pad_maximum_fusion), channel_id=1, source_target_pairs={{0,2},{1,3},{2,0},{3,1},{4,6},{5,7},{6,4},{7,5},{8,10},{9,11},{10,... | collective-permute-start | bytes 540680 | tf_op jit(solution)/shard_map/ppermute | solution.py:275
  40.9 13.4 %collective-permute-start.6 = (bf16[64,2304]{1,0:T(8,128)(2,1)S(1)}, bf16[64,2304]{1,0:T(8,128)(2,1)S(1)}, u32[]{:S(2)}, u32[]{:S(2)}) collective-permute-start(bf16[64,2304]{1,0:T(8,128)(2,1)S(1)} %get-tuple-element.64), channel_id=1, source_target_pairs={{0,1},{1,0},{2,3},{3,2},{4,5},{5,4},{6,7},{7,6},{8,9},{9,8},{10,11... | collective-permute-start | bytes 884744 | tf_op jit(solution)/shard_map/ppermute | solution.py:275
  41.5 12.8 %collective-permute-start.7 = (bf16[32,2560]{1,0:T(8,128)(2,1)S(1)}, bf16[32,2560]{1,0:T(8,128)(2,1)S(1)}, u32[]{:S(2)}, u32[]{:S(2)}) collective-permute-start(bf16[32,2560]{1,0:T(8,128)(2,1)S(1)} %pad_maximum_fusion.1), channel_id=1, source_target_pairs={{0,2},{1,3},{2,0},{3,1},{4,6},{5,7},{6,4},{7,5},{8,10},{9,11},{10,... | collective-permute-start | bytes 491528 | tf_op jit(solution)/shard_map/ppermute | solution.py:275
  51.7 10.1 %collective-permute-start.10 = (bf16[64,2048]{1,0:T(8,128)(2,1)S(1)}, bf16[64,2048]{1,0:T(8,128)(2,1)S(1)}, u32[]{:S(2)}, u32[]{:S(2)}) collective-permute-start(bf16[64,2048]{1,0:T(8,128)(2,1)S(1)} %get-tuple-element.75), channel_id=1, source_target_pairs={{0,1},{1,0},{2,3},{3,2},{4,5},{5,4},{6,7},{7,6},{8,9},{9,8},{10,11... | collective-permute-start | bytes 786440 | tf_op jit(solution)/shard_map/ppermute | solution.py:275
  54.8 8.6 %collective-permute-start.9 = (bf16[32,2304]{1,0:T(8,128)(2,1)S(1)}, bf16[32,2304]{1,0:T(8,128)(2,1)S(1)}, u32[]{:S(2)}, u32[]{:S(2)}) collective-permute-start(bf16[32,2304]{1,0:T(8,128)(2,1)S(1)} %add_convert_fusion.1), channel_id=1, source_target_pairs={{0,2},{1,3},{2,0},{3,1},{4,6},{5,7},{6,4},{7,5},{8,10},{9,11},{10,... | collective-permute-start | bytes 442376 | tf_op jit(solution)/shard_map/ppermute | solution.py:275
  55.6 10.9 %collective-permute-start.8 = (bf16[32,2304]{1,0:T(8,128)(2,1)S(1)}, bf16[32,2304]{1,0:T(8,128)(2,1)S(1)}, u32[]{:S(2)}, u32[]{:S(2)}) collective-permute-start(bf16[32,2304]{1,0:T(8,128)(2,1)S(1)} %multiply_convert_fusion.2), channel_id=1, source_target_pairs={{8,0},{12,4},{0,8},{4,12},{9,1},{13,5},{1,9},{5,13},{10,2},{14,6},... | collective-permute-start | bytes 442376 | tf_op jit(solution)/shard_map/ppermute | solution.py:272
  63.4 6.7 %collective-permute-start.11 = (bf16[32,2048]{1,0:T(8,128)(2,1)S(1)}, bf16[32,2048]{1,0:T(8,128)(2,1)S(1)}, u32[]{:S(2)}, u32[]{:S(2)}) collective-permute-start(bf16[32,2048]{1,0:T(8,128)(2,1)S(1)} %add_convert_fusion.3), channel_id=1, source_target_pairs={{0,2},{1,3},{2,0},{3,1},{4,6},{5,7},{6,4},{7,5},{8,10},{9,11},{10,... | collective-permute-start | bytes 393224 | tf_op jit(solution)/shard_map/ppermute | solution.py:275
  65.0 5.9 %collective-permute-start.14 = (bf16[32,2304]{1,0:T(8,128)(2,1)S(1)}, bf16[32,2304]{1,0:T(8,128)(2,1)S(1)}, u32[]{:S(2)}, u32[]{:S(2)}) collective-permute-start(bf16[32,2304]{1,0:T(8,128)(2,1)S(1)} %multiply_convert_fusion.1), channel_id=1, source_target_pairs={{8,0},{12,4},{0,8},{4,12},{9,1},{13,5},{1,9},{5,13},{10,2},{14,6},... | collective-permute-start | bytes 442376 | tf_op jit(solution)/shard_map/ppermute | solution.py:272
  70.2 1.4 %collective-permute-start.16 = (bf16[32,2048]{1,0:T(8,128)(2,1)S(1)}, bf16[32,2048]{1,0:T(8,128)(2,1)S(1)}, u32[]{:S(2)}, u32[]{:S(2)}) collective-permute-start(bf16[32,2048]{1,0:T(8,128)(2,1)S(1)} %multiply_convert_fusion.3.refs_10_), channel_id=1, source_target_pairs={{4,0},{0,4},{12,8},{8,12},{5,1},{1,5},{13,9},{9,13},{6,2},{2,6},{1... | collective-permute-start | bytes 393224 | tf_op jit(solution)/shard_map/ppermute | solution.py:272
  70.3 1.5 %collective-permute-start.13 = (bf16[32,2304]{1,0:T(8,128)(2,1)S(1)}, bf16[32,2304]{1,0:T(8,128)(2,1)S(1)}, u32[]{:S(2)}, u32[]{:S(2)}) collective-permute-start(bf16[32,2304]{1,0:T(8,128)(2,1)S(1)} %collective-permute-done.8.refs_6_), channel_id=1, source_target_pairs={{4,0},{0,4},{12,8},{8,12},{5,1},{1,5},{13,9},{9,13},{6,2},{2,6},{1... | collective-permute-start | bytes 442376 | tf_op jit(solution)/shard_map/ppermute | solution.py:272
  70.8 1.6 %collective-permute-start.12 = (bf16[32,2560]{1,0:T(8,128)(2,1)S(1)}, bf16[32,2560]{1,0:T(8,128)(2,1)S(1)}, u32[]{:S(2)}, u32[]{:S(2)}) collective-permute-start(bf16[32,2560]{1,0:T(8,128)(2,1)S(1)} %multiply_convert_fusion.refs_4_), channel_id=1, source_target_pairs={{4,0},{0,4},{12,8},{8,12},{5,1},{1,5},{13,9},{9,13},{6,2},{2,6},{1... | collective-permute-start | bytes 491528 | tf_op jit(solution)/shard_map/ppermute | solution.py:272
  70.9 1.5 %collective-permute-start.15 = (bf16[32,2304]{1,0:T(8,128)(2,1)S(1)}, bf16[32,2304]{1,0:T(8,128)(2,1)S(1)}, u32[]{:S(2)}, u32[]{:S(2)}) collective-permute-start(bf16[32,2304]{1,0:T(8,128)(2,1)S(1)} %collective-permute-done.14.refs_8_), channel_id=1, source_target_pairs={{4,0},{0,4},{12,8},{8,12},{5,1},{1,5},{13,9},{9,13},{6,2},{2,6},{1... | collective-permute-start | bytes 442376 | tf_op jit(solution)/shard_map/ppermute | solution.py:272

commit v10 on v8

--- a/solution.py
+++ b/solution.py
@@ -14,7 +14,7 @@
 HEAD_DIM = 128
 GROUP = HEADS // KV_HEADS
 CORES = 2
-IN_FLIGHT = 3
+IN_FLIGHT = 4
 OWN_SHARE = 0.56
 OTHER_SHARE = 0.5
 

time: 77 us -> 76.9 us (level)
  no operation moved by 1% of the time
where the time goes in v10:
time: 76.9 us; the launch traced here: 76.7 us
  Pallas kernels  42.5 us (55%)
  starting transfers between devices  20.4 us (27%)
  waiting for transfers between devices  11.1 us (14%)
  other arithmetic  1.08 us (1%)
  between operations  0.83 us (1%)
    pallas_call x4, Pallas kernels, project(): pl.pallas_call(functools.partial(project_kernel, rows, kept, first, tiles...  34.6 us
    ppermute x8, starting transfers between devices, on_z(): return lax.ppermute(array, 'gy', [(s, s ^ flip) for s in range(along_z)])  13.1 us
    ppermute x9, starting transfers between devices, on_gx(): return lax.ppermute(array, 'gx', pairs)  7.3 us
    ppermute x8, waiting for transfers between devices, on_z(): return lax.ppermute(array, 'gy', [(s, s ^ flip) for s in range(along_z)])  7.23 us
    pallas_call x1, Pallas kernels, attend(): pl.pallas_call(functools.partial(attend_kernel, plan, rows, width // HEAD...  4.42 us
    ppermute x9, waiting for transfers between devices, on_gx(): return lax.ppermute(array, 'gx', pairs)  3.92 us
    pallas_call x1, Pallas kernels, fetch(): pl.pallas_call(fetch_kernel, out_shape=(shape, shape, jax.ShapeDtypeStruc...  3.48 us
  transfers between devices with their start and end apart: 17, of which 7 were waited for; matrix products, arithmetic and copies ran while one was open for 2% of the time, Pallas kernels for 50%

profile of v10, /device:TPU:0, one launch (start us, length us, event | category | flops | bytes accessed | tf_op | source)
XLA Modules:
  0.0 76.7 jit_solution(17479883691628045882)
XLA Ops:
  0.6 0.5 collective-permute-start.1
  1.1 2.6 %collective-permute-start = (bf16[64,4096]{1,0:T(8,128)(2,1)}, bf16[64,4096]{1,0:T(8,128)(2,1)S(1)}, u32[]{:S(2)}, u32[]{:S(2)}) collective-permute-start(bf16[64,4096]{1,0:T(8,128)(2,1)} %a0_ref.2), channel_id=1, source_target_pairs={{8,0},{12,4},{0,8},{4,12},{9,1},{13,5},{1,9},{5,13},{10,2},{14,6},... | collective-permute-start | bytes 1572872 | tf_op jit(solution)/shard_map/ppermute | solution.py:272
  3.7 0.7 reshape.17.gain_ref
  4.4 0.0 collective-permute-done.1.a1_ref
  4.4 0.0 copy-start
  4.4 9.0 %project.4 = (f32[64,2688]{1,0:T(8,128)S(1)}, bf16[64,2816]{1,0:T(8,128)(2,1)S(1)}) custom-call(s32[1]{0:T(128)} %bitcast.4.z_ref, bf16[64,4096]{1,0:T(8,128)(2,1)} %a0_ref.2, bf16[64,4096]{1,0:T(8,128)(2,1)S(1)} %collective-permute-done.1.a1_ref, bf16[1,4096]{1,0:T(2,128)(2,1)S(1)} %reshape.17.gain_ref, bf16[4096,4608]{1,0:T(8,128)(2,1)} %w_hbm.7), custom_call_target="tpu_custom_call" | custom-call | tf_op jit(solution)/shard_map/project/pallas_call | solution.py:94
  13.5 3.0 %collective-permute-done.a0_ref = bf16[64,4096]{1,0:T(8,128)(2,1)S(1)} collective-permute-done((bf16[64,4096]{1,0:T(8,128)(2,1)}, bf16[64,4096]{1,0:T(8,128)(2,1)S(1)}, u32[]{:S(2)}, u32[]{:S(2)}) %collective-permute-start) | collective-permute-done | bytes 524320 | tf_op jit(solution)/shard_map/ppermute | solution.py:272
  16.4 0.0 collective-permute-start.3
  16.4 1.8 %collective-permute-start.2 = (bf16[64,2816]{1,0:T(8,128)(2,1)S(1)}, bf16[64,2816]{1,0:T(8,128)(2,1)S(1)}, u32[]{:S(2)}, u32[]{:S(2)}) collective-permute-start(bf16[64,2816]{1,0:T(8,128)(2,1)S(1)} %get-tuple-element.46), channel_id=1, source_target_pairs={{0,1},{1,0},{2,3},{3,2},{4,5},{5,4},{6,7},{7,6},{8,9},{9,8},{10,11... | collective-permute-start | bytes 1081352 | tf_op jit(solution)/shard_map/ppermute | solution.py:275
  18.3 0.1 fusion.16
  18.4 0.0 collective-permute-done.3.a1_ref
  18.4 9.0 %project.5 = (f32[64,2432]{1,0:T(8,128)S(1)}, bf16[64,2560]{1,0:T(8,128)(2,1)S(1)}) custom-call(s32[1]{0:T(128)} %bitcast.4.z_ref, bf16[64,4096]{1,0:T(8,128)(2,1)S(1)} %collective-permute-done.a0_ref, bf16[64,4096]{1,0:T(8,128)(2,1)S(1)} %collective-permute-done.3.a1_ref, bf16[1,4096]{1,0:T(2,128)(2,1)S(1)} %reshape.17.gain_ref, bf16[4096,4608]{1,0:T(8,128)(2,1)} %w_hbm.7), custom_call_target="tpu_custom_call" | custom-call | tf_op jit(solution)/shard_map/project/pallas_call | solution.py:94
  27.5 1.8 %collective-permute-start.4 = (bf16[64,2560]{1,0:T(8,128)(2,1)S(1)}, bf16[64,2560]{1,0:T(8,128)(2,1)S(1)}, u32[]{:S(2)}, u32[]{:S(2)}) collective-permute-start(bf16[64,2560]{1,0:T(8,128)(2,1)S(1)} %get-tuple-element.51), channel_id=1, source_target_pairs={{0,1},{1,0},{2,3},{3,2},{4,5},{5,4},{6,7},{7,6},{8,9},{9,8},{10,11... | collective-permute-start | bytes 983048 | tf_op jit(solution)/shard_map/ppermute | solution.py:275
  29.3 2.7 %collective-permute-start.5 = (bf16[32,2816]{1,0:T(8,128)(2,1)S(1)}, bf16[32,2816]{1,0:T(8,128)(2,1)S(1)}, u32[]{:S(2)}, u32[]{:S(2)}) collective-permute-start(bf16[32,2816]{1,0:T(8,128)(2,1)S(1)} %pad_maximum_fusion), channel_id=1, source_target_pairs={{0,2},{1,3},{2,0},{3,1},{4,6},{5,7},{6,4},{7,5},{8,10},{9,11},{10,... | collective-permute-start | bytes 540680 | tf_op jit(solution)/shard_map/ppermute | solution.py:275
  32.0 8.9 %project.6 = (f32[64,2304]{1,0:T(8,128)S(1)}, bf16[64,2304]{1,0:T(8,128)(2,1)S(1)}) custom-call(s32[1]{0:T(128)} %bitcast.4.z_ref, bf16[64,4096]{1,0:T(8,128)(2,1)S(1)} %collective-permute-done.a0_ref, bf16[64,4096]{1,0:T(8,128)(2,1)S(1)} %collective-permute-done.3.a1_ref, bf16[1,4096]{1,0:T(2,128)(2,1)S(1)} %reshape.17.gain_ref, bf16[4096,4608]{1,0:T(8,128)(2,1)} %w_hbm.7), custom_call_target="tpu_custom_call" | custom-call | tf_op jit(solution)/shard_map/project/pallas_call | solution.py:94
  40.9 0.5 collective-permute-start.6
  41.4 0.0 collective-permute-done.4
  41.5 0.0 collective-permute-done.5
  41.5 2.4 %collective-permute-start.7 = (bf16[32,2560]{1,0:T(8,128)(2,1)S(1)}, bf16[32,2560]{1,0:T(8,128)(2,1)S(1)}, u32[]{:S(2)}, u32[]{:S(2)}) collective-permute-start(bf16[32,2560]{1,0:T(8,128)(2,1)S(1)} %pad_maximum_fusion.1), channel_id=1, source_target_pairs={{0,2},{1,3},{2,0},{3,1},{4,6},{5,7},{6,4},{7,5},{8,10},{9,11},{10,... | collective-permute-start | bytes 491528 | tf_op jit(solution)/shard_map/ppermute | solution.py:275
  44.0 7.6 %project.7 = (f32[64,2048]{1,0:T(8,128)S(1)}, bf16[64,2048]{1,0:T(8,128)(2,1)S(1)}) custom-call(s32[1]{0:T(128)} %bitcast.4.z_ref, bf16[64,4096]{1,0:T(8,128)(2,1)} %a0_ref.2, bf16[64,4096]{1,0:T(8,128)(2,1)S(1)} %collective-permute-done.1.a1_ref, bf16[1,4096]{1,0:T(2,128)(2,1)S(1)} %reshape.17.gain_ref, bf16[4096,4608]{1,0:T(8,128)(2,1)} %w_hbm.7), custom_call_target="tpu_custom_call" | custom-call | tf_op jit(solution)/shard_map/project/pallas_call | solution.py:94
  51.6 2.5 %collective-permute-start.10 = (bf16[64,2048]{1,0:T(8,128)(2,1)S(1)}, bf16[64,2048]{1,0:T(8,128)(2,1)S(1)}, u32[]{:S(2)}, u32[]{:S(2)}) collective-permute-start(bf16[64,2048]{1,0:T(8,128)(2,1)S(1)} %get-tuple-element.74), channel_id=1, source_target_pairs={{0,1},{1,0},{2,3},{3,2},{4,5},{5,4},{6,7},{7,6},{8,9},{9,8},{10,11... | collective-permute-start | bytes 786440 | tf_op jit(solution)/shard_map/ppermute | solution.py:275
  54.2 0.0 collective-permute-done.6
  54.2 0.0 collective-permute-done.7
  54.2 0.1 fusion.15
  54.3 0.1 multiply_convert_fusion.refs_4_
  54.5 0.1 fusion.8
  54.6 0.1 multiply_convert_fusion.2
  54.7 1.6 %collective-permute-start.8 = (bf16[32,2304]{1,0:T(8,128)(2,1)S(1)}, bf16[32,2304]{1,0:T(8,128)(2,1)S(1)}, u32[]{:S(2)}, u32[]{:S(2)}) collective-permute-start(bf16[32,2304]{1,0:T(8,128)(2,1)S(1)} %multiply_convert_fusion.2), channel_id=1, source_target_pairs={{8,0},{12,4},{0,8},{4,12},{9,1},{13,5},{1,9},{5,13},{10,2},{14,6},... | collective-permute-start | bytes 442376 | tf_op jit(solution)/shard_map/ppermute | solution.py:272
  56.2 0.7 collective-permute-start.9
  57.0 3.4 %collective-permute-done.10 = bf16[64,2048]{1,0:T(8,128)(2,1)S(1)} collective-permute-done((bf16[64,2048]{1,0:T(8,128)(2,1)S(1)}, bf16[64,2048]{1,0:T(8,128)(2,1)S(1)}, u32[]{:S(2)}, u32[]{:S(2)}) %collective-permute-start.10) | collective-permute-done | bytes 262176 | tf_op jit(solution)/shard_map/ppermute | solution.py:275
  60.5 3.7 %collective-permute-done.9 = bf16[32,2304]{1,0:T(8,128)(2,1)S(1)} collective-permute-done((bf16[32,2304]{1,0:T(8,128)(2,1)S(1)}, bf16[32,2304]{1,0:T(8,128)(2,1)S(1)}, u32[]{:S(2)}, u32[]{:S(2)}) %collective-permute-start.9) | collective-permute-done | bytes 147488 | tf_op jit(solution)/shard_map/ppermute | solution.py:275
  64.1 0.6 collective-permute-start.11
  64.7 0.1 multiply_convert_fusion.1
  64.8 1.6 %collective-permute-start.14 = (bf16[32,2304]{1,0:T(8,128)(2,1)S(1)}, bf16[32,2304]{1,0:T(8,128)(2,1)S(1)}, u32[]{:S(2)}, u32[]{:S(2)}) collective-permute-start(bf16[32,2304]{1,0:T(8,128)(2,1)S(1)} %multiply_convert_fusion.1), channel_id=1, source_target_pairs={{8,0},{12,4},{0,8},{4,12},{9,1},{13,5},{1,9},{5,13},{10,2},{14,6},... | collective-permute-start | bytes 442376 | tf_op jit(solution)/shard_map/ppermute | solution.py:272
  66.4 3.5 %fetch.1 = (bf16[16,128,1024]{2,1,0:T(8,128)(2,1)S(1)}, bf16[16,128,1024]{2,1,0:T(8,128)(2,1)S(1)}, f32[8,128]{1,0:T(8,128)S(1)}) custom-call(bf16[16,128,1024]{2,1,0:T(8,128)(2,1)} %keys_hbm, bf16[16,128,1024]{2,1,0:T(8,128)(2,1)} %values_hbm.1), custom_call_target="tpu_custom_call" | custom-call | tf_op jit(solution)/shard_map/fetch/pallas_call | solution.py:234
  69.9 0.1 collective-permute-done.11
  70.0 0.1 multiply_convert_fusion.3.refs_10_
  70.1 0.1 collective-permute-start.16
  70.2 0.5 collective-permute-start.13
  70.7 0.1 collective-permute-start.12
  70.7 0.0 collective-permute-done.14.refs_8_
  70.8 0.4 collective-permute-start.15
  71.2 0.1 pad_add_fusion.refs_0_
  71.3 0.1 pad_maximum_fusion.2
  71.3 0.2 collective-permute-done.16.refs_11_
  71.5 0.2 collective-permute-done.13.refs_7_
  71.7 0.6 collective-permute-done.15.refs_9_
  72.3 4.4 %attend.1 = (bf16[16,16384]{1,0:T(8,128)(2,1)}, bf16[16,2048]{1,0:T(8,128)(2,1)}) custom-call(s32[4]{0:T(128)S(1)} %pad_add_fusion.refs_0_, s32[16]{0:T(128)S(1)} %copy-done, f32[16,128]{1,0:T(8,128)S(1)} %get-tuple-element.103.refs_2_, f32[16,128]{1,0:T(8,128)S(1)} %get-tuple-element.104.refs_3_, bf16[32,2560]{1,0:T(8,128)(2,1)S(1)} %multiply_convert_fusion.refs_4_, ...), custom_call_target="tpu_custom_call" | custom-call | tf_op jit(solution)/shard_map/attend/pallas_call | solution.py:199
  (18 shorter events, 0.2 us)
Async XLA Ops:
  0.6 3.8 %collective-permute-start.1 = (bf16[64,4096]{1,0:T(8,128)(2,1)}, bf16[64,4096]{1,0:T(8,128)(2,1)S(1)}, u32[]{:S(2)}, u32[]{:S(2)}) collective-permute-start(bf16[64,4096]{1,0:T(8,128)(2,1)} %a0_ref.2), channel_id=1, source_target_pairs={{4,0},{0,4},{12,8},{8,12},{5,1},{1,5},{13,9},{9,13},{6,2},{2,6},{1... | collective-permute-start | bytes 1572872 | tf_op jit(solution)/shard_map/ppermute | solution.py:272
  1.1 15.3 %collective-permute-start = (bf16[64,4096]{1,0:T(8,128)(2,1)}, bf16[64,4096]{1,0:T(8,128)(2,1)S(1)}, u32[]{:S(2)}, u32[]{:S(2)}) collective-permute-start(bf16[64,4096]{1,0:T(8,128)(2,1)} %a0_ref.2), channel_id=1, source_target_pairs={{8,0},{12,4},{0,8},{4,12},{9,1},{13,5},{1,9},{5,13},{10,2},{14,6},... | collective-permute-start | bytes 1572872 | tf_op jit(solution)/shard_map/ppermute | solution.py:272
  4.4 13.9 %copy-start = (s32[16]{0:T(128)S(1)}, s32[16]{0:T(128)}, u32[]{:S(2)}) copy-start(s32[16]{0:T(128)} %refs_1_.1) | copy-start | bytes 196
  16.4 2.0 %collective-permute-start.3 = (bf16[64,4096]{1,0:T(8,128)(2,1)S(1)}, bf16[64,4096]{1,0:T(8,128)(2,1)S(1)}, u32[]{:S(2)}, u32[]{:S(2)}) collective-permute-start(bf16[64,4096]{1,0:T(8,128)(2,1)S(1)} %collective-permute-done.a0_ref), channel_id=1, source_target_pairs={{4,0},{0,4},{12,8},{8,12},{5,1},{1,5},{13,9},{9,13},{6,2},{2,6},{1... | collective-permute-start | bytes 1572872 | tf_op jit(solution)/shard_map/ppermute | solution.py:272
  16.4 11.0 %collective-permute-start.2 = (bf16[64,2816]{1,0:T(8,128)(2,1)S(1)}, bf16[64,2816]{1,0:T(8,128)(2,1)S(1)}, u32[]{:S(2)}, u32[]{:S(2)}) collective-permute-start(bf16[64,2816]{1,0:T(8,128)(2,1)S(1)} %get-tuple-element.46), channel_id=1, source_target_pairs={{0,1},{1,0},{2,3},{3,2},{4,5},{5,4},{6,7},{7,6},{8,9},{9,8},{10,11... | collective-permute-start | bytes 1081352 | tf_op jit(solution)/shard_map/ppermute | solution.py:275
  27.5 13.9 %collective-permute-start.4 = (bf16[64,2560]{1,0:T(8,128)(2,1)S(1)}, bf16[64,2560]{1,0:T(8,128)(2,1)S(1)}, u32[]{:S(2)}, u32[]{:S(2)}) collective-permute-start(bf16[64,2560]{1,0:T(8,128)(2,1)S(1)} %get-tuple-element.51), channel_id=1, source_target_pairs={{0,1},{1,0},{2,3},{3,2},{4,5},{5,4},{6,7},{7,6},{8,9},{9,8},{10,11... | collective-permute-start | bytes 983048 | tf_op jit(solution)/shard_map/ppermute | solution.py:275
  29.3 12.2 %collective-permute-start.5 = (bf16[32,2816]{1,0:T(8,128)(2,1)S(1)}, bf16[32,2816]{1,0:T(8,128)(2,1)S(1)}, u32[]{:S(2)}, u32[]{:S(2)}) collective-permute-start(bf16[32,2816]{1,0:T(8,128)(2,1)S(1)} %pad_maximum_fusion), channel_id=1, source_target_pairs={{0,2},{1,3},{2,0},{3,1},{4,6},{5,7},{6,4},{7,5},{8,10},{9,11},{10,... | collective-permute-start | bytes 540680 | tf_op jit(solution)/shard_map/ppermute | solution.py:275
  40.9 13.2 %collective-permute-start.6 = (bf16[64,2304]{1,0:T(8,128)(2,1)S(1)}, bf16[64,2304]{1,0:T(8,128)(2,1)S(1)}, u32[]{:S(2)}, u32[]{:S(2)}) collective-permute-start(bf16[64,2304]{1,0:T(8,128)(2,1)S(1)} %get-tuple-element.63), channel_id=1, source_target_pairs={{0,1},{1,0},{2,3},{3,2},{4,5},{5,4},{6,7},{7,6},{8,9},{9,8},{10,11... | collective-permute-start | bytes 884744 | tf_op jit(solution)/shard_map/ppermute | solution.py:275
  41.5 12.6 %collective-permute-start.7 = (bf16[32,2560]{1,0:T(8,128)(2,1)S(1)}, bf16[32,2560]{1,0:T(8,128)(2,1)S(1)}, u32[]{:S(2)}, u32[]{:S(2)}) collective-permute-start(bf16[32,2560]{1,0:T(8,128)(2,1)S(1)} %pad_maximum_fusion.1), channel_id=1, source_target_pairs={{0,2},{1,3},{2,0},{3,1},{4,6},{5,7},{6,4},{7,5},{8,10},{9,11},{10,... | collective-permute-start | bytes 491528 | tf_op jit(solution)/shard_map/ppermute | solution.py:275
  51.6 8.8 %collective-permute-start.10 = (bf16[64,2048]{1,0:T(8,128)(2,1)S(1)}, bf16[64,2048]{1,0:T(8,128)(2,1)S(1)}, u32[]{:S(2)}, u32[]{:S(2)}) collective-permute-start(bf16[64,2048]{1,0:T(8,128)(2,1)S(1)} %get-tuple-element.74), channel_id=1, source_target_pairs={{0,1},{1,0},{2,3},{3,2},{4,5},{5,4},{6,7},{7,6},{8,9},{9,8},{10,11... | collective-permute-start | bytes 786440 | tf_op jit(solution)/shard_map/ppermute | solution.py:275
  54.7 15.2 %collective-permute-start.8 = (bf16[32,2304]{1,0:T(8,128)(2,1)S(1)}, bf16[32,2304]{1,0:T(8,128)(2,1)S(1)}, u32[]{:S(2)}, u32[]{:S(2)}) collective-permute-start(bf16[32,2304]{1,0:T(8,128)(2,1)S(1)} %multiply_convert_fusion.2), channel_id=1, source_target_pairs={{8,0},{12,4},{0,8},{4,12},{9,1},{13,5},{1,9},{5,13},{10,2},{14,6},... | collective-permute-start | bytes 442376 | tf_op jit(solution)/shard_map/ppermute | solution.py:272
  56.2 7.9 %collective-permute-start.9 = (bf16[32,2304]{1,0:T(8,128)(2,1)S(1)}, bf16[32,2304]{1,0:T(8,128)(2,1)S(1)}, u32[]{:S(2)}, u32[]{:S(2)}) collective-permute-start(bf16[32,2304]{1,0:T(8,128)(2,1)S(1)} %add_convert_fusion.1), channel_id=1, source_target_pairs={{0,2},{1,3},{2,0},{3,1},{4,6},{5,7},{6,4},{7,5},{8,10},{9,11},{10,... | collective-permute-start | bytes 442376 | tf_op jit(solution)/shard_map/ppermute | solution.py:275
  64.1 5.9 %collective-permute-start.11 = (bf16[32,2048]{1,0:T(8,128)(2,1)S(1)}, bf16[32,2048]{1,0:T(8,128)(2,1)S(1)}, u32[]{:S(2)}, u32[]{:S(2)}) collective-permute-start(bf16[32,2048]{1,0:T(8,128)(2,1)S(1)} %add_convert_fusion.3), channel_id=1, source_target_pairs={{0,2},{1,3},{2,0},{3,1},{4,6},{5,7},{6,4},{7,5},{8,10},{9,11},{10,... | collective-permute-start | bytes 393224 | tf_op jit(solution)/shard_map/ppermute | solution.py:275
  64.8 5.9 %collective-permute-start.14 = (bf16[32,2304]{1,0:T(8,128)(2,1)S(1)}, bf16[32,2304]{1,0:T(8,128)(2,1)S(1)}, u32[]{:S(2)}, u32[]{:S(2)}) collective-permute-start(bf16[32,2304]{1,0:T(8,128)(2,1)S(1)} %multiply_convert_fusion.1), channel_id=1, source_target_pairs={{8,0},{12,4},{0,8},{4,12},{9,1},{13,5},{1,9},{5,13},{10,2},{14,6},... | collective-permute-start | bytes 442376 | tf_op jit(solution)/shard_map/ppermute | solution.py:272
  70.1 1.4 %collective-permute-start.16 = (bf16[32,2048]{1,0:T(8,128)(2,1)S(1)}, bf16[32,2048]{1,0:T(8,128)(2,1)S(1)}, u32[]{:S(2)}, u32[]{:S(2)}) collective-permute-start(bf16[32,2048]{1,0:T(8,128)(2,1)S(1)} %multiply_convert_fusion.3.refs_10_), channel_id=1, source_target_pairs={{4,0},{0,4},{12,8},{8,12},{5,1},{1,5},{13,9},{9,13},{6,2},{2,6},{1... | collective-permute-start | bytes 393224 | tf_op jit(solution)/shard_map/ppermute | solution.py:272
  70.2 1.5 %collective-permute-start.13 = (bf16[32,2304]{1,0:T(8,128)(2,1)S(1)}, bf16[32,2304]{1,0:T(8,128)(2,1)S(1)}, u32[]{:S(2)}, u32[]{:S(2)}) collective-permute-start(bf16[32,2304]{1,0:T(8,128)(2,1)S(1)} %collective-permute-done.8.refs_6_), channel_id=1, source_target_pairs={{4,0},{0,4},{12,8},{8,12},{5,1},{1,5},{13,9},{9,13},{6,2},{2,6},{1... | collective-permute-start | bytes 442376 | tf_op jit(solution)/shard_map/ppermute | solution.py:272
  70.7 1.6 %collective-permute-start.12 = (bf16[32,2560]{1,0:T(8,128)(2,1)S(1)}, bf16[32,2560]{1,0:T(8,128)(2,1)S(1)}, u32[]{:S(2)}, u32[]{:S(2)}) collective-permute-start(bf16[32,2560]{1,0:T(8,128)(2,1)S(1)} %multiply_convert_fusion.refs_4_), channel_id=1, source_target_pairs={{4,0},{0,4},{12,8},{8,12},{5,1},{1,5},{13,9},{9,13},{6,2},{2,6},{1... | collective-permute-start | bytes 491528 | tf_op jit(solution)/shard_map/ppermute | solution.py:272
  70.8 1.5 %collective-permute-start.15 = (bf16[32,2304]{1,0:T(8,128)(2,1)S(1)}, bf16[32,2304]{1,0:T(8,128)(2,1)S(1)}, u32[]{:S(2)}, u32[]{:S(2)}) collective-permute-start(bf16[32,2304]{1,0:T(8,128)(2,1)S(1)} %collective-permute-done.14.refs_8_), channel_id=1, source_target_pairs={{4,0},{0,4},{12,8},{8,12},{5,1},{1,5},{13,9},{9,13},{6,2},{2,6},{1... | collective-permute-start | bytes 442376 | tf_op jit(solution)/shard_map/ppermute | solution.py:272
